TPU v7x, 32 devices: a whole 2x2x4 slice. The times are simulated.
32 devices in a mesh: parts: 1, basis: 32 (over z, y, x, core).
Axes of the slice: x: 2, y: 2, z: 4, core: 2. Of those that a mesh axis runs over, the one named last changes fastest.
Arguments:
- coulomb: bfloat16 [64, 32, 8, 1024], P(('parts', 'basis')), may hold values from -0.625 to 0.625
- occ_tiles: bfloat16 [32, 2, 1024], P(('parts', 'basis')), may hold values from -0.75 to 0.75
- virt_tiles: bfloat16 [32, 2, 1024], P(('parts', 'basis')), may hold values from -0.75 to 0.75
- tile_count: int32 [32], replicated, may hold values from 1 to 8, 128 in all
- tile_col: int32 [32, 8], replicated, may hold values from 0 to 31, as said below
- dens_col: int32 [32, 2], replicated, may hold values from 0 to 31, as said below
Outputs:
- chi: float32 [64, 64], P(('parts', 'basis'))
Inputs may be any that keep to these rules, and one draw needn't show every extreme that they name: `tile_count`: 128 live tiles in all, at most 8 in one block row. `tile_col`: the blocks of one row are distinct. `dens_col`: the blocks of one row are distinct.
All inputs are finite; a program needn't handle non-finite values.
Results may differ from a plain program's by a relative error of at most 0.0042.
Values may be sent and summed in bfloat16 or wider, within the bound.
No kernel may reach another device: no remote copies, remote signals or barrier semaphores. Data moves between devices by JAX's collectives and lax.ppermute only.
A program may use at most 64 MiB of HBM per device.

v0:
```python
import functools

import jax
import jax.numpy as jnp
from jax import lax
from jax.experimental import pallas as pl
from jax.experimental.pallas import tpu as pltpu
from jax.sharding import PartitionSpec as P

F32, BF16, I32 = jnp.float32, jnp.bfloat16, jnp.int32
BW = 32
TILE = BW * BW
LANES = 128
PACK = LANES // BW
GROUPS = TILE // LANES
PARAMS = pltpu.CompilerParams(vmem_limit_bytes=48 * 1024 * 1024)


def mm(a, b):
    return jnp.dot(a, b, preferred_element_type=F32)


def mm_nt(a, b):
    return lax.dot_general(a, b, (((1,), (1,)), ((), ())), preferred_element_type=F32)


def iota(shape, dim):
    return lax.broadcasted_iota(I32, shape, dim)


def onehot(mask):
    return jnp.where(mask, 1.0, 0.0).astype(BF16)


def spread_tiles(perm_ref):
    for step in range(GROUPS):
        row = iota((LANES, TILE), 0) + step * LANES
        col = iota((LANES, TILE), 1)
        x, y = row // BW, row % BW
        perm_ref[step * LANES : (step + 1) * LANES, :] = onehot(
            col == y * BW + (x % PACK) * GROUPS + x // PACK
        )


def pack_columns(flat, out_ref, aux_dev, first, per_aux, rows, device):
    chunk = iota((rows, LANES), 1) // BW
    for group in range(GROUPS):
        for aux in range(aux_dev):
            turned = []
            for q in range(PACK):
                begin = aux * per_aux + first + q * rows
                part = flat[begin : begin + rows, group * LANES : (group + 1) * LANES]
                turned.append(pltpu.roll(part, q * BW, 1) if q else part)
            for inner in range(PACK):
                picked = turned[-inner % PACK]
                for place in range(1, PACK):
                    picked = jnp.where(chunk == place, turned[(place - inner) % PACK], picked)
                out_ref[device(PACK * group + inner), aux * rows : (aux + 1) * rows, :] = (
                    picked.astype(BF16)
                )


def prepare_kernel(copies, slots_row, cols_ref, dens_ref, t_ref, xt_ref, a_ref, table_ref, perm_ref,
                   flat, planes, lined, swapped):
    aux_dev, slots, _ = t_ref.shape
    live = table_ref.shape[1]
    cols = cols_ref[...]
    is_live = cols >= 0.0
    row_of = (iota((1, slots), 1) // slots_row).astype(F32)
    before = onehot(iota((slots, slots), 0) < iota((slots, slots), 1))
    counted = mm(jnp.broadcast_to(onehot(is_live), (16, slots)), before)[0:1, :]
    compact = jnp.where(is_live, counted, -1.0)
    keep = onehot(iota((live, slots), 0).astype(F32) == compact)
    sub = iota((LANES, slots), 0)
    facts = jnp.where(sub == 0, row_of, jnp.where(sub == 1, cols, 0.0)).astype(BF16)
    places = jnp.where(sub == 0, compact + 1.0, 0.0).astype(BF16)
    own = mm_nt(keep, facts)
    own_row, own_col = own[:, 0:1], own[:, 1:2]
    wide = iota((live, LANES), 1).astype(F32)
    dens = dens_ref[...]
    col_partner = mm_nt(onehot(own_col == wide), dens)
    row_partner = mm_nt(onehot(own_row == wide), dens)
    own_table = mm_nt(facts, keep)
    table_ref[0:2, :] = own_table[0:2, :].astype(I32)
    virt_pick = []
    for j in range(2):
        virt_pick.append(onehot((own_row == row_of) & (col_partner[:, j : j + 1] == cols)))
        occ_pick = onehot((row_partner[:, j : j + 1] == row_of) & (own_col == cols))
        table_ref[2 + j : 3 + j, :] = mm_nt(places, occ_pick)[0:1, :].astype(I32)
    table_ref[4:8, :] = jnp.zeros((4, live), I32)

    spread_tiles(perm_ref)
    for aux in range(aux_dev):
        swapped[aux * live : (aux + 1) * live, :] = mm(keep, t_ref[aux]).astype(BF16)
    flat[...] = mm(swapped[...], perm_ref[...])
    for copy in range(copies):
        pack_columns(flat, xt_ref, aux_dev, 0, live, live // PACK, lambda n: copy * BW + n)

    lane = iota((LANES, LANES), 0)
    x = lane % BW
    within = onehot(
        iota((LANES, LANES), 1) == lane // BW * BW + (x % PACK) * GROUPS + x // PACK
    )
    for aux in range(aux_dev):
        for group in range(GROUPS):
            span = slice(group * LANES, (group + 1) * LANES)
            lined[:, span] = mm(t_ref[aux, :, span], within).astype(BF16)
        for j in range(2):
            gathered = mm(virt_pick[j], lined[...])
            for group in range(GROUPS):
                planes[pl.ds(j * live * 2 * GROUPS + aux * GROUPS + group, live, stride=2 * GROUPS), :] = (
                    gathered[:, group * LANES : (group + 1) * LANES]
                )
    if aux_dev == 1:
        for group in range(GROUPS):
            planes[pl.ds(GROUPS + group, 2 * live, stride=2 * GROUPS), :] = (
                jnp.zeros((2 * live, LANES), F32)
            )
    half = live * 2 * GROUPS
    for j in range(2):
        a_ref[:, j * LANES : (j + 1) * LANES] = planes[j * half : (j + 1) * half, :].astype(BF16)


def virt_kernel(aux_dev, halves, table_ref, dens_ref, a_ref, perm_ref, xm_ref,
                weights, result, swapped, flat):
    live = table_ref.shape[1]
    blocks = dens_ref.shape[0]
    chunk = iota((GROUPS, LANES), 1) // BW

    def build(e, carry):
        tiles = dens_ref[e].astype(F32)
        for j in range(2):
            tile = tiles[j * GROUPS : (j + 1) * GROUPS, :]
            turned = [tile] + [pltpu.roll(tile, d * BW, 1) for d in range(1, PACK)]
            for i in range(PACK):
                for pair in range(PACK // 2):
                    both = [
                        jnp.where(chunk == i, turned[(i - inner) % PACK], 0.0)
                        for inner in (2 * pair, 2 * pair + 1)
                    ]
                    start = pl.multiple_of(e * 2 * LANES, 2 * LANES) + (
                        j * LANES + i * BW + pair * 2 * GROUPS
                    )
                    weights[pl.ds(start, 2 * GROUPS), :] = jnp.concatenate(both, 0).astype(BF16)
        return carry

    lax.fori_loop(0, blocks, build, 0, unroll=4)

    def multiply(step, carry):
        for inner in range(8):
            s = step * 8 + inner
            start = pl.multiple_of(s * 2 * GROUPS, 2 * GROUPS)
            e = pl.multiple_of(table_ref[1, s] * 2 * LANES, 2 * LANES)
            result[pl.ds(start, 2 * GROUPS), :] = mm(
                a_ref[pl.ds(start, 2 * GROUPS), :], weights[pl.ds(e, 2 * LANES), :]
            )
        return carry

    lax.fori_loop(0, live // 8, multiply, 0)
    for aux in range(aux_dev):
        for group in range(GROUPS):
            swapped[aux * live : (aux + 1) * live, group * LANES : (group + 1) * LANES] = (
                result[pl.ds(aux * GROUPS + group, live, stride=2 * GROUPS), :].astype(BF16)
            )
    flat[...] = mm(swapped[...], perm_ref[...])
    part = live // halves
    for half in range(halves):
        pack_columns(flat, xm_ref, aux_dev, half * part, live, part // PACK,
                     lambda n: half * BW + n)


def by_slot(source_ref, wide, aux_dev, rows, devices, r):
    return jnp.concatenate(
        [wide[pl.ds(aux * rows + r, devices, stride=aux_dev * rows), :] for aux in range(aux_dev)],
        0,
    ).astype(BF16)


def widen(source_ref, wide):
    devices, rows, _ = source_ref.shape
    for d in range(devices):
        wide[d * rows : (d + 1) * rows, :] = source_ref[d].astype(F32)


def occ_kernel(aux_dev, table_ref, place_ref, dens_ref, xt_ref, perm_ref, mo_ref,
               wide, held, tiles, lined, planes, weights):
    devices, rows_all, _ = xt_ref.shape
    rows = rows_all // aux_dev
    blocks = dens_ref.shape[0]
    out_rows, aux, _ = mo_ref.shape
    turn, first = place_ref[0], place_ref[1]

    widen(xt_ref, wide)
    for r in range(rows):
        held[r * aux : (r + 1) * aux, :] = by_slot(xt_ref, wide, aux_dev, rows, devices, r)

    height = dens_ref.shape[1]
    for a in range(blocks):
        tiles[a * height : (a + 1) * height, :] = dens_ref[a].astype(F32)
    for j in range(2):
        for group in range(GROUPS):
            lined[j * blocks : (j + 1) * blocks, group * LANES : (group + 1) * LANES] = (
                tiles[pl.ds(2 * GROUPS + j * GROUPS + group, blocks, stride=height), :].astype(BF16)
            )
    turned_tiles = mm(lined[...], perm_ref[...])
    for j in range(2):
        for group in range(GROUPS):
            planes[pl.ds(j * GROUPS + group, blocks, stride=2 * GROUPS), :] = (
                turned_tiles[j * blocks : (j + 1) * blocks, group * LANES : (group + 1) * LANES]
            )
    chunk8 = iota((GROUPS, LANES), 1) // BW

    def build(a, carry):
        base = pl.multiple_of(a * 2 * GROUPS, 2 * GROUPS)
        for j in range(2):
            tile = planes[pl.ds(base + j * GROUPS, GROUPS), :]
            turned = [tile] + [pltpu.roll(tile, d * BW, 1) for d in range(1, PACK)]
            copies = []
            for inner in range(PACK):
                copy = turned[-inner % PACK]
                for place in range(1, PACK):
                    copy = jnp.where(chunk8 == place, turned[(place - inner) % PACK], copy)
                copies.append(copy)
            block = jnp.concatenate(copies, 0).astype(BF16)
            for place in range(PACK):
                start = pl.multiple_of(a * 2 * LANES, 2 * LANES) + j * LANES + place * BW
                weights[pl.ds(start, BW), :] = block
        return carry

    lax.fori_loop(0, blocks, build, 0, unroll=4)
    chunk = iota((aux, LANES), 1) // BW

    def multiply(r, carry):
        total = jnp.zeros((aux, LANES), F32)
        for q in range(PACK):
            s = first + q * out_rows + r
            parts = []
            for j in range(2):
                found = table_ref[2 + j, s] - 1
                source = jnp.maximum(found, 0)
                place = jnp.where(found < 0, -1, (source // rows + turn) % PACK)
                start = pl.multiple_of(source % rows * aux, aux)
                parts.append(jnp.where(chunk == place, held[pl.ds(start, aux), :].astype(F32), 0.0).astype(BF16))
            a = pl.multiple_of(table_ref[0, s] * 2 * LANES, 2 * LANES)
            product = mm(jnp.concatenate(parts, 1), weights[pl.ds(a, 2 * LANES), :])
            total = jnp.where(chunk == (q + turn) % PACK, product, total)
        mo_ref[r] = total.astype(BF16)
        return carry

    lax.fori_loop(0, out_rows, multiply, 0, unroll=2)


def gram_kernel(aux_dev, mo_ref, xm_ref, out_ref, wide):
    devices, rows_all, _ = xm_ref.shape
    rows = rows_all // aux_dev
    aux = aux_dev * devices
    widen(xm_ref, wide)
    total = jnp.zeros((aux, aux), F32)
    for r in range(rows):
        total = total + mm_nt(mo_ref[r], by_slot(xm_ref, wide, aux_dev, rows, devices, r))
    out_ref[...] = jnp.concatenate(
        [total[aux_i * devices : (aux_i + 1) * devices, :] for aux_i in range(aux_dev)], 1
    )


def sum_kernel(aux_dev, part_ref, out_ref):
    devices, width = part_ref.shape
    aux = aux_dev * devices
    total = jnp.sum(part_ref[...], axis=0, keepdims=True)
    lane, col = iota((width, aux), 0), iota((width, aux), 1)
    for row in range(aux_dev):
        chosen = lane == row * aux + col % aux_dev * devices + col // aux_dev
        out_ref[row : row + 1, :] = jnp.dot(
            jnp.broadcast_to(total, (8, width)),
            jnp.where(chosen, 1.0, 0.0),
            precision=lax.Precision.HIGHEST,
            preferred_element_type=F32,
        )[0:1, :]


def call(kernel, outs, scratch, smem, args, name):
    specs = [
        pl.BlockSpec(memory_space=pltpu.SMEM if i < smem else pltpu.VMEM) for i in range(len(args))
    ]
    out_specs = jax.tree.map(lambda _: pl.BlockSpec(memory_space=pltpu.VMEM), outs)
    return pl.pallas_call(
        kernel,
        out_shape=outs,
        in_specs=specs,
        out_specs=out_specs,
        scratch_shapes=scratch,
        compiler_params=PARAMS,
        name=name,
    )(*args)


def exchange(x):
    return lax.all_to_all(x, "basis", split_axis=0, concat_axis=0, tiled=True)


def body(devices, coulomb, occ_tiles, virt_tiles, tile_count, tile_col, dens_col):
    aux_dev, blocks, slots_row, _ = coulomb.shape
    slots = blocks * slots_row
    live = slots // 2
    halves = devices // BW
    aux = aux_dev * devices
    shape = jax.ShapeDtypeStruct

    own = jnp.concatenate([virt_tiles.reshape(-1, LANES), occ_tiles.reshape(-1, LANES)], 0)
    dens = exchange(jnp.broadcast_to(own[None], (devices,) + own.shape))

    live_slot = jnp.arange(slots_row, dtype=I32)[None, :] < tile_count[:, None]
    cols = jnp.where(live_slot, tile_col, -1).astype(F32).reshape(1, slots)
    partners = jnp.pad(dens_col.T.astype(BF16), ((0, LANES - 2), (0, LANES - blocks)))
    rows_t = live // PACK
    rows_m = live // halves // PACK
    xt, gathered, table, perm = call(
        functools.partial(prepare_kernel, halves, slots_row),
        (
            shape((devices, aux_dev * rows_t, LANES), BF16),
            shape((live * 2 * GROUPS, 2 * LANES), BF16),
            shape((8, live), I32),
            shape((TILE, TILE), BF16),
        ),
        [
            pltpu.VMEM((aux_dev * live, TILE), F32),
            pltpu.VMEM((live * 4 * GROUPS, LANES), F32),
            pltpu.VMEM((slots, TILE), BF16),
            pltpu.VMEM((aux_dev * live, TILE), BF16),
        ],
        0,
        (cols, partners, coulomb.reshape(aux_dev, slots, TILE)),
        "prepare",
    )
    xt = exchange(xt)
    xm = call(
        functools.partial(virt_kernel, aux_dev, halves),
        shape((devices, aux_dev * rows_m, LANES), BF16),
        [
            pltpu.VMEM((blocks * 2 * LANES, LANES), BF16),
            pltpu.VMEM((live * 2 * GROUPS, LANES), F32),
            pltpu.VMEM((aux_dev * live, TILE), BF16),
            pltpu.VMEM((aux_dev * live, TILE), F32),
        ],
        1,
        (table, dens, gathered, perm),
        "virt",
    )
    xm = exchange(xm)
    index = lax.axis_index("basis")
    place = jnp.stack([index % PACK, index // BW * (live // halves)]).astype(I32)
    mo = call(
        functools.partial(occ_kernel, aux_dev),
        shape((rows_m, aux, LANES), BF16),
        [
            pltpu.VMEM((devices * aux_dev * rows_t, LANES), F32),
            pltpu.VMEM((rows_t * aux, LANES), BF16),
            pltpu.VMEM((blocks * 4 * GROUPS, LANES), F32),
            pltpu.VMEM((2 * blocks, TILE), BF16),
            pltpu.VMEM((blocks * 2 * GROUPS, LANES), F32),
            pltpu.VMEM((blocks * 2 * LANES, LANES), BF16),
        ],
        2,
        (table, place, dens, xt, perm),
        "occ",
    )
    part = call(
        functools.partial(gram_kernel, aux_dev),
        shape((devices, aux_dev * aux), F32),
        [pltpu.VMEM((devices * aux_dev * rows_m, LANES), F32)],
        0,
        (mo, xm),
        "gram",
    )
    part = exchange(part)
    return call(
        functools.partial(sum_kernel, aux_dev), shape((aux_dev, aux), F32), [], 0, (part,), "total"
    )


def solution(mesh):
    in_specs = (
        P(("parts", "basis"), None, None, None),
        P(("parts", "basis"), None, None),
        P(("parts", "basis"), None, None),
        P(),
        P(),
        P(),
    )
    out_specs = P(("parts", "basis"), None)
    return jax.shard_map(
        functools.partial(body, mesh.shape["basis"]),
        mesh=mesh,
        in_specs=in_specs,
        out_specs=out_specs,
        check_vma=False,
    )
```

profile of v0, /device:TPU:0, one launch (start us, length us, event | category | flops | bytes accessed | tf_op | source)
XLA Modules:
  0.0 69.4 jit_solution(9344820275065407885)
XLA Ops:
  0.0 0.7 %reshape.18 = bf16[16,128]{1,0:T(8,128)(2,1)S(1)} reshape(bf16[1,2,1024]{2,1,0:T(2,128)(2,1)} %param.8) | data formatting | bytes 8192 | tf_op jit(solution)/shard_map/reshape | solution.py:309
  0.7 0.7 %reshape.19 = bf16[16,128]{1,0:T(8,128)(2,1)S(1)} reshape(bf16[1,2,1024]{2,1,0:T(2,128)(2,1)} %param.7) | data formatting | bytes 8192 | tf_op jit(solution)/shard_map/reshape | solution.py:309
  1.4 0.7 %broadcast_in_dim.6 = bf16[32,32,128]{2,1,0:T(8,128)(2,1)} broadcast(bf16[32,128]{1,0:T(8,128)(2,1)S(1)} %pad_maximum_fusion), dimensions={1,2} | broadcast | bytes 270336 | tf_op jit(solution)/shard_map/broadcast_in_dim | solution.py:310
  2.1 7.3 %all-to-all-start = ((bf16[32,32,128]{2,1,0:T(8,128)(2,1)}), bf16[32,32,128]{2,1,0:T(8,128)(2,1)S(1)}, u32[]{:S(2)}, u32[]{:S(2)}) async-start(bf16[32,32,128]{2,1,0:T(8,128)(2,1)} %broadcast_in_dim.6), calls=%async_computation | async-start | bytes 524288 | tf_op jit(solution)/shard_map/all_to_all | solution.py:298
  9.4 0.7 %select_convert_fusion = f32[32,8]{0,1:T(8,128)S(1)} fusion(s32[32,8]{0,1:T(8,128)} %param.10, s32[32]{0:T(128)} %param.9), kind=kLoop, calls=%fused_computation.1 | loop fusion | flops 768 | bytes 2176 | tf_op jit(solution)/shard_map/convert_element_type | solution.py:313
  10.1 0.1 copy.9
  10.2 0.1 reshape.16.cols_ref
  10.3 0.7 convert_bitcast_fusion
  11.0 0.0 copy-start.4
  11.0 1.2 %copy-done.4 = bf16[2,32,8,1024]{3,2,1,0:T(8,128)(2,1)S(1)} copy-done((bf16[2,32,8,1024]{3,2,1,0:T(8,128)(2,1)S(1)}, bf16[2,32,8,1024]{3,2,1,0:T(8,128)(2,1)}, u32[]{:S(2)}) %copy-start.4) | copy-done | bytes 1048600
  12.2 3.3 %prepare.1 = (bf16[32,64,128]{2,1,0:T(8,128)(2,1)}, bf16[2048,256]{1,0:T(8,128)(2,1)S(1)}, s32[8,128]{1,0:T(8,128)S(1)}, bf16[1024,1024]{1,0:T(8,128)(2,1)S(1)}) custom-call(f32[1,256]{1,0:T(1,128)S(1)} %reshape.16.cols_ref, bf16[128,128]{1,0:T(8,128)(2,1)S(1)} %pad.4.dens_ref, bf16[2,256,1024]{2,1,0:T(8,128)(2,1)S(1)} %bitcast.9), custom_call_target="tpu_custom_call" | custom-call | tf_op jit(solution)/shard_map/prepare/pallas_call | solution.py:286
  15.5 0.0 copy-start.2
  15.5 1.0 %copy-done.2 = bf16[2048,256]{1,0:T(8,128)(2,1)} copy-done((bf16[2048,256]{1,0:T(8,128)(2,1)}, bf16[2048,256]{1,0:T(8,128)(2,1)S(1)}, u32[]{:S(2)}) %copy-start.2) | copy-done | bytes 1048600
  16.5 3.5 %all-to-all-done.dens_ref = bf16[32,32,128]{2,1,0:T(8,128)(2,1)S(1)} async-done(((bf16[32,32,128]{2,1,0:T(8,128)(2,1)}), bf16[32,32,128]{2,1,0:T(8,128)(2,1)S(1)}, u32[]{:S(2)}, u32[]{:S(2)}) %all-to-all-start) | async-done | bytes 262176 | tf_op jit(solution)/shard_map/all_to_all | solution.py:298
  20.0 2.6 %all-to-all-start.1 = ((bf16[32,64,128]{2,1,0:T(8,128)(2,1)}), bf16[32,64,128]{2,1,0:T(8,128)(2,1)S(1)}, u32[]{:S(2)}, u32[]{:S(2)}) async-start(bf16[32,64,128]{2,1,0:T(8,128)(2,1)} %get-tuple-element.10), calls=%async_computation.1 | async-start | bytes 1048576 | tf_op jit(solution)/shard_map/all_to_all | solution.py:298
  22.7 0.0 copy-start.3
  22.7 1.2 %copy-done.3 = bf16[2048,256]{1,0:T(8,128)(2,1)S(1)} copy-done((bf16[2048,256]{1,0:T(8,128)(2,1)S(1)}, bf16[2048,256]{1,0:T(8,128)(2,1)}, u32[]{:S(2)}) %copy-start.3) | copy-done | bytes 1048600
  23.9 6.6 %virt.1 = bf16[32,64,128]{2,1,0:T(8,128)(2,1)} custom-call(s32[8,128]{1,0:T(8,128)S(1)} %get-tuple-element.9.table_ref, bf16[32,32,128]{2,1,0:T(8,128)(2,1)S(1)} %all-to-all-done.dens_ref, bf16[2048,256]{1,0:T(8,128)(2,1)S(1)} %copy-done.3, bf16[1024,1024]{1,0:T(8,128)(2,1)S(1)} %get-tuple-element.11.perm_ref), custom_call_target="tpu_custom_call" | custom-call | tf_op jit(solution)/shard_map/virt/pallas_call | solution.py:286
  30.5 7.7 %all-to-all-done.1.xt_ref = bf16[32,64,128]{2,1,0:T(8,128)(2,1)S(1)} async-done(((bf16[32,64,128]{2,1,0:T(8,128)(2,1)}), bf16[32,64,128]{2,1,0:T(8,128)(2,1)S(1)}, u32[]{:S(2)}, u32[]{:S(2)}) %all-to-all-start.1) | async-done | bytes 524320 | tf_op jit(solution)/shard_map/all_to_all | solution.py:298
  38.2 3.0 %all-to-all-start.2 = ((bf16[32,64,128]{2,1,0:T(8,128)(2,1)}), bf16[32,64,128]{2,1,0:T(8,128)(2,1)S(1)}, u32[]{:S(2)}, u32[]{:S(2)}) async-start(bf16[32,64,128]{2,1,0:T(8,128)(2,1)} %virt.1), calls=%async_computation.2 | async-start | bytes 1048576 | tf_op jit(solution)/shard_map/all_to_all | solution.py:298
  41.2 0.1 pad_add_fusion.place_ref
  41.3 7.2 %occ.1.mo_ref = bf16[32,64,128]{2,1,0:T(8,128)(2,1)S(1)} custom-call(s32[8,128]{1,0:T(8,128)S(1)} %get-tuple-element.9.table_ref, s32[2]{0:T(128)S(1)} %pad_add_fusion.place_ref, bf16[32,32,128]{2,1,0:T(8,128)(2,1)S(1)} %all-to-all-done.dens_ref, bf16[32,64,128]{2,1,0:T(8,128)(2,1)S(1)} %all-to-all-done.1.xt_ref, ...), custom_call_target="tpu_custom_call" | custom-call | tf_op jit(solution)/shard_map/occ/pallas_call | solution.py:286
  48.5 0.0 copy-start
  48.5 0.8 %copy-done = bf16[32,64,128]{2,1,0:T(8,128)(2,1)} copy-done((bf16[32,64,128]{2,1,0:T(8,128)(2,1)}, bf16[32,64,128]{2,1,0:T(8,128)(2,1)S(1)}, u32[]{:S(2)}) %copy-start) | copy-done | bytes 524312
  49.3 7.5 %all-to-all-done.2.xm_ref = bf16[32,64,128]{2,1,0:T(8,128)(2,1)S(1)} async-done(((bf16[32,64,128]{2,1,0:T(8,128)(2,1)}), bf16[32,64,128]{2,1,0:T(8,128)(2,1)S(1)}, u32[]{:S(2)}, u32[]{:S(2)}) %all-to-all-start.2) | async-done | bytes 524320 | tf_op jit(solution)/shard_map/all_to_all | solution.py:298
  56.7 0.0 copy-start.1
  56.7 1.0 %copy-done.1 = bf16[32,64,128]{2,1,0:T(8,128)(2,1)S(1)} copy-done((bf16[32,64,128]{2,1,0:T(8,128)(2,1)S(1)}, bf16[32,64,128]{2,1,0:T(8,128)(2,1)}, u32[]{:S(2)}) %copy-start.1) | copy-done | bytes 524312
  57.8 0.8 %gram.1 = f32[32,128]{1,0:T(8,128)S(1)} custom-call(bf16[32,64,128]{2,1,0:T(8,128)(2,1)S(1)} %copy-done.1, bf16[32,64,128]{2,1,0:T(8,128)(2,1)S(1)} %all-to-all-done.2.xm_ref), custom_call_target="tpu_custom_call" | custom-call | tf_op jit(solution)/shard_map/gram/pallas_call | solution.py:286
  58.6 10.0 %all_to_all.26 = f32[32,1,128]{2,1,0:T(1,128)S(1)} all-to-all(f32[32,1,128]{2,1,0:T(1,128)S(1)} %bitcast.10), channel_id=1, replica_groups=mesh['parts'=1,'basis'=32] {'basis'}, dimensions={0} | all-to-all | bytes 32768 | tf_op jit(solution)/shard_map/all_to_all | solution.py:298
  68.6 0.8 %total.1 = f32[2,64]{1,0:T(2,128)} custom-call(f32[32,128]{1,0:T(8,128)S(1)} %bitcast.11), custom_call_target="tpu_custom_call" | custom-call | tf_op jit(solution)/shard_map/total/pallas_call | solution.py:286
  (2 shorter events, 0.0 us)
Async XLA Ops:
  2.1 17.9 %all-to-all-start = ((bf16[32,32,128]{2,1,0:T(8,128)(2,1)}), bf16[32,32,128]{2,1,0:T(8,128)(2,1)S(1)}, u32[]{:S(2)}, u32[]{:S(2)}) async-start(bf16[32,32,128]{2,1,0:T(8,128)(2,1)} %broadcast_in_dim.6), calls=%async_computation | async-start | bytes 524288 | tf_op jit(solution)/shard_map/all_to_all | solution.py:298
  11.0 1.2 %copy-start.4 = (bf16[2,32,8,1024]{3,2,1,0:T(8,128)(2,1)S(1)}, bf16[2,32,8,1024]{3,2,1,0:T(8,128)(2,1)}, u32[]{:S(2)}) copy-start(bf16[2,32,8,1024]{3,2,1,0:T(8,128)(2,1)} %param.6) | copy-start | bytes 3145732
  15.5 1.0 %copy-start.2 = (bf16[2048,256]{1,0:T(8,128)(2,1)}, bf16[2048,256]{1,0:T(8,128)(2,1)S(1)}, u32[]{:S(2)}) copy-start(bf16[2048,256]{1,0:T(8,128)(2,1)S(1)} %get-tuple-element.12.a_ref) | copy-start | bytes 3145732
  20.0 18.2 %all-to-all-start.1 = ((bf16[32,64,128]{2,1,0:T(8,128)(2,1)}), bf16[32,64,128]{2,1,0:T(8,128)(2,1)S(1)}, u32[]{:S(2)}, u32[]{:S(2)}) async-start(bf16[32,64,128]{2,1,0:T(8,128)(2,1)} %get-tuple-element.10), calls=%async_computation.1 | async-start | bytes 1048576 | tf_op jit(solution)/shard_map/all_to_all | solution.py:298
  22.7 1.2 %copy-start.3 = (bf16[2048,256]{1,0:T(8,128)(2,1)S(1)}, bf16[2048,256]{1,0:T(8,128)(2,1)}, u32[]{:S(2)}) copy-start(bf16[2048,256]{1,0:T(8,128)(2,1)} %copy-done.2) | copy-start | bytes 3145732
  38.2 18.5 %all-to-all-start.2 = ((bf16[32,64,128]{2,1,0:T(8,128)(2,1)}), bf16[32,64,128]{2,1,0:T(8,128)(2,1)S(1)}, u32[]{:S(2)}, u32[]{:S(2)}) async-start(bf16[32,64,128]{2,1,0:T(8,128)(2,1)} %virt.1), calls=%async_computation.2 | async-start | bytes 1048576 | tf_op jit(solution)/shard_map/all_to_all | solution.py:298
  48.5 0.8 %copy-start = (bf16[32,64,128]{2,1,0:T(8,128)(2,1)}, bf16[32,64,128]{2,1,0:T(8,128)(2,1)S(1)}, u32[]{:S(2)}) copy-start(bf16[32,64,128]{2,1,0:T(8,128)(2,1)S(1)} %occ.1.mo_ref) | copy-start | bytes 1572868
  56.7 1.0 %copy-start.1 = (bf16[32,64,128]{2,1,0:T(8,128)(2,1)S(1)}, bf16[32,64,128]{2,1,0:T(8,128)(2,1)}, u32[]{:S(2)}) copy-start(bf16[32,64,128]{2,1,0:T(8,128)(2,1)} %copy-done) | copy-start | bytes 1572868
where the time goes:
time: 70 us; the launch traced here: 69.4 us
  Pallas kernels  18.7 us (27%)
  waiting for transfers between devices  18.7 us (27%)
  starting transfers between devices  12.9 us (18%)
  blocking collectives  10 us (14%)
  local copies, waits for them, and re-layouts  7.53 us (11%)
  other arithmetic  1.46 us (2%)
    pallas_call x5, Pallas kernels, call(): pl.pallas_call(kernel, out_shape=outs, in_specs=specs, out_specs=out_spec...  18.7 us
    all_to_all x3, waiting for transfers between devices, exchange(): return lax.all_to_all(x, 'basis', split_axis=0, concat_axis=0, tiled=True)  18.7 us
    all_to_all x3, starting transfers between devices, exchange(): return lax.all_to_all(x, 'basis', split_axis=0, concat_axis=0, tiled=True)  12.9 us
    all_to_all x1, blocking collectives, exchange(): return lax.all_to_all(x, 'basis', split_axis=0, concat_axis=0, tiled=True)  10 us
    unnamed x10, local copies, waits for them, and re-layouts  5.22 us
  transfers between devices with their start and end apart: 3, of which 3 were waited for; matrix products, arithmetic and copies ran while one was open for 2% of the time, Pallas kernels for 25%

commit v1 on v0

v1 whole, which is shorter than its diff:
```python
import functools

import jax
import jax.numpy as jnp
from jax import lax
from jax.experimental import pallas as pl
from jax.experimental.pallas import tpu as pltpu
from jax.sharding import PartitionSpec as P

F32, BF16, I32 = jnp.float32, jnp.bfloat16, jnp.int32
BW = 32
TILE = BW * BW
LANES = 128
PACK = LANES // BW
GROUPS = TILE // LANES
NEAR = 8


def mm(a, b):
    return jnp.dot(a, b, preferred_element_type=F32)


def mm_nt(a, b):
    return lax.dot_general(a, b, (((1,), (1,)), ((), ())), preferred_element_type=F32)


def iota(shape, dim):
    return lax.broadcasted_iota(I32, shape, dim)


def onehot(mask):
    return jnp.where(mask, 1.0, 0.0).astype(BF16)


def spread_tiles(perm_ref):
    for step in range(GROUPS):
        row = iota((LANES, TILE), 0) + step * LANES
        col = iota((LANES, TILE), 1)
        x, y = row // BW, row % BW
        perm_ref[step * LANES : (step + 1) * LANES, :] = onehot(
            col == y * BW + (x % PACK) * GROUPS + x // PACK
        )


def pack_columns(flat, out_ref, aux_dev, first, per_aux, rows, device):
    chunk = iota((rows, LANES), 1) // BW
    for group in range(GROUPS):
        for aux in range(aux_dev):
            turned = []
            for q in range(PACK):
                begin = aux * per_aux + first + q * rows
                part = flat[begin : begin + rows, group * LANES : (group + 1) * LANES]
                turned.append(pltpu.roll(part, q * BW, 1) if q else part)
            for inner in range(PACK):
                picked = turned[-inner % PACK]
                for place in range(1, PACK):
                    picked = jnp.where(chunk == place, turned[(place - inner) % PACK], picked)
                out_ref[device(PACK * group + inner), aux * rows : (aux + 1) * rows, :] = (
                    picked.astype(BF16)
                )


def format_kernel(virt_hbm, occ_hbm, out_ref, virt_ref, occ_ref, own, sems):
    fetches = [
        pltpu.make_async_copy(virt_hbm, virt_ref, sems.at[0]),
        pltpu.make_async_copy(occ_hbm, occ_ref, sems.at[1]),
    ]
    for fetch in fetches:
        fetch.start()
    for fetch in fetches:
        fetch.wait()
    virt, occ = virt_ref[...].astype(F32), occ_ref[...].astype(F32)
    for group in range(GROUPS):
        span = slice(group * LANES, (group + 1) * LANES)
        own[pl.ds(group, 2, stride=GROUPS), :] = virt[:, span]
        own[pl.ds(2 * GROUPS + group, 2, stride=GROUPS), :] = occ[:, span]
    own_tiles = own[...].astype(BF16)
    for d in range(out_ref.shape[0]):
        out_ref[d] = own_tiles


def index_slots(count_ref, cols_ref):
    slots_row, blocks = cols_ref.shape
    slots = slots_row * blocks
    raw = jnp.where(iota((slots_row, blocks), 0) < count_ref[...], cols_ref[...], -1).astype(F32)
    raw = jnp.concatenate([raw, jnp.zeros((2 * GROUPS - slots_row, blocks), F32)], 0).astype(BF16)
    slot_row = iota((blocks, slots), 1) // slots_row
    spread = mm(raw, onehot(slot_row == iota((blocks, slots), 0)))[:slots_row, :]
    mine = iota((slots_row, slots), 1) % slots_row == iota((slots_row, slots), 0)
    cols = jnp.sum(jnp.where(mine, spread, 0.0), axis=0, keepdims=True)
    is_live = cols >= 0.0
    before = onehot(iota((slots, slots), 0) < iota((slots, slots), 1))
    counted = mm(jnp.broadcast_to(onehot(is_live), (16, slots)), before)[0:1, :]
    row_of = (iota((1, slots), 1) // slots_row).astype(F32)
    return row_of, cols, jnp.where(is_live, counted, -1.0)


def keep_live(compact, live):
    return onehot(iota((live, compact.shape[1]), 0).astype(F32) == compact)


def start_fetches(pairs, sems):
    fetches = [pltpu.make_async_copy(*pair, sems.at[i]) for i, pair in enumerate(pairs)]
    for fetch in fetches:
        fetch.start()
    return fetches


def prepare_kernel(copies, count_hbm, cols_hbm, dens_hbm, t_hbm, *rest):
    outer = len(rest) - 13
    x_refs, (a_ref, table_ref, perm_ref, count_ref, cols_ref, dens_ref, t_ref, xt_ref, flat, planes,
             lined, swapped, sems) = rest[:outer], rest[outer:]
    fetches = start_fetches(
        ((count_hbm, count_ref), (cols_hbm, cols_ref), (dens_hbm, dens_ref), (t_hbm, t_ref)), sems
    )
    aux_dev, slots, _ = t_ref.shape
    live = table_ref.shape[1]
    blocks = cols_ref.shape[1]
    spread_tiles(perm_ref)
    for fetch in fetches[:3]:
        fetch.wait()
    row_of, cols, compact = index_slots(count_ref, cols_ref)
    keep = keep_live(compact, live)
    fetches[3].wait()
    for aux in range(aux_dev):
        swapped[aux * live : (aux + 1) * live, :] = mm(keep, t_ref[aux]).astype(BF16)
    flat[...] = mm(swapped[...], perm_ref[...])
    me = lax.axis_index("basis")
    for copy in range(copies):
        pack_columns(flat, xt_ref, aux_dev, 0, live, live // PACK, lambda n: (copy * BW + n) ^ me)
    for far, x_ref in enumerate(x_refs):
        x_ref[...] = xt_ref[far * NEAR : (far + 1) * NEAR]

    sub = iota((LANES, slots), 0)
    facts = jnp.where(sub == 0, row_of, jnp.where(sub == 1, cols, 0.0)).astype(BF16)
    places = jnp.where(sub == 0, compact + 1.0, 0.0).astype(BF16)
    own_facts = mm_nt(keep, facts)
    own_row, own_col = own_facts[:, 0:1], own_facts[:, 1:2]
    block = iota((live, blocks), 1).astype(F32)
    table_ref[0:2, :] = mm_nt(facts, keep)[0:2, :].astype(I32)
    virt_pick = []
    for j in range(2):
        partner = dens_ref[j : j + 1, :].astype(F32)
        col_partner, row_partner = (
            jnp.sum(jnp.where(place == block, partner, 0.0), axis=1, keepdims=True)
            for place in (own_col, own_row)
        )
        virt_pick.append(onehot((own_row == row_of) & (col_partner == cols)))
        occ_pick = onehot((row_partner == row_of) & (own_col == cols))
        table_ref[2 + j : 3 + j, :] = mm_nt(places, occ_pick)[0:1, :].astype(I32)
    table_ref[4:8, :] = jnp.zeros((4, live), I32)
    lane = iota((LANES, LANES), 0)
    x = lane % BW
    within = onehot(
        iota((LANES, LANES), 1) == lane // BW * BW + (x % PACK) * GROUPS + x // PACK
    )
    for aux in range(aux_dev):
        for group in range(GROUPS):
            span = slice(group * LANES, (group + 1) * LANES)
            lined[:, span] = mm(t_ref[aux, :, span], within).astype(BF16)
        for j in range(2):
            gathered = mm(virt_pick[j], lined[...])
            for group in range(GROUPS):
                planes[pl.ds(j * live * 2 * GROUPS + aux * GROUPS + group, live, stride=2 * GROUPS), :] = (
                    gathered[:, group * LANES : (group + 1) * LANES]
                )
    if aux_dev == 1:
        for group in range(GROUPS):
            planes[pl.ds(GROUPS + group, 2 * live, stride=2 * GROUPS), :] = (
                jnp.zeros((2 * live, LANES), F32)
            )
    half = live * 2 * GROUPS
    for j in range(2):
        a_ref[:, j * LANES : (j + 1) * LANES] = planes[j * half : (j + 1) * half, :].astype(BF16)


def virt_kernel(aux_dev, halves, table_hbm, dens_hbm, a_hbm, perm_hbm, xm_ref, token_ref,
                table_ref, dens_ref, a_ref, perm_ref, weights, result, swapped, flat, sems):
    fetch_dens, fetch_table, fetch_a, fetch_perm = start_fetches(
        ((dens_hbm, dens_ref), (table_hbm, table_ref), (a_hbm, a_ref), (perm_hbm, perm_ref)), sems
    )
    live = table_ref.shape[1]
    token_ref[...] = jnp.zeros(token_ref.shape, F32)
    blocks, rows, _ = dens_ref.shape
    chunk = iota((GROUPS, LANES), 1) // BW

    def build(e, carry):
        tiles = dens_ref[e, : 2 * GROUPS, :].astype(F32)
        for j in range(2):
            tile = tiles[j * GROUPS : (j + 1) * GROUPS, :]
            turned = [tile] + [pltpu.roll(tile, d * BW, 1) for d in range(1, PACK)]
            for i in range(PACK):
                for pair in range(PACK // 2):
                    both = [
                        jnp.where(chunk == i, turned[(i - inner) % PACK], 0.0)
                        for inner in (2 * pair, 2 * pair + 1)
                    ]
                    start = pl.multiple_of(e * 2 * LANES, 2 * LANES) + (
                        j * LANES + i * BW + pair * 2 * GROUPS
                    )
                    weights[pl.ds(start, 2 * GROUPS), :] = jnp.concatenate(both, 0).astype(BF16)
        return carry

    fetch_dens.wait()
    lax.fori_loop(0, blocks, build, 0, unroll=4)
    fetch_table.wait()
    fetch_a.wait()

    def multiply(step, carry):
        for inner in range(32):
            s = step * 32 + inner
            start = pl.multiple_of(s * 2 * GROUPS, 2 * GROUPS)
            e = pl.multiple_of(table_ref[1, s] * 2 * LANES, 2 * LANES)
            result[pl.ds(start, 2 * GROUPS), :] = mm(
                a_ref[pl.ds(start, 2 * GROUPS), :], weights[pl.ds(e, 2 * LANES), :]
            )
        return carry

    lax.fori_loop(0, live // 32, multiply, 0)
    fetch_perm.wait()
    for aux in range(aux_dev):
        for group in range(GROUPS):
            swapped[aux * live : (aux + 1) * live, group * LANES : (group + 1) * LANES] = (
                result[pl.ds(aux * GROUPS + group, live, stride=2 * GROUPS), :].astype(BF16)
            )
    flat[...] = mm(swapped[...], perm_ref[...])
    part = live // halves
    for half in range(halves):
        pack_columns(flat, xm_ref, aux_dev, half * part, live, part // PACK,
                     lambda n: half * BW + n)


def regroup_kernel(token_ref, *refs):
    sources, targets = refs[:-NEAR], refs[-NEAR:]
    for near in range(NEAR):
        for far, source in enumerate(sources):
            targets[near][far] = source[near]


def by_slot(wide, aux_dev, rows, devices, r):
    return jnp.concatenate(
        [wide[pl.ds(aux * rows + r, devices, stride=aux_dev * rows), :] for aux in range(aux_dev)],
        0,
    )


def widen(source_ref, rows, wide):
    devices = source_ref.shape[0]
    for d in range(devices):
        wide[d * rows : (d + 1) * rows, :] = source_ref[d, :rows, :].astype(F32)


def turn_kernel(token_ref, dens_ref, perm_ref, out_ref, tiles, lined, planes):
    blocks = dens_ref.shape[0]
    for a in range(blocks):
        tiles[a * 2 * GROUPS : (a + 1) * 2 * GROUPS, :] = dens_ref[a, 2 * GROUPS :, :].astype(F32)
    for j in range(2):
        for group in range(GROUPS):
            lined[j * blocks : (j + 1) * blocks, group * LANES : (group + 1) * LANES] = (
                tiles[pl.ds(j * GROUPS + group, blocks, stride=2 * GROUPS), :].astype(BF16)
            )
    turned_tiles = mm(lined[...], perm_ref[...])
    for j in range(2):
        for group in range(GROUPS):
            planes[pl.ds(j * GROUPS + group, blocks, stride=2 * GROUPS), :] = (
                turned_tiles[j * blocks : (j + 1) * blocks, group * LANES : (group + 1) * LANES]
            )
    chunk = iota((GROUPS, LANES), 1) // BW

    def build(tile_index, carry):
        tile = planes[pl.ds(pl.multiple_of(tile_index * GROUPS, GROUPS), GROUPS), :]
        turned = [tile] + [pltpu.roll(tile, d * BW, 1) for d in range(1, PACK)]
        copies = []
        for inner in range(PACK):
            copy = turned[-inner % PACK]
            for place in range(1, PACK):
                copy = jnp.where(chunk == place, turned[(place - inner) % PACK], copy)
            copies.append(copy)
        start = pl.multiple_of(tile_index * BW, BW)
        out_ref[pl.ds(start, BW), :] = jnp.concatenate(copies, 0).astype(BF16)
        return carry

    lax.fori_loop(0, 2 * blocks, build, 0, unroll=8)


def occ_kernel(aux_dev, table_ref, turned_ref, *rest):
    x_refs, (mo_ref, wide, held) = rest[:NEAR], rest[NEAR:]
    far_count = x_refs[0].shape[0]
    devices = far_count * NEAR
    rows = table_ref.shape[1] // PACK
    out_rows, aux, _ = mo_ref.shape
    me = lax.axis_index("basis")
    turn, first = me % PACK, me // BW * (out_rows * PACK)
    for near in range(NEAR):
        for far in range(far_count):
            start = pl.multiple_of((me ^ (far * NEAR + near)) * aux_dev * rows, aux_dev * rows)
            wide[pl.ds(start, aux_dev * rows), :] = x_refs[near][far].astype(F32)
    for r in range(rows):
        row = by_slot(wide, aux_dev, rows, devices, r)
        for steps in range(PACK):
            start = (steps * rows + r) * aux
            held[start : start + aux, :] = (
                pltpu.roll(row, steps * BW, 1) if steps else row
            ).astype(BF16)
    none = PACK * rows
    held[none * aux : (none + 1) * aux, :] = jnp.zeros((aux, LANES), BF16)
    in_chunk = [onehot(iota((aux, LANES), 1) // BW == place) for place in range(PACK)]
    of_chunk = [onehot(iota((2 * BW, LANES), 1) // BW == place) for place in range(PACK)]

    def multiply(r, carry):
        parts, blocks = [], []
        for place in range(PACK):
            s = first + (place + PACK - turn) % PACK * out_rows + r
            for j in range(2):
                found = table_ref[2 + j, s] - 1
                source = jnp.maximum(found, 0)
                target = (2 * place + j) % PACK
                steps = (target + 2 * PACK - source // rows - turn) % PACK
                index = jnp.where(found < 0, none, steps * rows + source % rows)
                start = pl.multiple_of(index * aux, aux)
                parts.append(held[pl.ds(start, aux), :] * in_chunk[target])
            a = pl.multiple_of(table_ref[0, s] * 2 * BW, 2 * BW)
            blocks.append(turned_ref[pl.ds(a, 2 * BW), :] * of_chunk[place])
        left = jnp.concatenate([sum(parts[1:PACK], parts[0]), sum(parts[PACK + 1 :], parts[PACK])], 1)
        mo_ref[r] = mm(left, jnp.concatenate(blocks, 0)).astype(BF16)
        return carry

    lax.fori_loop(0, out_rows, multiply, 0, unroll=4)


def gram_kernel(aux_dev, mo_hbm, xm_ref, out_ref, mo_ref, wide, sem):
    fetch = pltpu.make_async_copy(mo_hbm, mo_ref, sem)
    fetch.start()
    devices, rows_all, _ = xm_ref.shape
    rows = rows_all // aux_dev
    aux = aux_dev * devices
    widen(xm_ref, rows_all, wide)
    fetch.wait()
    total = jnp.zeros((aux, aux), F32)
    for r in range(rows):
        total = total + mm_nt(mo_ref[r], by_slot(wide, aux_dev, rows, devices, r).astype(BF16))
    out_ref[...] = jnp.concatenate(
        [total[aux_i * devices : (aux_i + 1) * devices, :] for aux_i in range(aux_dev)], 1
    )


def sum_kernel(aux_dev, part_ref, out_ref):
    devices, width = part_ref.shape
    aux = aux_dev * devices
    total = jnp.sum(part_ref[...], axis=0, keepdims=True)
    lane, col = iota((width, aux), 0), iota((width, aux), 1)
    for row in range(aux_dev):
        chosen = lane == row * aux + col % aux_dev * devices + col // aux_dev
        out_ref[row : row + 1, :] = jnp.dot(
            jnp.broadcast_to(total, (8, width)),
            jnp.where(chosen, 1.0, 0.0),
            precision=lax.Precision.HIGHEST,
            preferred_element_type=F32,
        )[0:1, :]


def call(kernel, outs, scratch, places, args, name, micros, mib=20):
    spaces = {"s": pltpu.SMEM, "v": pltpu.VMEM, "a": pl.ANY}
    return pl.pallas_call(
        kernel,
        out_shape=outs,
        in_specs=[pl.BlockSpec(memory_space=spaces[place]) for place in places],
        out_specs=jax.tree.map(lambda _: pl.BlockSpec(memory_space=pltpu.VMEM), outs),
        scratch_shapes=scratch,
        compiler_params=pltpu.CompilerParams(vmem_limit_bytes=mib * 1024 * 1024),
        cost_estimate=pl.CostEstimate(flops=micros * 1_000_000_000, bytes_accessed=micros * 3_000_000, transcendentals=0),
        name=name,
    )(*args)


def exchange(x):
    return lax.all_to_all(x, "basis", split_axis=0, concat_axis=0, tiled=True)


def permute(x, devices, step):
    return lax.ppermute(x, "basis", [(i, i ^ step) for i in range(devices)])


def body(devices, coulomb, occ_tiles, virt_tiles, tile_count, tile_col, dens_col):
    aux_dev, blocks, slots_row, _ = coulomb.shape
    slots = blocks * slots_row
    live = slots // 2
    halves = devices // BW
    aux = aux_dev * devices
    rows_t = live // PACK
    rows_m = live // halves // PACK
    shape, vmem, dma = jax.ShapeDtypeStruct, pltpu.VMEM, pltpu.SemaphoreType.DMA

    outer = devices // NEAR
    dens = call(
        format_kernel,
        shape((devices, 4 * GROUPS, LANES), BF16),
        [vmem((2, TILE), BF16), vmem((2, TILE), BF16), vmem((4 * GROUPS, LANES), F32), dma((2,))],
        "aa",
        (virt_tiles.reshape(2, TILE), occ_tiles.reshape(2, TILE)),
        "format",
        1,
        60,
    )
    dens = exchange(dens)
    block = (aux_dev * rows_t, LANES)
    counts = tile_count.reshape(1, blocks)
    tiles = coulomb.reshape(aux_dev, slots, TILE)
    *xt, gathered, table, perm = call(
        functools.partial(prepare_kernel, halves),
        (
            *[shape((NEAR,) + block, BF16)] * outer,
            shape((live * 2 * GROUPS, 2 * LANES), BF16),
            shape((8, live), I32),
            shape((TILE, TILE), BF16),
        ),
        [
            vmem((1, blocks), I32),
            vmem((slots_row, blocks), I32),
            vmem((2, blocks), I32),
            vmem((aux_dev, slots, TILE), BF16),
            vmem((devices,) + block, BF16),
            vmem((aux_dev * live, TILE), F32),
            vmem((live * 4 * GROUPS, LANES), F32),
            vmem((slots, TILE), BF16),
            vmem((aux_dev * live, TILE), BF16),
            dma((4,)),
        ],
        "aaaa",
        (counts, tile_col.T, dens_col.T, tiles),
        "prepare",
        5,
        60,
    )
    for far in range(1, outer):
        xt[far] = permute(xt[far], devices, far * NEAR)
    xm, token = call(
        functools.partial(virt_kernel, aux_dev, halves),
        (shape((devices, aux_dev * rows_m, LANES), BF16), shape((8, LANES), F32)),
        [
            pltpu.SMEM((8, live), I32),
            vmem((devices, 4 * GROUPS, LANES), BF16),
            vmem((live * 2 * GROUPS, 2 * LANES), BF16),
            vmem((TILE, TILE), BF16),
            vmem((blocks * 2 * LANES, LANES), BF16),
            vmem((live * 2 * GROUPS, LANES), F32),
            vmem((aux_dev * live, TILE), BF16),
            vmem((aux_dev * live, TILE), F32),
            dma((4,)),
        ],
        "aaaa",
        (table, dens, gathered, perm),
        "virt",
        100,
        60,
    )
    xm = exchange(xm)
    xt = list(call(
        regroup_kernel,
        (shape((outer,) + block, BF16),) * NEAR,
        [],
        "v" * (outer + 1),
        (token, *xt),
        "regroup",
        1,
    ))
    for near in range(1, NEAR):
        xt[near] = permute(xt[near], devices, near)
    turned = call(
        turn_kernel,
        shape((blocks * 2 * BW, LANES), BF16),
        [
            vmem((blocks * 2 * GROUPS, LANES), F32),
            vmem((2 * blocks, TILE), BF16),
            vmem((blocks * 2 * GROUPS, LANES), F32),
        ],
        "vvv",
        (token, dens, perm),
        "turn",
        1,
    )
    mo = call(
        functools.partial(occ_kernel, aux_dev),
        shape((rows_m, aux, LANES), BF16),
        [
            vmem((devices * aux_dev * rows_t, LANES), F32),
            vmem(((PACK * rows_t + 1) * aux, LANES), BF16),
        ],
        "sv" + "v" * NEAR,
        (table, turned, *xt),
        "occ",
        7,
    )
    part = call(
        functools.partial(gram_kernel, aux_dev),
        shape((devices, aux_dev * aux), F32),
        [
            vmem((rows_m, aux, LANES), BF16),
            vmem((devices * aux_dev * rows_m, LANES), F32),
            dma,
        ],
        "av",
        (mo, xm),
        "gram",
        1,
    )
    part = exchange(part)
    return call(
        functools.partial(sum_kernel, aux_dev), shape((aux_dev, aux), F32), [], "v", (part,), "total", 1
    )


def solution(mesh):
    in_specs = (
        P(("parts", "basis"), None, None, None),
        P(("parts", "basis"), None, None),
        P(("parts", "basis"), None, None),
        P(),
        P(),
        P(),
    )
    out_specs = P(("parts", "basis"), None)
    return jax.shard_map(
        functools.partial(body, mesh.shape["basis"]),
        mesh=mesh,
        in_specs=in_specs,
        out_specs=out_specs,
        check_vma=False,
    )
```

time: 70 us -> 63.8 us (0.911)
  waiting for transfers between devices: 18.7 us -> 5.79 us
  starting transfers between devices: 12.9 us -> 24 us
  local copies, waits for them, and re-layouts: 7.53 us -> 1.53 us
  Pallas kernels: 18.7 us -> 20.4 us
  blocking collectives: 10 us -> 11.5 us
  other arithmetic: 1.46 us -> 0 us
    all_to_all x3 -> x2, waiting for transfers between devices: 18.7 us -> 1.16 us  [exchange(): return lax.all_to_all(x, 'basis', split_axis=0, concat_axis=0, tiled=True)]
    ppermute x0 -> x10, starting transfers between devices: none -> 12 us  [permute(): return lax.ppermute(x, 'basis', [(i, i ^ step) for i in range(devices)])]
    ppermute x0 -> x10, waiting for transfers between devices: none -> 4.62 us  [permute(): return lax.ppermute(x, 'basis', [(i, i ^ step) for i in range(devices)])]
    unnamed x10 -> x12, local copies, waits for them, and re-layouts: 5.22 us -> 1.53 us
    pallas_call x5 -> x8, Pallas kernels: 18.7 us -> 20.4 us  [call(): pl.pallas_call(kernel, out_shape=outs, in_specs=[pl.BlockSpec(memory_spac...]
    reshape x3 -> x0, local copies, waits for them, and re-layouts: 1.48 us -> none  [the longest x1 0.7 us: body(): virt_tiles.reshape(-1, LANES)]
    all_to_all x1, blocking collectives: 10 us -> 11.5 us  [exchange(): return lax.all_to_all(x, 'basis', split_axis=0, concat_axis=0, tiled=True)]
    convert_element_type x2 -> x0, other arithmetic: 1.38 us -> none  [the longest x1 0.7 us: body(): cols = jnp.where(live_slot, tile_col, -1).astype(F32).reshape(1, slots)]
  transfers between devices with their start and end apart: 3 -> 12, of which waited for: 3 -> 4; matrix products, arithmetic and copies ran while one was open for 2% -> 0% of each run, Pallas kernels for 25% -> 27%
where the time goes in v1:
time: 63.8 us; the launch traced here: 63.4 us
  starting transfers between devices  24 us (38%)
  Pallas kernels  20.4 us (32%)
  blocking collectives  11.5 us (18%)
  waiting for transfers between devices  5.79 us (9%)
  local copies, waits for them, and re-layouts  1.53 us (2%)
    pallas_call x8, Pallas kernels, call(): pl.pallas_call(kernel, out_shape=outs, in_specs=[pl.BlockSpec(memory_spac...  20.4 us
    ppermute x10, starting transfers between devices, permute(): return lax.ppermute(x, 'basis', [(i, i ^ step) for i in range(devices)])  12 us
    all_to_all x2, starting transfers between devices, exchange(): return lax.all_to_all(x, 'basis', split_axis=0, concat_axis=0, tiled=True)  12 us
    all_to_all x1, blocking collectives, exchange(): return lax.all_to_all(x, 'basis', split_axis=0, concat_axis=0, tiled=True)  11.5 us
    ppermute x10, waiting for transfers between devices, permute(): return lax.ppermute(x, 'basis', [(i, i ^ step) for i in range(devices)])  4.62 us
    unnamed x12, local copies, waits for them, and re-layouts  1.53 us
  transfers between devices with their start and end apart: 12, of which 4 were waited for; matrix products, arithmetic and copies ran while one was open for 0% of the time, Pallas kernels for 27%

profile of v1, /device:TPU:0, one launch (start us, length us, event | category | flops | bytes accessed | tf_op | source)
XLA Modules:
  0.0 63.4 jit_solution(15662721601650482887)
XLA Ops:
  0.0 1.4 %format.1 = bf16[32,32,128]{2,1,0:T(8,128)(2,1)} custom-call(bf16[2,1024]{1,0:T(2,128)(2,1)} %bitcast.13, bf16[2,1024]{1,0:T(2,128)(2,1)} %bitcast.14), custom_call_target="tpu_custom_call" | custom-call | flops 1000000000 | bytes 3000000 | tf_op jit(solution)/shard_map/format/pallas_call | solution.py:364
  1.4 7.3 %all-to-all-start = ((bf16[32,32,128]{2,1,0:T(8,128)(2,1)}), bf16[32,32,128]{2,1,0:T(8,128)(2,1)S(1)}, u32[]{:S(2)}, u32[]{:S(2)}) async-start(bf16[32,32,128]{2,1,0:T(8,128)(2,1)} %format.1), calls=%async_computation | async-start | bytes 524288 | tf_op jit(solution)/shard_map/all_to_all | solution.py:377
  8.8 5.0 %prepare.1 = (bf16[8,64,128]{2,1,0:T(8,128)(2,1)}, bf16[8,64,128]{2,1,0:T(8,128)(2,1)}, bf16[8,64,128]{2,1,0:T(8,128)(2,1)}, bf16[8,64,128]{2,1,0:T(8,128)(2,1)}...) custom-call(s32[1,32]{1,0:T(1,128)} %bitcast.17, s32[8,32]{1,0:T(8,128)} %bitcast.15, ...), custom_call_target="tpu_custom_call" | custom-call | flops 5000000000 | bytes 15000000 | tf_op jit(solution)/shard_map/prepare/pallas_call | solution.py:364
  13.8 1.8 %collective-permute-start = (bf16[8,64,128]{2,1,0:T(8,128)(2,1)}, bf16[8,64,128]{2,1,0:T(8,128)(2,1)S(1)}, u32[]{:S(2)}, u32[]{:S(2)}) collective-permute-start(bf16[8,64,128]{2,1,0:T(8,128)(2,1)} %get-tuple-element.27), channel_id=1, source_target_pairs={{0,8},{1,9},{2,10},{3,11},{4,12},{5,13},{6,14},{7,15},{8,0},{9,1},... | collective-permute-start | bytes 393224 | tf_op jit(solution)/shard_map/ppermute | solution.py:381
  15.6 2.4 %collective-permute-start.1 = (bf16[8,64,128]{2,1,0:T(8,128)(2,1)}, bf16[8,64,128]{2,1,0:T(8,128)(2,1)S(1)}, u32[]{:S(2)}, u32[]{:S(2)}) collective-permute-start(bf16[8,64,128]{2,1,0:T(8,128)(2,1)} %get-tuple-element.28), channel_id=1, source_target_pairs={{0,16},{1,17},{2,18},{3,19},{4,20},{5,21},{6,22},{7,23},{8,24},{9,... | collective-permute-start | bytes 393224 | tf_op jit(solution)/shard_map/ppermute | solution.py:381
  18.0 0.2 collective-permute-start.2
  18.2 1.2 %all-to-all-done.dens_hbm.dens_ref = bf16[32,32,128]{2,1,0:T(8,128)(2,1)S(1)} async-done(((bf16[32,32,128]{2,1,0:T(8,128)(2,1)}), bf16[32,32,128]{2,1,0:T(8,128)(2,1)S(1)}, u32[]{:S(2)}, u32[]{:S(2)}) %all-to-all-start) | async-done | bytes 262176 | tf_op jit(solution)/shard_map/all_to_all | solution.py:377
  19.4 0.0 copy-start
  19.4 0.7 %copy-done = bf16[32,32,128]{2,1,0:T(8,128)(2,1)} copy-done((bf16[32,32,128]{2,1,0:T(8,128)(2,1)}, bf16[32,32,128]{2,1,0:T(8,128)(2,1)S(1)}, u32[]{:S(2)}) %copy-start) | copy-done | bytes 262168
  20.1 0.0 copy-start.3
  20.1 5.4 %virt.1 = (bf16[32,64,128]{2,1,0:T(8,128)(2,1)}, f32[8,128]{1,0:T(8,128)}) custom-call(s32[8,128]{1,0:T(8,128)} %get-tuple-element.22.table_hbm.table_ref, bf16[32,32,128]{2,1,0:T(8,128)(2,1)} %copy-done, bf16[2048,256]{1,0:T(8,128)(2,1)} %get-tuple-element.23.a_hbm, bf16[1024,1024]{1,0:T(8,128)(2,1)} %get-tuple-element.24.perm_hbm.perm_ref), custom_call_target="tpu_custom_call" | custom-call | flops 99999997952 | bytes 300000000 | tf_op jit(solution)/shard_map/virt/pallas_call | solution.py:364
  25.5 4.7 %all-to-all-start.1 = ((bf16[32,64,128]{2,1,0:T(8,128)(2,1)}), bf16[32,64,128]{2,1,0:T(8,128)(2,1)S(1)}, u32[]{:S(2)}, u32[]{:S(2)}) async-start(bf16[32,64,128]{2,1,0:T(8,128)(2,1)} %get-tuple-element.38), calls=%async_computation.1 | async-start | bytes 1048576 | tf_op jit(solution)/shard_map/all_to_all | solution.py:377
  30.2 0.0 copy-start.1
  30.2 0.0 copy-start.2
  30.2 0.0 collective-permute-done.refs_1_
  30.2 0.0 collective-permute-done.1.refs_2_
  30.2 0.0 collective-permute-done.2.refs_3_
  30.3 0.0 copy-done.3
  30.3 0.0 copy-start.4
  30.3 0.8 %copy-done.4 = f32[8,128]{1,0:T(8,128)S(1)} copy-done((f32[8,128]{1,0:T(8,128)S(1)}, f32[8,128]{1,0:T(8,128)}, u32[]{:S(2)}) %copy-start.4) | copy-done | bytes 4120
  31.1 0.0 copy-start.5
  31.1 0.3 collective-permute-start.3
  31.5 1.7 %collective-permute-start.4 = (bf16[4,64,128]{2,1,0:T(8,128)(2,1)S(1)}, bf16[4,64,128]{2,1,0:T(8,128)(2,1)S(1)}, u32[]{:S(2)}, u32[]{:S(2)}) collective-permute-start(bf16[4,64,128]{2,1,0:T(8,128)(2,1)S(1)} %get-tuple-element.32), channel_id=1, source_target_pairs={{0,2},{1,3},{2,0},{3,1},{4,6},{5,7},{6,4},{7,5},{8,10},{9,11},{10,... | collective-permute-start | bytes 196616 | tf_op jit(solution)/shard_map/ppermute | solution.py:381
  33.1 0.0 collective-permute-start.5
  33.2 1.7 %collective-permute-start.6 = (bf16[4,64,128]{2,1,0:T(8,128)(2,1)S(1)}, bf16[4,64,128]{2,1,0:T(8,128)(2,1)S(1)}, u32[]{:S(2)}, u32[]{:S(2)}) collective-permute-start(bf16[4,64,128]{2,1,0:T(8,128)(2,1)S(1)} %get-tuple-element.34), channel_id=1, source_target_pairs={{0,4},{1,5},{2,6},{3,7},{4,0},{5,1},{6,2},{7,3},{8,12},{9,13},{10,... | collective-permute-start | bytes 196616 | tf_op jit(solution)/shard_map/ppermute | solution.py:381
  34.8 0.1 collective-permute-start.7
  35.0 0.0 collective-permute-done.3.rest_1_
  35.0 2.6 %collective-permute-start.8 = (bf16[4,64,128]{2,1,0:T(8,128)(2,1)S(1)}, bf16[4,64,128]{2,1,0:T(8,128)(2,1)S(1)}, u32[]{:S(2)}, u32[]{:S(2)}) collective-permute-start(bf16[4,64,128]{2,1,0:T(8,128)(2,1)S(1)} %get-tuple-element.36), channel_id=1, source_target_pairs={{0,6},{1,7},{2,4},{3,5},{4,2},{5,3},{6,0},{7,1},{8,14},{9,15},{10,... | collective-permute-start | bytes 196616 | tf_op jit(solution)/shard_map/ppermute | solution.py:381
  37.5 1.3 %collective-permute-done.4.rest_2_ = bf16[4,64,128]{2,1,0:T(8,128)(2,1)S(1)} collective-permute-done((bf16[4,64,128]{2,1,0:T(8,128)(2,1)S(1)}, bf16[4,64,128]{2,1,0:T(8,128)(2,1)S(1)}, u32[]{:S(2)}, u32[]{:S(2)}) %collective-permute-start.4) | collective-permute-done | bytes 65568 | tf_op jit(solution)/shard_map/ppermute | solution.py:381
  38.9 1.2 %collective-permute-start.9 = (bf16[4,64,128]{2,1,0:T(8,128)(2,1)S(1)}, bf16[4,64,128]{2,1,0:T(8,128)(2,1)S(1)}, u32[]{:S(2)}, u32[]{:S(2)}) collective-permute-start(bf16[4,64,128]{2,1,0:T(8,128)(2,1)S(1)} %get-tuple-element.37), channel_id=1, source_target_pairs={{0,7},{1,6},{2,5},{3,4},{4,3},{5,2},{6,1},{7,0},{8,15},{9,14},{10,... | collective-permute-start | bytes 196616 | tf_op jit(solution)/shard_map/ppermute | solution.py:381
  40.0 0.0 copy-done.1
  40.0 0.0 copy-done.2
  40.0 1.3 %turn.1.turned_ref = bf16[2048,128]{1,0:T(8,128)(2,1)S(1)} custom-call(f32[8,128]{1,0:T(8,128)S(1)} %copy-done.4, bf16[32,32,128]{2,1,0:T(8,128)(2,1)S(1)} %copy-done.1, bf16[1024,1024]{1,0:T(8,128)(2,1)S(1)} %copy-done.2), custom_call_target="tpu_custom_call" | custom-call | flops 1000000000 | bytes 3000000 | tf_op jit(solution)/shard_map/turn/pallas_call | solution.py:364
  41.3 0.0 collective-permute-done.5.rest_3_
  41.3 0.0 collective-permute-done.6.rest_4_
  41.4 2.3 %collective-permute-done.7.rest_5_ = bf16[4,64,128]{2,1,0:T(8,128)(2,1)S(1)} collective-permute-done((bf16[4,64,128]{2,1,0:T(8,128)(2,1)S(1)}, bf16[4,64,128]{2,1,0:T(8,128)(2,1)S(1)}, u32[]{:S(2)}, u32[]{:S(2)}) %collective-permute-start.7) | collective-permute-done | bytes 65568 | tf_op jit(solution)/shard_map/ppermute | solution.py:381
  43.6 0.0 collective-permute-done.8.rest_6_
  43.6 1.0 %collective-permute-done.9.rest_7_ = bf16[4,64,128]{2,1,0:T(8,128)(2,1)S(1)} collective-permute-done((bf16[4,64,128]{2,1,0:T(8,128)(2,1)S(1)}, bf16[4,64,128]{2,1,0:T(8,128)(2,1)S(1)}, u32[]{:S(2)}, u32[]{:S(2)}) %collective-permute-start.9) | collective-permute-done | bytes 65568 | tf_op jit(solution)/shard_map/ppermute | solution.py:381
  44.6 0.0 copy-done.5
  44.6 5.6 %occ.1.mo_hbm = bf16[32,64,128]{2,1,0:T(8,128)(2,1)S(1)} custom-call(s32[8,128]{1,0:T(8,128)S(1)} %copy-done.5, bf16[2048,128]{1,0:T(8,128)(2,1)S(1)} %turn.1.turned_ref, bf16[4,64,128]{2,1,0:T(8,128)(2,1)S(1)} %get-tuple-element.30.rest_0_, bf16[4,64,128]{2,1,0:T(8,128)(2,1)S(1)} %collective-permute-done.3.rest_1_, ...), custom_call_target="tpu_custom_call" | custom-call | flops 7000000000 | bytes 21000000 | tf_op jit(solution)/shard_map/occ/pallas_call | solution.py:364
  50.2 0.0 all-to-all-done.1.xm_ref
  50.2 0.9 %gram.1 = f32[32,128]{1,0:T(8,128)S(1)} custom-call(bf16[32,64,128]{2,1,0:T(8,128)(2,1)S(1)} %occ.1.mo_hbm, bf16[32,64,128]{2,1,0:T(8,128)(2,1)S(1)} %all-to-all-done.1.xm_ref), custom_call_target="tpu_custom_call" | custom-call | flops 1000000000 | bytes 3000000 | tf_op jit(solution)/shard_map/gram/pallas_call | solution.py:364
  51.1 11.5 %all_to_all.21 = f32[32,1,128]{2,1,0:T(1,128)S(1)} all-to-all(f32[32,1,128]{2,1,0:T(1,128)S(1)} %bitcast.10), channel_id=1, replica_groups=mesh['parts'=1,'basis'=32] {'basis'}, dimensions={0} | all-to-all | bytes 32768 | tf_op jit(solution)/shard_map/all_to_all | solution.py:377
  62.6 0.8 %total.1 = f32[2,64]{1,0:T(2,128)} custom-call(f32[32,128]{1,0:T(8,128)S(1)} %bitcast.11), custom_call_target="tpu_custom_call" | custom-call | flops 1000000000 | bytes 3000000 | tf_op jit(solution)/shard_map/total/pallas_call | solution.py:364
  (1 shorter events, 0.0 us)
Async XLA Ops:
  1.4 17.9 %all-to-all-start = ((bf16[32,32,128]{2,1,0:T(8,128)(2,1)}), bf16[32,32,128]{2,1,0:T(8,128)(2,1)S(1)}, u32[]{:S(2)}, u32[]{:S(2)}) async-start(bf16[32,32,128]{2,1,0:T(8,128)(2,1)} %format.1), calls=%async_computation | async-start | bytes 524288 | tf_op jit(solution)/shard_map/all_to_all | solution.py:377
  13.8 16.5 %collective-permute-start = (bf16[8,64,128]{2,1,0:T(8,128)(2,1)}, bf16[8,64,128]{2,1,0:T(8,128)(2,1)S(1)}, u32[]{:S(2)}, u32[]{:S(2)}) collective-permute-start(bf16[8,64,128]{2,1,0:T(8,128)(2,1)} %get-tuple-element.27), channel_id=1, source_target_pairs={{0,8},{1,9},{2,10},{3,11},{4,12},{5,13},{6,14},{7,15},{8,0},{9,1},... | collective-permute-start | bytes 393224 | tf_op jit(solution)/shard_map/ppermute | solution.py:381
  15.6 14.6 %collective-permute-start.1 = (bf16[8,64,128]{2,1,0:T(8,128)(2,1)}, bf16[8,64,128]{2,1,0:T(8,128)(2,1)S(1)}, u32[]{:S(2)}, u32[]{:S(2)}) collective-permute-start(bf16[8,64,128]{2,1,0:T(8,128)(2,1)} %get-tuple-element.28), channel_id=1, source_target_pairs={{0,16},{1,17},{2,18},{3,19},{4,20},{5,21},{6,22},{7,23},{8,24},{9,... | collective-permute-start | bytes 393224 | tf_op jit(solution)/shard_map/ppermute | solution.py:381
  18.0 12.2 %collective-permute-start.2 = (bf16[8,64,128]{2,1,0:T(8,128)(2,1)}, bf16[8,64,128]{2,1,0:T(8,128)(2,1)S(1)}, u32[]{:S(2)}, u32[]{:S(2)}) collective-permute-start(bf16[8,64,128]{2,1,0:T(8,128)(2,1)} %get-tuple-element.29), channel_id=1, source_target_pairs={{0,24},{1,25},{2,26},{3,27},{4,28},{5,29},{6,30},{7,31},{8,16},{9,... | collective-permute-start | bytes 393224 | tf_op jit(solution)/shard_map/ppermute | solution.py:381
  19.4 0.7 %copy-start = (bf16[32,32,128]{2,1,0:T(8,128)(2,1)}, bf16[32,32,128]{2,1,0:T(8,128)(2,1)S(1)}, u32[]{:S(2)}) copy-start(bf16[32,32,128]{2,1,0:T(8,128)(2,1)S(1)} %all-to-all-done.dens_hbm.dens_ref) | copy-start | bytes 786436
  20.1 10.2 %copy-start.3 = (bf16[8,64,128]{2,1,0:T(8,128)(2,1)S(1)}, bf16[8,64,128]{2,1,0:T(8,128)(2,1)}, u32[]{:S(2)}) copy-start(bf16[8,64,128]{2,1,0:T(8,128)(2,1)} %get-tuple-element.26.refs_0_) | copy-start | bytes 393220
  25.5 24.7 %all-to-all-start.1 = ((bf16[32,64,128]{2,1,0:T(8,128)(2,1)}), bf16[32,64,128]{2,1,0:T(8,128)(2,1)S(1)}, u32[]{:S(2)}, u32[]{:S(2)}) async-start(bf16[32,64,128]{2,1,0:T(8,128)(2,1)} %get-tuple-element.38), calls=%async_computation.1 | async-start | bytes 1048576 | tf_op jit(solution)/shard_map/all_to_all | solution.py:377
  30.2 9.8 %copy-start.1 = (bf16[32,32,128]{2,1,0:T(8,128)(2,1)S(1)}, bf16[32,32,128]{2,1,0:T(8,128)(2,1)}, u32[]{:S(2)}) copy-start(bf16[32,32,128]{2,1,0:T(8,128)(2,1)} %copy-done) | copy-start | bytes 786436
  30.2 9.8 %copy-start.2 = (bf16[1024,1024]{1,0:T(8,128)(2,1)S(1)}, bf16[1024,1024]{1,0:T(8,128)(2,1)}, u32[]{:S(2)}) copy-start(bf16[1024,1024]{1,0:T(8,128)(2,1)} %get-tuple-element.24.perm_hbm.perm_ref) | copy-start | bytes 6291460
  30.3 0.8 %copy-start.4 = (f32[8,128]{1,0:T(8,128)S(1)}, f32[8,128]{1,0:T(8,128)}, u32[]{:S(2)}) copy-start(f32[8,128]{1,0:T(8,128)} %get-tuple-element.25.token_ref) | copy-start | bytes 12292
  31.1 13.5 %copy-start.5 = (s32[8,128]{1,0:T(8,128)S(1)}, s32[8,128]{1,0:T(8,128)}, u32[]{:S(2)}) copy-start(s32[8,128]{1,0:T(8,128)} %get-tuple-element.22.table_hbm.table_ref) | copy-start | bytes 12292
  31.1 3.8 %collective-permute-start.3 = (bf16[4,64,128]{2,1,0:T(8,128)(2,1)S(1)}, bf16[4,64,128]{2,1,0:T(8,128)(2,1)S(1)}, u32[]{:S(2)}, u32[]{:S(2)}) collective-permute-start(bf16[4,64,128]{2,1,0:T(8,128)(2,1)S(1)} %get-tuple-element.31), channel_id=1, source_target_pairs={{0,1},{1,0},{2,3},{3,2},{4,5},{5,4},{6,7},{7,6},{8,9},{9,8},{10,11... | collective-permute-start | bytes 196616 | tf_op jit(solution)/shard_map/ppermute | solution.py:381
  31.5 7.4 %collective-permute-start.4 = (bf16[4,64,128]{2,1,0:T(8,128)(2,1)S(1)}, bf16[4,64,128]{2,1,0:T(8,128)(2,1)S(1)}, u32[]{:S(2)}, u32[]{:S(2)}) collective-permute-start(bf16[4,64,128]{2,1,0:T(8,128)(2,1)S(1)} %get-tuple-element.32), channel_id=1, source_target_pairs={{0,2},{1,3},{2,0},{3,1},{4,6},{5,7},{6,4},{7,5},{8,10},{9,11},{10,... | collective-permute-start | bytes 196616 | tf_op jit(solution)/shard_map/ppermute | solution.py:381
  33.1 8.2 %collective-permute-start.5 = (bf16[4,64,128]{2,1,0:T(8,128)(2,1)S(1)}, bf16[4,64,128]{2,1,0:T(8,128)(2,1)S(1)}, u32[]{:S(2)}, u32[]{:S(2)}) collective-permute-start(bf16[4,64,128]{2,1,0:T(8,128)(2,1)S(1)} %get-tuple-element.33), channel_id=1, source_target_pairs={{0,3},{1,2},{2,1},{3,0},{4,7},{5,6},{6,5},{7,4},{8,11},{9,10},{10,... | collective-permute-start | bytes 196616 | tf_op jit(solution)/shard_map/ppermute | solution.py:381
  33.2 8.2 %collective-permute-start.6 = (bf16[4,64,128]{2,1,0:T(8,128)(2,1)S(1)}, bf16[4,64,128]{2,1,0:T(8,128)(2,1)S(1)}, u32[]{:S(2)}, u32[]{:S(2)}) collective-permute-start(bf16[4,64,128]{2,1,0:T(8,128)(2,1)S(1)} %get-tuple-element.34), channel_id=1, source_target_pairs={{0,4},{1,5},{2,6},{3,7},{4,0},{5,1},{6,2},{7,3},{8,12},{9,13},{10,... | collective-permute-start | bytes 196616 | tf_op jit(solution)/shard_map/ppermute | solution.py:381
  34.8 8.8 %collective-permute-start.7 = (bf16[4,64,128]{2,1,0:T(8,128)(2,1)S(1)}, bf16[4,64,128]{2,1,0:T(8,128)(2,1)S(1)}, u32[]{:S(2)}, u32[]{:S(2)}) collective-permute-start(bf16[4,64,128]{2,1,0:T(8,128)(2,1)S(1)} %get-tuple-element.35), channel_id=1, source_target_pairs={{0,5},{1,4},{2,7},{3,6},{4,1},{5,0},{6,3},{7,2},{8,13},{9,12},{10,... | collective-permute-start | bytes 196616 | tf_op jit(solution)/shard_map/ppermute | solution.py:381
  35.0 8.7 %collective-permute-start.8 = (bf16[4,64,128]{2,1,0:T(8,128)(2,1)S(1)}, bf16[4,64,128]{2,1,0:T(8,128)(2,1)S(1)}, u32[]{:S(2)}, u32[]{:S(2)}) collective-permute-start(bf16[4,64,128]{2,1,0:T(8,128)(2,1)S(1)} %get-tuple-element.36), channel_id=1, source_target_pairs={{0,6},{1,7},{2,4},{3,5},{4,2},{5,3},{6,0},{7,1},{8,14},{9,15},{10,... | collective-permute-start | bytes 196616 | tf_op jit(solution)/shard_map/ppermute | solution.py:381
  38.9 5.7 %collective-permute-start.9 = (bf16[4,64,128]{2,1,0:T(8,128)(2,1)S(1)}, bf16[4,64,128]{2,1,0:T(8,128)(2,1)S(1)}, u32[]{:S(2)}, u32[]{:S(2)}) collective-permute-start(bf16[4,64,128]{2,1,0:T(8,128)(2,1)S(1)} %get-tuple-element.37), channel_id=1, source_target_pairs={{0,7},{1,6},{2,5},{3,4},{4,3},{5,2},{6,1},{7,0},{8,15},{9,14},{10,... | collective-permute-start | bytes 196616 | tf_op jit(solution)/shard_map/ppermute | solution.py:381

commit v2 on v1

--- a/solution.py
+++ b/solution.py
@@ -60,23 +60,19 @@
                 )
 
 
-def format_kernel(virt_hbm, occ_hbm, out_ref, virt_ref, occ_ref, own, sems):
-    fetches = [
-        pltpu.make_async_copy(virt_hbm, virt_ref, sems.at[0]),
-        pltpu.make_async_copy(occ_hbm, occ_ref, sems.at[1]),
-    ]
-    for fetch in fetches:
-        fetch.start()
-    for fetch in fetches:
-        fetch.wait()
-    virt, occ = virt_ref[...].astype(F32), occ_ref[...].astype(F32)
+def as_rows(tiles, rows_ref):
     for group in range(GROUPS):
-        span = slice(group * LANES, (group + 1) * LANES)
-        own[pl.ds(group, 2, stride=GROUPS), :] = virt[:, span]
-        own[pl.ds(2 * GROUPS + group, 2, stride=GROUPS), :] = occ[:, span]
-    own_tiles = own[...].astype(BF16)
+        rows_ref[pl.ds(group, 2, stride=GROUPS), :] = tiles[0:2, group * LANES : (group + 1) * LANES]
+    return rows_ref[...].astype(BF16)
+
+
+def format_kernel(virt_hbm, out_ref, virt_ref, rows_ref, sem):
+    fetch = pltpu.make_async_copy(virt_hbm, virt_ref, sem)
+    fetch.start()
+    fetch.wait()
+    own = as_rows(virt_ref[...].astype(F32), rows_ref)
     for d in range(out_ref.shape[0]):
-        out_ref[d] = own_tiles
+        out_ref[d] = own
 
 
 def index_slots(count_ref, cols_ref):
@@ -106,30 +102,41 @@
     return fetches
 
 
-def prepare_kernel(copies, count_hbm, cols_hbm, dens_hbm, t_hbm, *rest):
-    outer = len(rest) - 13
-    x_refs, (a_ref, table_ref, perm_ref, count_ref, cols_ref, dens_ref, t_ref, xt_ref, flat, planes,
-             lined, swapped, sems) = rest[:outer], rest[outer:]
+def prepare_kernel(copies, count_hbm, cols_hbm, dens_hbm, occ_hbm, t_hbm, *rest):
+    outer = len(rest) - 16
+    x_refs, (a_ref, table_ref, perm_hbm, perm_ref, count_ref, cols_ref, dens_ref, occ_ref, t_ref,
+             rows_ref, xt_ref, flat, planes, lined, swapped, sems) = rest[:outer], rest[outer:]
     fetches = start_fetches(
-        ((count_hbm, count_ref), (cols_hbm, cols_ref), (dens_hbm, dens_ref), (t_hbm, t_ref)), sems
+        ((count_hbm, count_ref), (cols_hbm, cols_ref), (dens_hbm, dens_ref), (occ_hbm, occ_ref),
+         (t_hbm, t_ref)),
+        sems,
     )
     aux_dev, slots, _ = t_ref.shape
     live = table_ref.shape[1]
     blocks = cols_ref.shape[1]
     spread_tiles(perm_ref)
-    for fetch in fetches[:3]:
+    keep_perm = pltpu.make_async_copy(perm_ref, perm_hbm, sems.at[5])
+    keep_perm.start()
+    for fetch in fetches[:4]:
         fetch.wait()
+    occ = jnp.concatenate(
+        [occ_ref[...].astype(F32), jnp.zeros((2 * GROUPS - 2, TILE), F32)], 0
+    ).astype(BF16)
+    own = as_rows(mm(occ, perm_ref[...]), rows_ref)
     row_of, cols, compact = index_slots(count_ref, cols_ref)
     keep = keep_live(compact, live)
-    fetches[3].wait()
+    fetches[4].wait()
     for aux in range(aux_dev):
         swapped[aux * live : (aux + 1) * live, :] = mm(keep, t_ref[aux]).astype(BF16)
     flat[...] = mm(swapped[...], perm_ref[...])
     me = lax.axis_index("basis")
     for copy in range(copies):
         pack_columns(flat, xt_ref, aux_dev, 0, live, live // PACK, lambda n: (copy * BW + n) ^ me)
+    height = xt_ref.shape[1]
     for far, x_ref in enumerate(x_refs):
-        x_ref[...] = xt_ref[far * NEAR : (far + 1) * NEAR]
+        for near in range(NEAR):
+            x_ref[near * height : (near + 1) * height, :] = xt_ref[far * NEAR + near]
+        x_ref[NEAR * height :, :] = own
 
     sub = iota((LANES, slots), 0)
     facts = jnp.where(sub == 0, row_of, jnp.where(sub == 1, cols, 0.0)).astype(BF16)
@@ -137,7 +144,13 @@
     own_facts = mm_nt(keep, facts)
     own_row, own_col = own_facts[:, 0:1], own_facts[:, 1:2]
     block = iota((live, blocks), 1).astype(F32)
-    table_ref[0:2, :] = mm_nt(facts, keep)[0:2, :].astype(I32)
+    own_table = mm_nt(facts, keep)[0:2, :].astype(I32)
+    table_ref[0:1, :] = own_table[0:1, :] * (2 * BW)
+    table_ref[1:2, :] = own_table[1:2, :] * (2 * LANES)
+    turn = me % PACK
+    part, rows = live // copies, live // PACK
+    out_place = ((iota((1, live), 1) + live - me // BW * part) // (part // PACK) + turn) % PACK
+    aux = aux_dev * len(x_refs) * NEAR
     virt_pick = []
     for j in range(2):
         partner = dens_ref[j : j + 1, :].astype(F32)
@@ -147,7 +160,11 @@
         )
         virt_pick.append(onehot((own_row == row_of) & (col_partner == cols)))
         occ_pick = onehot((row_partner == row_of) & (own_col == cols))
-        table_ref[2 + j : 3 + j, :] = mm_nt(places, occ_pick)[0:1, :].astype(I32)
+        found = mm_nt(places, occ_pick)[0:1, :].astype(I32) - 1
+        source = jnp.maximum(found, 0)
+        steps = (out_place * 2 + j + 3 * PACK - source // rows - turn) % PACK
+        index = jnp.where(found < 0, PACK * rows, steps * rows + source % rows)
+        table_ref[2 + j : 3 + j, :] = index * aux
     table_ref[4:8, :] = jnp.zeros((4, live), I32)
     lane = iota((LANES, LANES), 0)
     x = lane % BW
@@ -172,20 +189,19 @@
     half = live * 2 * GROUPS
     for j in range(2):
         a_ref[:, j * LANES : (j + 1) * LANES] = planes[j * half : (j + 1) * half, :].astype(BF16)
-
-
-def virt_kernel(aux_dev, halves, table_hbm, dens_hbm, a_hbm, perm_hbm, xm_ref, token_ref,
-                table_ref, dens_ref, a_ref, perm_ref, weights, result, swapped, flat, sems):
-    fetch_dens, fetch_table, fetch_a, fetch_perm = start_fetches(
-        ((dens_hbm, dens_ref), (table_hbm, table_ref), (a_hbm, a_ref), (perm_hbm, perm_ref)), sems
-    )
+    keep_perm.wait()
+
+
+def virt_kernel(aux_dev, halves, table_hbm, dens_ref, a_ref, perm_hbm, xm_ref, token_ref,
+                table_ref, perm_ref, weights, result, swapped, flat, sems):
+    fetch_table, fetch_perm = start_fetches(((table_hbm, table_ref), (perm_hbm, perm_ref)), sems)
     live = table_ref.shape[1]
     token_ref[...] = jnp.zeros(token_ref.shape, F32)
     blocks, rows, _ = dens_ref.shape
     chunk = iota((GROUPS, LANES), 1) // BW
 
     def build(e, carry):
-        tiles = dens_ref[e, : 2 * GROUPS, :].astype(F32)
+        tiles = dens_ref[e].astype(F32)
         for j in range(2):
             tile = tiles[j * GROUPS : (j + 1) * GROUPS, :]
             turned = [tile] + [pltpu.roll(tile, d * BW, 1) for d in range(1, PACK)]
@@ -201,28 +217,26 @@
                     weights[pl.ds(start, 2 * GROUPS), :] = jnp.concatenate(both, 0).astype(BF16)
         return carry
 
-    fetch_dens.wait()
-    lax.fori_loop(0, blocks, build, 0, unroll=4)
+    lax.fori_loop(0, blocks, build, 0, unroll=8)
     fetch_table.wait()
-    fetch_a.wait()
 
     def multiply(step, carry):
-        for inner in range(32):
-            s = step * 32 + inner
+        for inner in range(64):
+            s = step * 64 + inner
             start = pl.multiple_of(s * 2 * GROUPS, 2 * GROUPS)
-            e = pl.multiple_of(table_ref[1, s] * 2 * LANES, 2 * LANES)
+            e = pl.multiple_of(table_ref[1, s], 2 * LANES)
             result[pl.ds(start, 2 * GROUPS), :] = mm(
                 a_ref[pl.ds(start, 2 * GROUPS), :], weights[pl.ds(e, 2 * LANES), :]
             )
         return carry
 
-    lax.fori_loop(0, live // 32, multiply, 0)
-    fetch_perm.wait()
+    lax.fori_loop(0, live // 64, multiply, 0)
     for aux in range(aux_dev):
         for group in range(GROUPS):
             swapped[aux * live : (aux + 1) * live, group * LANES : (group + 1) * LANES] = (
                 result[pl.ds(aux * GROUPS + group, live, stride=2 * GROUPS), :].astype(BF16)
             )
+    fetch_perm.wait()
     flat[...] = mm(swapped[...], perm_ref[...])
     part = live // halves
     for half in range(halves):
@@ -232,9 +246,15 @@
 
 def regroup_kernel(token_ref, *refs):
     sources, targets = refs[:-NEAR], refs[-NEAR:]
-    for near in range(NEAR):
+    outer = len(sources)
+    height = (sources[0].shape[0] - 2 * GROUPS) // NEAR
+    for near, target in enumerate(targets):
         for far, source in enumerate(sources):
-            targets[near][far] = source[near]
+            target[far * height : (far + 1) * height, :] = (
+                source[near * height : (near + 1) * height, :]
+            )
+            tiles = outer * height + far * 2 * GROUPS
+            target[tiles : tiles + 2 * GROUPS, :] = source[NEAR * height :, :]
 
 
 def by_slot(wide, aux_dev, rows, devices, r):
@@ -250,20 +270,25 @@
         wide[d * rows : (d + 1) * rows, :] = source_ref[d, :rows, :].astype(F32)
 
 
-def turn_kernel(token_ref, dens_ref, perm_ref, out_ref, tiles, lined, planes):
-    blocks = dens_ref.shape[0]
-    for a in range(blocks):
-        tiles[a * 2 * GROUPS : (a + 1) * 2 * GROUPS, :] = dens_ref[a, 2 * GROUPS :, :].astype(F32)
-    for j in range(2):
-        for group in range(GROUPS):
-            lined[j * blocks : (j + 1) * blocks, group * LANES : (group + 1) * LANES] = (
-                tiles[pl.ds(j * GROUPS + group, blocks, stride=2 * GROUPS), :].astype(BF16)
+def occ_kernel(aux_dev, table_hbm, *rest):
+    x_refs, (mo_ref, table_ref, wide, planes, weights, held, sem) = rest[:NEAR], rest[NEAR:]
+    fetch_table = pltpu.make_async_copy(table_hbm, table_ref, sem)
+    fetch_table.start()
+    rows = table_ref.shape[1] // PACK
+    height = aux_dev * rows
+    outer = x_refs[0].shape[0] // (height + 2 * GROUPS)
+    devices = outer * NEAR
+    out_rows, aux, _ = mo_ref.shape
+    me = lax.axis_index("basis")
+    for near, x_ref in enumerate(x_refs):
+        for far in range(outer):
+            owner = me ^ (far * NEAR + near)
+            wide[pl.ds(pl.multiple_of(owner * height, height), height), :] = (
+                x_ref[far * height : (far + 1) * height, :].astype(F32)
             )
-    turned_tiles = mm(lined[...], perm_ref[...])
-    for j in range(2):
-        for group in range(GROUPS):
-            planes[pl.ds(j * GROUPS + group, blocks, stride=2 * GROUPS), :] = (
-                turned_tiles[j * blocks : (j + 1) * blocks, group * LANES : (group + 1) * LANES]
+            tiles = outer * height + far * 2 * GROUPS
+            planes[pl.ds(pl.multiple_of(owner * 2 * GROUPS, 2 * GROUPS), 2 * GROUPS), :] = (
+                x_ref[tiles : tiles + 2 * GROUPS, :].astype(F32)
             )
     chunk = iota((GROUPS, LANES), 1) // BW
 
@@ -277,24 +302,10 @@
                 copy = jnp.where(chunk == place, turned[(place - inner) % PACK], copy)
             copies.append(copy)
         start = pl.multiple_of(tile_index * BW, BW)
-        out_ref[pl.ds(start, BW), :] = jnp.concatenate(copies, 0).astype(BF16)
+        weights[pl.ds(start, BW), :] = jnp.concatenate(copies, 0).astype(BF16)
         return carry
 
-    lax.fori_loop(0, 2 * blocks, build, 0, unroll=8)
-
-
-def occ_kernel(aux_dev, table_ref, turned_ref, *rest):
-    x_refs, (mo_ref, wide, held) = rest[:NEAR], rest[NEAR:]
-    far_count = x_refs[0].shape[0]
-    devices = far_count * NEAR
-    rows = table_ref.shape[1] // PACK
-    out_rows, aux, _ = mo_ref.shape
-    me = lax.axis_index("basis")
-    turn, first = me % PACK, me // BW * (out_rows * PACK)
-    for near in range(NEAR):
-        for far in range(far_count):
-            start = pl.multiple_of((me ^ (far * NEAR + near)) * aux_dev * rows, aux_dev * rows)
-            wide[pl.ds(start, aux_dev * rows), :] = x_refs[near][far].astype(F32)
+    lax.fori_loop(0, 2 * devices, build, 0, unroll=8)
     for r in range(rows):
         row = by_slot(wide, aux_dev, rows, devices, r)
         for steps in range(PACK):
@@ -306,36 +317,31 @@
     held[none * aux : (none + 1) * aux, :] = jnp.zeros((aux, LANES), BF16)
     in_chunk = [onehot(iota((aux, LANES), 1) // BW == place) for place in range(PACK)]
     of_chunk = [onehot(iota((2 * BW, LANES), 1) // BW == place) for place in range(PACK)]
+    first = me // BW * (out_rows * PACK)
+    bases = [first + (place + PACK - me % PACK) % PACK * out_rows for place in range(PACK)]
+    fetch_table.wait()
 
     def multiply(r, carry):
         parts, blocks = [], []
         for place in range(PACK):
-            s = first + (place + PACK - turn) % PACK * out_rows + r
+            s = bases[place] + r
             for j in range(2):
-                found = table_ref[2 + j, s] - 1
-                source = jnp.maximum(found, 0)
-                target = (2 * place + j) % PACK
-                steps = (target + 2 * PACK - source // rows - turn) % PACK
-                index = jnp.where(found < 0, none, steps * rows + source % rows)
-                start = pl.multiple_of(index * aux, aux)
-                parts.append(held[pl.ds(start, aux), :] * in_chunk[target])
-            a = pl.multiple_of(table_ref[0, s] * 2 * BW, 2 * BW)
-            blocks.append(turned_ref[pl.ds(a, 2 * BW), :] * of_chunk[place])
+                start = pl.multiple_of(table_ref[2 + j, s], aux)
+                parts.append(held[pl.ds(start, aux), :] * in_chunk[(2 * place + j) % PACK])
+            a = pl.multiple_of(table_ref[0, s], 2 * BW)
+            blocks.append(weights[pl.ds(a, 2 * BW), :] * of_chunk[place])
         left = jnp.concatenate([sum(parts[1:PACK], parts[0]), sum(parts[PACK + 1 :], parts[PACK])], 1)
         mo_ref[r] = mm(left, jnp.concatenate(blocks, 0)).astype(BF16)
         return carry
 
-    lax.fori_loop(0, out_rows, multiply, 0, unroll=4)
-
-
-def gram_kernel(aux_dev, mo_hbm, xm_ref, out_ref, mo_ref, wide, sem):
-    fetch = pltpu.make_async_copy(mo_hbm, mo_ref, sem)
-    fetch.start()
+    lax.fori_loop(0, out_rows, multiply, 0, unroll=8)
+
+
+def gram_kernel(aux_dev, mo_ref, xm_ref, out_ref, wide):
     devices, rows_all, _ = xm_ref.shape
     rows = rows_all // aux_dev
     aux = aux_dev * devices
     widen(xm_ref, rows_all, wide)
-    fetch.wait()
     total = jnp.zeros((aux, aux), F32)
     for r in range(rows):
         total = total + mm_nt(mo_ref[r], by_slot(wide, aux_dev, rows, devices, r).astype(BF16))
@@ -359,16 +365,29 @@
         )[0:1, :]
 
 
-def call(kernel, outs, scratch, places, args, name, micros, mib=20):
-    spaces = {"s": pltpu.SMEM, "v": pltpu.VMEM, "a": pl.ANY}
+def is_hbm(out):
+    return getattr(out, "memory_space", None) == pltpu.HBM
+
+
+def call(kernel, outs, scratch, places, args, name, micros, mib=24):
+    specs = {"v": pltpu.VMEM, "m": pltpu.VMEM, "a": pl.ANY, "h": pl.ANY}
+    held = {"m": pltpu.VMEM, "a": pltpu.VMEM, "h": pltpu.HBM}
+    args = [
+        pltpu.with_memory_space_constraint(arg, held[place]) if place in held else arg
+        for place, arg in zip(places, args)
+    ]
     return pl.pallas_call(
         kernel,
         out_shape=outs,
-        in_specs=[pl.BlockSpec(memory_space=spaces[place]) for place in places],
-        out_specs=jax.tree.map(lambda _: pl.BlockSpec(memory_space=pltpu.VMEM), outs),
+        in_specs=[pl.BlockSpec(memory_space=specs[place]) for place in places],
+        out_specs=jax.tree.map(
+            lambda out: pl.BlockSpec(memory_space=pl.ANY if is_hbm(out) else pltpu.VMEM), outs
+        ),
         scratch_shapes=scratch,
         compiler_params=pltpu.CompilerParams(vmem_limit_bytes=mib * 1024 * 1024),
-        cost_estimate=pl.CostEstimate(flops=micros * 1_000_000_000, bytes_accessed=micros * 3_000_000, transcendentals=0),
+        cost_estimate=pl.CostEstimate(
+            flops=micros * 1_000_000_000, bytes_accessed=micros * 3_000_000, transcendentals=0
+        ),
         name=name,
     )(*args)
 
@@ -394,112 +413,103 @@
     outer = devices // NEAR
     dens = call(
         format_kernel,
-        shape((devices, 4 * GROUPS, LANES), BF16),
-        [vmem((2, TILE), BF16), vmem((2, TILE), BF16), vmem((4 * GROUPS, LANES), F32), dma((2,))],
-        "aa",
-        (virt_tiles.reshape(2, TILE), occ_tiles.reshape(2, TILE)),
+        shape((devices, 2 * GROUPS, LANES), BF16),
+        [vmem((2, TILE), BF16), vmem((2 * GROUPS, LANES), F32), dma],
+        "h",
+        (virt_tiles.reshape(2, TILE),),
         "format",
         1,
-        60,
     )
     dens = exchange(dens)
-    block = (aux_dev * rows_t, LANES)
-    counts = tile_count.reshape(1, blocks)
-    tiles = coulomb.reshape(aux_dev, slots, TILE)
+    height = aux_dev * rows_t
     *xt, gathered, table, perm = call(
         functools.partial(prepare_kernel, halves),
         (
-            *[shape((NEAR,) + block, BF16)] * outer,
-            shape((live * 2 * GROUPS, 2 * LANES), BF16),
-            shape((8, live), I32),
-            shape((TILE, TILE), BF16),
+            *[shape((NEAR * height + 2 * GROUPS, LANES), BF16)] * outer,
+            vmem((live * 2 * GROUPS, 2 * LANES), BF16),
+            vmem((8, live), I32),
+            pltpu.HBM((TILE, TILE), BF16),
         ),
         [
+            vmem((TILE, TILE), BF16),
             vmem((1, blocks), I32),
             vmem((slots_row, blocks), I32),
             vmem((2, blocks), I32),
+            vmem((2, TILE), BF16),
             vmem((aux_dev, slots, TILE), BF16),
-            vmem((devices,) + block, BF16),
+            vmem((2 * GROUPS, LANES), F32),
+            vmem((devices, height, LANES), BF16),
             vmem((aux_dev * live, TILE), F32),
             vmem((live * 4 * GROUPS, LANES), F32),
             vmem((slots, TILE), BF16),
             vmem((aux_dev * live, TILE), BF16),
-            dma((4,)),
+            dma((6,)),
         ],
-        "aaaa",
-        (counts, tile_col.T, dens_col.T, tiles),
+        "hhhhh",
+        (
+            tile_count.reshape(1, blocks),
+            tile_col.T,
+            dens_col.T,
+            occ_tiles.reshape(2, TILE),
+            coulomb.reshape(aux_dev, slots, TILE),
+        ),
         "prepare",
         5,
-        60,
     )
     for far in range(1, outer):
         xt[far] = permute(xt[far], devices, far * NEAR)
     xm, token = call(
         functools.partial(virt_kernel, aux_dev, halves),
-        (shape((devices, aux_dev * rows_m, LANES), BF16), shape((8, LANES), F32)),
+        (shape((devices, aux_dev * rows_m, LANES), BF16), vmem((8, LANES), F32)),
         [
             pltpu.SMEM((8, live), I32),
-            vmem((devices, 4 * GROUPS, LANES), BF16),
-            vmem((live * 2 * GROUPS, 2 * LANES), BF16),
             vmem((TILE, TILE), BF16),
             vmem((blocks * 2 * LANES, LANES), BF16),
             vmem((live * 2 * GROUPS, LANES), F32),
             vmem((aux_dev * live, TILE), BF16),
             vmem((aux_dev * live, TILE), F32),
-            dma((4,)),
+            dma((2,)),
         ],
-        "aaaa",
+        "avmh",
         (table, dens, gathered, perm),
         "virt",
         100,
-        60,
     )
     xm = exchange(xm)
     xt = list(call(
         regroup_kernel,
-        (shape((outer,) + block, BF16),) * NEAR,
+        (shape((outer * (height + 2 * GROUPS), LANES), BF16),) * NEAR,
         [],
-        "v" * (outer + 1),
+        "m" + "v" * outer,
         (token, *xt),
         "regroup",
         1,
     ))
     for near in range(1, NEAR):
         xt[near] = permute(xt[near], devices, near)
-    turned = call(
-        turn_kernel,
-        shape((blocks * 2 * BW, LANES), BF16),
-        [
-            vmem((blocks * 2 * GROUPS, LANES), F32),
-            vmem((2 * blocks, TILE), BF16),
-            vmem((blocks * 2 * GROUPS, LANES), F32),
-        ],
-        "vvv",
-        (token, dens, perm),
-        "turn",
-        1,
-    )
     mo = call(
         functools.partial(occ_kernel, aux_dev),
-        shape((rows_m, aux, LANES), BF16),
+        vmem((rows_m, aux, LANES), BF16),
         [
-            vmem((devices * aux_dev * rows_t, LANES), F32),
+            pltpu.SMEM((8, live), I32),
+            vmem((devices * height, LANES), F32),
+            vmem((devices * 2 * GROUPS, LANES), F32),
+            vmem((devices * 2 * BW, LANES), BF16),
             vmem(((PACK * rows_t + 1) * aux, LANES), BF16),
+            dma,
         ],
-        "sv" + "v" * NEAR,
-        (table, turned, *xt),
+        "a" + "v" * NEAR,
+        (table, *xt),
         "occ",
-        7,
+        8,
     )
     part = call(
         functools.partial(gram_kernel, aux_dev),
         shape((devices, aux_dev * aux), F32),
         [
-            vmem((rows_m, aux, LANES), BF16),
             vmem((devices * aux_dev * rows_m, LANES), F32),
-            dma,
         ],
-        "av",
+        "mv",
         (mo, xm),
         "gram",
         1,

time: 63.8 us -> 59.3 us (0.929)
  Pallas kernels: 20.4 us -> 14.4 us
  waiting for transfers between devices: 5.79 us -> 9.55 us
  local copies, waits for them, and re-layouts: 1.53 us -> 0 us
    pallas_call x8 -> x7, Pallas kernels: 20.4 us -> 14.4 us  [call(): pl.pallas_call(kernel, out_shape=outs, in_specs=[pl.BlockSpec(memory_spac...]
    ppermute x10, waiting for transfers between devices: 4.62 us -> 9.54 us  [permute(): return lax.ppermute(x, 'basis', [(i, i ^ step) for i in range(devices)])]
    unnamed x12 -> x0, local copies, waits for them, and re-layouts: 1.53 us -> none
    all_to_all x2, waiting for transfers between devices: 1.16 us -> 0.01 us  [exchange(): return lax.all_to_all(x, 'basis', split_axis=0, concat_axis=0, tiled=True)]
    all_to_all x2, starting transfers between devices: 12 us -> 13.1 us  [exchange(): return lax.all_to_all(x, 'basis', split_axis=0, concat_axis=0, tiled=True)]
    ppermute x10, starting transfers between devices: 12 us -> 10.9 us  [permute(): return lax.ppermute(x, 'basis', [(i, i ^ step) for i in range(devices)])]
  transfers between devices with their start and end apart: 12 -> 12, of which waited for: 4 -> 6; matrix products, arithmetic and copies ran while one was open for 0% -> 0% of each run, Pallas kernels for 27% -> 19%
where the time goes in v2:
time: 59.3 us; the launch traced here: 58.9 us
  starting transfers between devices  24 us (40%)
  Pallas kernels  14.4 us (24%)
  blocking collectives  10.9 us (18%)
  waiting for transfers between devices  9.55 us (16%)
    pallas_call x7, Pallas kernels, call(): pl.pallas_call(kernel, out_shape=outs, in_specs=[pl.BlockSpec(memory_spac...  14.4 us
    all_to_all x2, starting transfers between devices, exchange(): return lax.all_to_all(x, 'basis', split_axis=0, concat_axis=0, tiled=True)  13.1 us
    ppermute x10, starting transfers between devices, permute(): return lax.ppermute(x, 'basis', [(i, i ^ step) for i in range(devices)])  10.9 us
    all_to_all x1, blocking collectives, exchange(): return lax.all_to_all(x, 'basis', split_axis=0, concat_axis=0, tiled=True)  10.9 us
    ppermute x10, waiting for transfers between devices, permute(): return lax.ppermute(x, 'basis', [(i, i ^ step) for i in range(devices)])  9.54 us
  transfers between devices with their start and end apart: 12, of which 6 were waited for; matrix products, arithmetic and copies ran while one was open for 0% of the time, Pallas kernels for 19%

profile of v2, /device:TPU:0, one launch (start us, length us, event | category | flops | bytes accessed | tf_op | source)
XLA Modules:
  0.0 58.9 jit_solution(4081811331499793922)
XLA Ops:
  0.0 1.4 %format.1 = bf16[32,16,128]{2,1,0:T(8,128)(2,1)} custom-call(bf16[2,1024]{1,0:T(2,128)(2,1)} %bitcast.13), custom_call_target="tpu_custom_call" | custom-call | flops 1000000000 | bytes 3000000 | tf_op jit(solution)/shard_map/format/pallas_call | solution.py:379
  1.4 7.3 %all-to-all-start = ((bf16[32,16,128]{2,1,0:T(8,128)(2,1)}), bf16[32,16,128]{2,1,0:T(8,128)(2,1)S(1)}, u32[]{:S(2)}, u32[]{:S(2)}) async-start(bf16[32,16,128]{2,1,0:T(8,128)(2,1)} %format.1), calls=%async_computation | async-start | bytes 262144 | tf_op jit(solution)/shard_map/all_to_all | solution.py:396
  8.7 4.0 %prepare.1 = (bf16[528,128]{1,0:T(8,128)(2,1)S(1)}, bf16[528,128]{1,0:T(8,128)(2,1)S(1)}, bf16[528,128]{1,0:T(8,128)(2,1)S(1)}, bf16[528,128]{1,0:T(8,128)(2,1)S...) custom-call(s32[1,32]{1,0:T(1,128)} %bitcast.17, s32[8,32]{1,0:T(8,128)} %bitcast.14, ...), custom_call_target="tpu_custom_call" | custom-call | flops 5000000000 | bytes 15000000 | tf_op jit(solution)/shard_map/prepare/pallas_call | solution.py:379
  12.7 1.8 %collective-permute-start = (bf16[528,128]{1,0:T(8,128)(2,1)S(1)}, bf16[528,128]{1,0:T(8,128)(2,1)S(1)}, u32[]{:S(2)}, u32[]{:S(2)}) collective-permute-start(bf16[528,128]{1,0:T(8,128)(2,1)S(1)} %get-tuple-element.27), channel_id=1, source_target_pairs={{0,8},{1,9},{2,10},{3,11},{4,12},{5,13},{6,14},{7,15},{8,0},{9,1},... | collective-permute-start | bytes 405512 | tf_op jit(solution)/shard_map/ppermute | solution.py:400
  14.6 2.4 %collective-permute-start.1 = (bf16[528,128]{1,0:T(8,128)(2,1)S(1)}, bf16[528,128]{1,0:T(8,128)(2,1)S(1)}, u32[]{:S(2)}, u32[]{:S(2)}) collective-permute-start(bf16[528,128]{1,0:T(8,128)(2,1)S(1)} %get-tuple-element.28), channel_id=1, source_target_pairs={{0,16},{1,17},{2,18},{3,19},{4,20},{5,21},{6,22},{7,23},{8,24},{9,... | collective-permute-start | bytes 405512 | tf_op jit(solution)/shard_map/ppermute | solution.py:400
  17.0 0.2 collective-permute-start.2
  17.2 0.0 all-to-all-done.dens_ref
  17.2 4.3 %virt.1 = (bf16[32,64,128]{2,1,0:T(8,128)(2,1)}, f32[8,128]{1,0:T(8,128)S(1)}) custom-call(s32[8,128]{1,0:T(8,128)S(1)} %get-tuple-element.22.table_hbm, bf16[32,16,128]{2,1,0:T(8,128)(2,1)S(1)} %all-to-all-done.dens_ref, bf16[2048,256]{1,0:T(8,128)(2,1)S(1)} %get-tuple-element.23.a_ref, bf16[1024,1024]{1,0:T(8,128)(2,1)} %get-tuple-element.24.perm_hbm), custom_call_target="tpu_custom_call" | custom-call | flops 99999997952 | bytes 300000000 | tf_op jit(solution)/shard_map/virt/pallas_call | solution.py:379
  21.5 5.8 %all-to-all-start.1 = ((bf16[32,64,128]{2,1,0:T(8,128)(2,1)}), bf16[32,64,128]{2,1,0:T(8,128)(2,1)S(1)}, u32[]{:S(2)}, u32[]{:S(2)}) async-start(bf16[32,64,128]{2,1,0:T(8,128)(2,1)} %get-tuple-element.38), calls=%async_computation.1 | async-start | bytes 1048576 | tf_op jit(solution)/shard_map/all_to_all | solution.py:396
  27.4 0.0 collective-permute-done.refs_1_
  27.4 0.4 collective-permute-done.1.refs_2_
  27.7 0.0 collective-permute-done.2.refs_3_
  27.7 0.1 regroup.1
  27.8 0.1 collective-permute-start.3
  27.9 1.6 %collective-permute-start.4 = (bf16[320,128]{1,0:T(8,128)(2,1)S(1)}, bf16[320,128]{1,0:T(8,128)(2,1)S(1)}, u32[]{:S(2)}, u32[]{:S(2)}) collective-permute-start(bf16[320,128]{1,0:T(8,128)(2,1)S(1)} %get-tuple-element.32), channel_id=1, source_target_pairs={{0,2},{1,3},{2,0},{3,1},{4,6},{5,7},{6,4},{7,5},{8,10},{9,11},{10,... | collective-permute-start | bytes 245768 | tf_op jit(solution)/shard_map/ppermute | solution.py:400
  29.4 0.3 collective-permute-start.5
  29.7 1.5 %collective-permute-start.6 = (bf16[320,128]{1,0:T(8,128)(2,1)S(1)}, bf16[320,128]{1,0:T(8,128)(2,1)S(1)}, u32[]{:S(2)}, u32[]{:S(2)}) collective-permute-start(bf16[320,128]{1,0:T(8,128)(2,1)S(1)} %get-tuple-element.34), channel_id=1, source_target_pairs={{0,4},{1,5},{2,6},{3,7},{4,0},{5,1},{6,2},{7,3},{8,12},{9,13},{10,... | collective-permute-start | bytes 245768 | tf_op jit(solution)/shard_map/ppermute | solution.py:400
  31.2 0.2 collective-permute-start.7
  31.4 0.0 collective-permute-done.3.rest_1_
  31.4 2.4 %collective-permute-start.8 = (bf16[320,128]{1,0:T(8,128)(2,1)S(1)}, bf16[320,128]{1,0:T(8,128)(2,1)S(1)}, u32[]{:S(2)}, u32[]{:S(2)}) collective-permute-start(bf16[320,128]{1,0:T(8,128)(2,1)S(1)} %get-tuple-element.36), channel_id=1, source_target_pairs={{0,6},{1,7},{2,4},{3,5},{4,2},{5,3},{6,0},{7,1},{8,14},{9,15},{10,... | collective-permute-start | bytes 245768 | tf_op jit(solution)/shard_map/ppermute | solution.py:400
  33.8 2.8 %collective-permute-done.4.rest_2_ = bf16[320,128]{1,0:T(8,128)(2,1)S(1)} collective-permute-done((bf16[320,128]{1,0:T(8,128)(2,1)S(1)}, bf16[320,128]{1,0:T(8,128)(2,1)S(1)}, u32[]{:S(2)}, u32[]{:S(2)}) %collective-permute-start.4) | collective-permute-done | bytes 81952 | tf_op jit(solution)/shard_map/ppermute | solution.py:400
  36.7 0.4 collective-permute-start.9
  37.1 0.4 collective-permute-done.5.rest_3_
  37.5 0.0 collective-permute-done.6.rest_4_
  37.5 1.1 %collective-permute-done.7.rest_5_ = bf16[320,128]{1,0:T(8,128)(2,1)S(1)} collective-permute-done((bf16[320,128]{1,0:T(8,128)(2,1)S(1)}, bf16[320,128]{1,0:T(8,128)(2,1)S(1)}, u32[]{:S(2)}, u32[]{:S(2)}) %collective-permute-start.7) | collective-permute-done | bytes 81952 | tf_op jit(solution)/shard_map/ppermute | solution.py:400
  38.5 3.4 %collective-permute-done.8.rest_6_ = bf16[320,128]{1,0:T(8,128)(2,1)S(1)} collective-permute-done((bf16[320,128]{1,0:T(8,128)(2,1)S(1)}, bf16[320,128]{1,0:T(8,128)(2,1)S(1)}, u32[]{:S(2)}, u32[]{:S(2)}) %collective-permute-start.8) | collective-permute-done | bytes 81952 | tf_op jit(solution)/shard_map/ppermute | solution.py:400
  41.9 1.4 %collective-permute-done.9.rest_7_ = bf16[320,128]{1,0:T(8,128)(2,1)S(1)} collective-permute-done((bf16[320,128]{1,0:T(8,128)(2,1)S(1)}, bf16[320,128]{1,0:T(8,128)(2,1)S(1)}, u32[]{:S(2)}, u32[]{:S(2)}) %collective-permute-start.9) | collective-permute-done | bytes 81952 | tf_op jit(solution)/shard_map/ppermute | solution.py:400
  43.4 3.0 %occ.1.mo_ref = bf16[32,64,128]{2,1,0:T(8,128)(2,1)S(1)} custom-call(s32[8,128]{1,0:T(8,128)S(1)} %get-tuple-element.22.table_hbm, bf16[320,128]{1,0:T(8,128)(2,1)S(1)} %get-tuple-element.30.rest_0_, bf16[320,128]{1,0:T(8,128)(2,1)S(1)} %collective-permute-done.3.rest_1_, bf16[320,128]{1,0:T(8,128)(2,1)S(1)} %collective-permute-done.4.rest_2_, ...), custom_call_target="tpu_custom_call" | custom-call | flops 8000000000 | bytes 24000000 | tf_op jit(solution)/shard_map/occ/pallas_call | solution.py:379
  46.4 0.0 all-to-all-done.1.xm_ref
  46.4 0.8 %gram.1 = f32[32,128]{1,0:T(8,128)S(1)} custom-call(bf16[32,64,128]{2,1,0:T(8,128)(2,1)S(1)} %occ.1.mo_ref, bf16[32,64,128]{2,1,0:T(8,128)(2,1)S(1)} %all-to-all-done.1.xm_ref), custom_call_target="tpu_custom_call" | custom-call | flops 1000000000 | bytes 3000000 | tf_op jit(solution)/shard_map/gram/pallas_call | solution.py:379
  47.3 10.9 %all_to_all.21 = f32[32,1,128]{2,1,0:T(1,128)S(1)} all-to-all(f32[32,1,128]{2,1,0:T(1,128)S(1)} %bitcast.10), channel_id=1, replica_groups=mesh['parts'=1,'basis'=32] {'basis'}, dimensions={0} | all-to-all | bytes 32768 | tf_op jit(solution)/shard_map/all_to_all | solution.py:396
  58.1 0.8 %total.1 = f32[2,64]{1,0:T(2,128)} custom-call(f32[32,128]{1,0:T(8,128)S(1)} %bitcast.11), custom_call_target="tpu_custom_call" | custom-call | flops 1000000000 | bytes 3000000 | tf_op jit(solution)/shard_map/total/pallas_call | solution.py:379
Async XLA Ops:
  1.4 15.8 %all-to-all-start = ((bf16[32,16,128]{2,1,0:T(8,128)(2,1)}), bf16[32,16,128]{2,1,0:T(8,128)(2,1)S(1)}, u32[]{:S(2)}, u32[]{:S(2)}) async-start(bf16[32,16,128]{2,1,0:T(8,128)(2,1)} %format.1), calls=%async_computation | async-start | bytes 262144 | tf_op jit(solution)/shard_map/all_to_all | solution.py:396
  12.7 14.6 %collective-permute-start = (bf16[528,128]{1,0:T(8,128)(2,1)S(1)}, bf16[528,128]{1,0:T(8,128)(2,1)S(1)}, u32[]{:S(2)}, u32[]{:S(2)}) collective-permute-start(bf16[528,128]{1,0:T(8,128)(2,1)S(1)} %get-tuple-element.27), channel_id=1, source_target_pairs={{0,8},{1,9},{2,10},{3,11},{4,12},{5,13},{6,14},{7,15},{8,0},{9,1},... | collective-permute-start | bytes 405512 | tf_op jit(solution)/shard_map/ppermute | solution.py:400
  14.6 13.2 %collective-permute-start.1 = (bf16[528,128]{1,0:T(8,128)(2,1)S(1)}, bf16[528,128]{1,0:T(8,128)(2,1)S(1)}, u32[]{:S(2)}, u32[]{:S(2)}) collective-permute-start(bf16[528,128]{1,0:T(8,128)(2,1)S(1)} %get-tuple-element.28), channel_id=1, source_target_pairs={{0,16},{1,17},{2,18},{3,19},{4,20},{5,21},{6,22},{7,23},{8,24},{9,... | collective-permute-start | bytes 405512 | tf_op jit(solution)/shard_map/ppermute | solution.py:400
  17.0 10.7 %collective-permute-start.2 = (bf16[528,128]{1,0:T(8,128)(2,1)S(1)}, bf16[528,128]{1,0:T(8,128)(2,1)S(1)}, u32[]{:S(2)}, u32[]{:S(2)}) collective-permute-start(bf16[528,128]{1,0:T(8,128)(2,1)S(1)} %get-tuple-element.29), channel_id=1, source_target_pairs={{0,24},{1,25},{2,26},{3,27},{4,28},{5,29},{6,30},{7,31},{8,16},{9,... | collective-permute-start | bytes 405512 | tf_op jit(solution)/shard_map/ppermute | solution.py:400
  21.5 24.9 %all-to-all-start.1 = ((bf16[32,64,128]{2,1,0:T(8,128)(2,1)}), bf16[32,64,128]{2,1,0:T(8,128)(2,1)S(1)}, u32[]{:S(2)}, u32[]{:S(2)}) async-start(bf16[32,64,128]{2,1,0:T(8,128)(2,1)} %get-tuple-element.38), calls=%async_computation.1 | async-start | bytes 1048576 | tf_op jit(solution)/shard_map/all_to_all | solution.py:396
  27.8 3.6 %collective-permute-start.3 = (bf16[320,128]{1,0:T(8,128)(2,1)S(1)}, bf16[320,128]{1,0:T(8,128)(2,1)S(1)}, u32[]{:S(2)}, u32[]{:S(2)}) collective-permute-start(bf16[320,128]{1,0:T(8,128)(2,1)S(1)} %get-tuple-element.31), channel_id=1, source_target_pairs={{0,1},{1,0},{2,3},{3,2},{4,5},{5,4},{6,7},{7,6},{8,9},{9,8},{10,11... | collective-permute-start | bytes 245768 | tf_op jit(solution)/shard_map/ppermute | solution.py:400
  27.9 8.8 %collective-permute-start.4 = (bf16[320,128]{1,0:T(8,128)(2,1)S(1)}, bf16[320,128]{1,0:T(8,128)(2,1)S(1)}, u32[]{:S(2)}, u32[]{:S(2)}) collective-permute-start(bf16[320,128]{1,0:T(8,128)(2,1)S(1)} %get-tuple-element.32), channel_id=1, source_target_pairs={{0,2},{1,3},{2,0},{3,1},{4,6},{5,7},{6,4},{7,5},{8,10},{9,11},{10,... | collective-permute-start | bytes 245768 | tf_op jit(solution)/shard_map/ppermute | solution.py:400
  29.4 8.0 %collective-permute-start.5 = (bf16[320,128]{1,0:T(8,128)(2,1)S(1)}, bf16[320,128]{1,0:T(8,128)(2,1)S(1)}, u32[]{:S(2)}, u32[]{:S(2)}) collective-permute-start(bf16[320,128]{1,0:T(8,128)(2,1)S(1)} %get-tuple-element.33), channel_id=1, source_target_pairs={{0,3},{1,2},{2,1},{3,0},{4,7},{5,6},{6,5},{7,4},{8,11},{9,10},{10,... | collective-permute-start | bytes 245768 | tf_op jit(solution)/shard_map/ppermute | solution.py:400
  29.7 7.7 %collective-permute-start.6 = (bf16[320,128]{1,0:T(8,128)(2,1)S(1)}, bf16[320,128]{1,0:T(8,128)(2,1)S(1)}, u32[]{:S(2)}, u32[]{:S(2)}) collective-permute-start(bf16[320,128]{1,0:T(8,128)(2,1)S(1)} %get-tuple-element.34), channel_id=1, source_target_pairs={{0,4},{1,5},{2,6},{3,7},{4,0},{5,1},{6,2},{7,3},{8,12},{9,13},{10,... | collective-permute-start | bytes 245768 | tf_op jit(solution)/shard_map/ppermute | solution.py:400
  31.2 7.3 %collective-permute-start.7 = (bf16[320,128]{1,0:T(8,128)(2,1)S(1)}, bf16[320,128]{1,0:T(8,128)(2,1)S(1)}, u32[]{:S(2)}, u32[]{:S(2)}) collective-permute-start(bf16[320,128]{1,0:T(8,128)(2,1)S(1)} %get-tuple-element.35), channel_id=1, source_target_pairs={{0,5},{1,4},{2,7},{3,6},{4,1},{5,0},{6,3},{7,2},{8,13},{9,12},{10,... | collective-permute-start | bytes 245768 | tf_op jit(solution)/shard_map/ppermute | solution.py:400
  31.4 10.5 %collective-permute-start.8 = (bf16[320,128]{1,0:T(8,128)(2,1)S(1)}, bf16[320,128]{1,0:T(8,128)(2,1)S(1)}, u32[]{:S(2)}, u32[]{:S(2)}) collective-permute-start(bf16[320,128]{1,0:T(8,128)(2,1)S(1)} %get-tuple-element.36), channel_id=1, source_target_pairs={{0,6},{1,7},{2,4},{3,5},{4,2},{5,3},{6,0},{7,1},{8,14},{9,15},{10,... | collective-permute-start | bytes 245768 | tf_op jit(solution)/shard_map/ppermute | solution.py:400
  36.7 6.7 %collective-permute-start.9 = (bf16[320,128]{1,0:T(8,128)(2,1)S(1)}, bf16[320,128]{1,0:T(8,128)(2,1)S(1)}, u32[]{:S(2)}, u32[]{:S(2)}) collective-permute-start(bf16[320,128]{1,0:T(8,128)(2,1)S(1)} %get-tuple-element.37), channel_id=1, source_target_pairs={{0,7},{1,6},{2,5},{3,4},{4,3},{5,2},{6,1},{7,0},{8,15},{9,14},{10,... | collective-permute-start | bytes 245768 | tf_op jit(solution)/shard_map/ppermute | solution.py:400

commit v3 on v2

--- a/solution.py
+++ b/solution.py
@@ -217,12 +217,12 @@
                     weights[pl.ds(start, 2 * GROUPS), :] = jnp.concatenate(both, 0).astype(BF16)
         return carry
 
-    lax.fori_loop(0, blocks, build, 0, unroll=8)
+    lax.fori_loop(0, blocks, build, 0, unroll=16)
     fetch_table.wait()
 
     def multiply(step, carry):
-        for inner in range(64):
-            s = step * 64 + inner
+        for inner in range(128):
+            s = step * 128 + inner
             start = pl.multiple_of(s * 2 * GROUPS, 2 * GROUPS)
             e = pl.multiple_of(table_ref[1, s], 2 * LANES)
             result[pl.ds(start, 2 * GROUPS), :] = mm(
@@ -230,7 +230,7 @@
             )
         return carry
 
-    lax.fori_loop(0, live // 64, multiply, 0)
+    lax.fori_loop(0, live // 128, multiply, 0)
     for aux in range(aux_dev):
         for group in range(GROUPS):
             swapped[aux * live : (aux + 1) * live, group * LANES : (group + 1) * LANES] = (
@@ -244,9 +244,14 @@
                      lambda n: half * BW + n)
 
 
+def far_order(outer):
+    return [0, outer - 1, *range(1, outer - 1)]
+
+
 def regroup_kernel(token_ref, *refs):
     sources, targets = refs[:-NEAR], refs[-NEAR:]
     outer = len(sources)
+    sources = [sources[far_order(outer).index(far)] for far in range(outer)]
     height = (sources[0].shape[0] - 2 * GROUPS) // NEAR
     for near, target in enumerate(targets):
         for far, source in enumerate(sources):
@@ -270,15 +275,15 @@
         wide[d * rows : (d + 1) * rows, :] = source_ref[d, :rows, :].astype(F32)
 
 
-def occ_kernel(aux_dev, table_hbm, *rest):
-    x_refs, (mo_ref, table_ref, wide, planes, weights, held, sem) = rest[:NEAR], rest[NEAR:]
+def occ_kernel(aux_dev, table_hbm, xm_ref, *rest):
+    x_refs, (out_ref, table_ref, wide, planes, weights, held, wide_m, sem) = rest[:NEAR], rest[NEAR:]
     fetch_table = pltpu.make_async_copy(table_hbm, table_ref, sem)
     fetch_table.start()
     rows = table_ref.shape[1] // PACK
     height = aux_dev * rows
     outer = x_refs[0].shape[0] // (height + 2 * GROUPS)
     devices = outer * NEAR
-    out_rows, aux, _ = mo_ref.shape
+    out_rows, aux = xm_ref.shape[1] // aux_dev, aux_dev * devices
     me = lax.axis_index("basis")
     for near, x_ref in enumerate(x_refs):
         for far in range(outer):
@@ -305,7 +310,8 @@
         weights[pl.ds(start, BW), :] = jnp.concatenate(copies, 0).astype(BF16)
         return carry
 
-    lax.fori_loop(0, 2 * devices, build, 0, unroll=8)
+    lax.fori_loop(0, 2 * devices, build, 0, unroll=32)
+    widen(xm_ref, xm_ref.shape[1], wide_m)
     for r in range(rows):
         row = by_slot(wide, aux_dev, rows, devices, r)
         for steps in range(PACK):
@@ -321,7 +327,7 @@
     bases = [first + (place + PACK - me % PACK) % PACK * out_rows for place in range(PACK)]
     fetch_table.wait()
 
-    def multiply(r, carry):
+    def multiply(r, total):
         parts, blocks = [], []
         for place in range(PACK):
             s = bases[place] + r
@@ -331,20 +337,11 @@
             a = pl.multiple_of(table_ref[0, s], 2 * BW)
             blocks.append(weights[pl.ds(a, 2 * BW), :] * of_chunk[place])
         left = jnp.concatenate([sum(parts[1:PACK], parts[0]), sum(parts[PACK + 1 :], parts[PACK])], 1)
-        mo_ref[r] = mm(left, jnp.concatenate(blocks, 0)).astype(BF16)
-        return carry
-
-    lax.fori_loop(0, out_rows, multiply, 0, unroll=8)
-
-
-def gram_kernel(aux_dev, mo_ref, xm_ref, out_ref, wide):
-    devices, rows_all, _ = xm_ref.shape
-    rows = rows_all // aux_dev
-    aux = aux_dev * devices
-    widen(xm_ref, rows_all, wide)
-    total = jnp.zeros((aux, aux), F32)
-    for r in range(rows):
-        total = total + mm_nt(mo_ref[r], by_slot(wide, aux_dev, rows, devices, r).astype(BF16))
+        m_occ = mm(left, jnp.concatenate(blocks, 0)).astype(BF16)
+        m_virt = by_slot(wide_m, aux_dev, out_rows, devices, r).astype(BF16)
+        return total + mm_nt(m_occ, m_virt)
+
+    total = lax.fori_loop(0, out_rows, multiply, jnp.zeros((aux, aux), F32), unroll=32)
     out_ref[...] = jnp.concatenate(
         [total[aux_i * devices : (aux_i + 1) * devices, :] for aux_i in range(aux_dev)], 1
     )
@@ -481,37 +478,27 @@
         (shape((outer * (height + 2 * GROUPS), LANES), BF16),) * NEAR,
         [],
         "m" + "v" * outer,
-        (token, *xt),
+        (token, *[xt[far] for far in far_order(outer)]),
         "regroup",
-        1,
+        9,
     ))
     for near in range(1, NEAR):
         xt[near] = permute(xt[near], devices, near)
-    mo = call(
+    part = call(
         functools.partial(occ_kernel, aux_dev),
-        vmem((rows_m, aux, LANES), BF16),
+        shape((devices, aux_dev * aux), F32),
         [
             pltpu.SMEM((8, live), I32),
             vmem((devices * height, LANES), F32),
             vmem((devices * 2 * GROUPS, LANES), F32),
             vmem((devices * 2 * BW, LANES), BF16),
             vmem(((PACK * rows_t + 1) * aux, LANES), BF16),
+            vmem((devices * aux_dev * rows_m, LANES), F32),
             dma,
         ],
-        "a" + "v" * NEAR,
-        (table, *xt),
+        "av" + "v" * NEAR,
+        (table, xm, *xt),
         "occ",
-        8,
-    )
-    part = call(
-        functools.partial(gram_kernel, aux_dev),
-        shape((devices, aux_dev * aux), F32),
-        [
-            vmem((devices * aux_dev * rows_m, LANES), F32),
-        ],
-        "mv",
-        (mo, xm),
-        "gram",
         1,
     )
     part = exchange(part)

time: 59.3 us -> 57.8 us (0.975)
  Pallas kernels: 14.4 us -> 12.9 us
  starting transfers between devices: 24 us -> 24.6 us
    pallas_call x7 -> x6, Pallas kernels: 14.4 us -> 12.9 us  [call(): pl.pallas_call(kernel, out_shape=outs, in_specs=[pl.BlockSpec(memory_spac...]
    ppermute x10, starting transfers between devices: 10.9 us -> 11.5 us  [permute(): return lax.ppermute(x, 'basis', [(i, i ^ step) for i in range(devices)])]
  transfers between devices with their start and end apart: 12 -> 12, of which waited for: 6 -> 4; matrix products, arithmetic and copies ran while one was open for 0% -> 0% of each run, Pallas kernels for 19% -> 14%
where the time goes in v3:
time: 57.8 us; the launch traced here: 57.4 us
  starting transfers between devices  24.6 us (43%)
  Pallas kernels  12.9 us (22%)
  blocking collectives  10.6 us (18%)
  waiting for transfers between devices  9.19 us (16%)
    all_to_all x2, starting transfers between devices, exchange(): return lax.all_to_all(x, 'basis', split_axis=0, concat_axis=0, tiled=True)  13.1 us
    pallas_call x6, Pallas kernels, call(): pl.pallas_call(kernel, out_shape=outs, in_specs=[pl.BlockSpec(memory_spac...  12.9 us
    ppermute x10, starting transfers between devices, permute(): return lax.ppermute(x, 'basis', [(i, i ^ step) for i in range(devices)])  11.5 us
    all_to_all x1, blocking collectives, exchange(): return lax.all_to_all(x, 'basis', split_axis=0, concat_axis=0, tiled=True)  10.6 us
    ppermute x10, waiting for transfers between devices, permute(): return lax.ppermute(x, 'basis', [(i, i ^ step) for i in range(devices)])  9.19 us
  transfers between devices with their start and end apart: 12, of which 4 were waited for; matrix products, arithmetic and copies ran while one was open for 0% of the time, Pallas kernels for 14%

profile of v3, /device:TPU:0, one launch (start us, length us, event | category | flops | bytes accessed | tf_op | source)
XLA Modules:
  0.0 57.4 jit_solution(1149637564111271563)
XLA Ops:
  0.0 1.4 %format.1 = bf16[32,16,128]{2,1,0:T(8,128)(2,1)} custom-call(bf16[2,1024]{1,0:T(2,128)(2,1)} %bitcast.13), custom_call_target="tpu_custom_call" | custom-call | flops 1000000000 | bytes 3000000 | tf_op jit(solution)/shard_map/format/pallas_call | solution.py:376
  1.4 7.3 %all-to-all-start = ((bf16[32,16,128]{2,1,0:T(8,128)(2,1)}), bf16[32,16,128]{2,1,0:T(8,128)(2,1)S(1)}, u32[]{:S(2)}, u32[]{:S(2)}) async-start(bf16[32,16,128]{2,1,0:T(8,128)(2,1)} %format.1), calls=%async_computation | async-start | bytes 262144 | tf_op jit(solution)/shard_map/all_to_all | solution.py:393
  8.7 4.1 %prepare.1 = (bf16[528,128]{1,0:T(8,128)(2,1)S(1)}, bf16[528,128]{1,0:T(8,128)(2,1)S(1)}, bf16[528,128]{1,0:T(8,128)(2,1)S(1)}, bf16[528,128]{1,0:T(8,128)(2,1)S...) custom-call(s32[1,32]{1,0:T(1,128)} %bitcast.17, s32[8,32]{1,0:T(8,128)} %bitcast.14, ...), custom_call_target="tpu_custom_call" | custom-call | flops 5000000000 | bytes 15000000 | tf_op jit(solution)/shard_map/prepare/pallas_call | solution.py:376
  12.7 3.7 %collective-permute-start = (bf16[528,128]{1,0:T(8,128)(2,1)S(1)}, bf16[528,128]{1,0:T(8,128)(2,1)S(1)}, u32[]{:S(2)}, u32[]{:S(2)}) collective-permute-start(bf16[528,128]{1,0:T(8,128)(2,1)S(1)} %get-tuple-element.28), channel_id=1, source_target_pairs={{0,24},{1,25},{2,26},{3,27},{4,28},{5,29},{6,30},{7,31},{8,16},{9,... | collective-permute-start | bytes 405512 | tf_op jit(solution)/shard_map/ppermute | solution.py:397
  16.4 0.0 collective-permute-start.1
  16.4 0.8 %collective-permute-start.2 = (bf16[528,128]{1,0:T(8,128)(2,1)S(1)}, bf16[528,128]{1,0:T(8,128)(2,1)S(1)}, u32[]{:S(2)}, u32[]{:S(2)}) collective-permute-start(bf16[528,128]{1,0:T(8,128)(2,1)S(1)} %get-tuple-element.30), channel_id=1, source_target_pairs={{0,16},{1,17},{2,18},{3,19},{4,20},{5,21},{6,22},{7,23},{8,24},{9,... | collective-permute-start | bytes 405512 | tf_op jit(solution)/shard_map/ppermute | solution.py:397
  17.2 0.0 all-to-all-done.dens_ref
  17.2 3.9 %virt.1 = (bf16[32,64,128]{2,1,0:T(8,128)(2,1)}, f32[8,128]{1,0:T(8,128)S(1)}) custom-call(s32[8,128]{1,0:T(8,128)S(1)} %get-tuple-element.22.table_hbm, bf16[32,16,128]{2,1,0:T(8,128)(2,1)S(1)} %all-to-all-done.dens_ref, bf16[2048,256]{1,0:T(8,128)(2,1)S(1)} %get-tuple-element.23.a_ref, bf16[1024,1024]{1,0:T(8,128)(2,1)} %get-tuple-element.24.perm_hbm), custom_call_target="tpu_custom_call" | custom-call | flops 99999997952 | bytes 300000000 | tf_op jit(solution)/shard_map/virt/pallas_call | solution.py:376
  21.1 5.8 %all-to-all-start.1 = ((bf16[32,64,128]{2,1,0:T(8,128)(2,1)}), bf16[32,64,128]{2,1,0:T(8,128)(2,1)S(1)}, u32[]{:S(2)}, u32[]{:S(2)}) async-start(bf16[32,64,128]{2,1,0:T(8,128)(2,1)} %get-tuple-element.25), calls=%async_computation.1 | async-start | bytes 1048576 | tf_op jit(solution)/shard_map/all_to_all | solution.py:393
  27.0 0.0 collective-permute-done.refs_1_
  27.0 0.0 collective-permute-done.1.refs_2_
  27.0 1.4 %collective-permute-done.2.refs_3_ = bf16[528,128]{1,0:T(8,128)(2,1)S(1)} collective-permute-done((bf16[528,128]{1,0:T(8,128)(2,1)S(1)}, bf16[528,128]{1,0:T(8,128)(2,1)S(1)}, u32[]{:S(2)}, u32[]{:S(2)}) %collective-permute-start.2) | collective-permute-done | bytes 135200 | tf_op jit(solution)/shard_map/ppermute | solution.py:397
  28.3 0.1 regroup.1
  28.4 0.1 collective-permute-start.3
  28.5 1.5 %collective-permute-start.4 = (bf16[320,128]{1,0:T(8,128)(2,1)S(1)}, bf16[320,128]{1,0:T(8,128)(2,1)S(1)}, u32[]{:S(2)}, u32[]{:S(2)}) collective-permute-start(bf16[320,128]{1,0:T(8,128)(2,1)S(1)} %get-tuple-element.33), channel_id=1, source_target_pairs={{0,2},{1,3},{2,0},{3,1},{4,6},{5,7},{6,4},{7,5},{8,10},{9,11},{10,... | collective-permute-start | bytes 245768 | tf_op jit(solution)/shard_map/ppermute | solution.py:397
  30.0 0.3 collective-permute-start.5
  30.3 1.5 %collective-permute-start.6 = (bf16[320,128]{1,0:T(8,128)(2,1)S(1)}, bf16[320,128]{1,0:T(8,128)(2,1)S(1)}, u32[]{:S(2)}, u32[]{:S(2)}) collective-permute-start(bf16[320,128]{1,0:T(8,128)(2,1)S(1)} %get-tuple-element.35), channel_id=1, source_target_pairs={{0,4},{1,5},{2,6},{3,7},{4,0},{5,1},{6,2},{7,3},{8,12},{9,13},{10,... | collective-permute-start | bytes 245768 | tf_op jit(solution)/shard_map/ppermute | solution.py:397
  31.8 0.2 collective-permute-start.7
  32.0 0.0 collective-permute-done.3.rest_1_
  32.0 2.4 %collective-permute-start.8 = (bf16[320,128]{1,0:T(8,128)(2,1)S(1)}, bf16[320,128]{1,0:T(8,128)(2,1)S(1)}, u32[]{:S(2)}, u32[]{:S(2)}) collective-permute-start(bf16[320,128]{1,0:T(8,128)(2,1)S(1)} %get-tuple-element.37), channel_id=1, source_target_pairs={{0,6},{1,7},{2,4},{3,5},{4,2},{5,3},{6,0},{7,1},{8,14},{9,15},{10,... | collective-permute-start | bytes 245768 | tf_op jit(solution)/shard_map/ppermute | solution.py:397
  34.4 1.8 %collective-permute-done.4.rest_2_ = bf16[320,128]{1,0:T(8,128)(2,1)S(1)} collective-permute-done((bf16[320,128]{1,0:T(8,128)(2,1)S(1)}, bf16[320,128]{1,0:T(8,128)(2,1)S(1)}, u32[]{:S(2)}, u32[]{:S(2)}) %collective-permute-start.4) | collective-permute-done | bytes 81952 | tf_op jit(solution)/shard_map/ppermute | solution.py:397
  36.2 1.0 %collective-permute-start.9 = (bf16[320,128]{1,0:T(8,128)(2,1)S(1)}, bf16[320,128]{1,0:T(8,128)(2,1)S(1)}, u32[]{:S(2)}, u32[]{:S(2)}) collective-permute-start(bf16[320,128]{1,0:T(8,128)(2,1)S(1)} %get-tuple-element.38), channel_id=1, source_target_pairs={{0,7},{1,6},{2,5},{3,4},{4,3},{5,2},{6,1},{7,0},{8,15},{9,14},{10,... | collective-permute-start | bytes 245768 | tf_op jit(solution)/shard_map/ppermute | solution.py:397
  37.2 0.0 collective-permute-done.5.rest_3_
  37.2 0.0 collective-permute-done.6.rest_4_
  37.2 5.0 %collective-permute-done.7.rest_5_ = bf16[320,128]{1,0:T(8,128)(2,1)S(1)} collective-permute-done((bf16[320,128]{1,0:T(8,128)(2,1)S(1)}, bf16[320,128]{1,0:T(8,128)(2,1)S(1)}, u32[]{:S(2)}, u32[]{:S(2)}) %collective-permute-start.7) | collective-permute-done | bytes 81952 | tf_op jit(solution)/shard_map/ppermute | solution.py:397
  42.2 0.0 collective-permute-done.8.rest_6_
  42.2 1.0 %collective-permute-done.9.rest_7_ = bf16[320,128]{1,0:T(8,128)(2,1)S(1)} collective-permute-done((bf16[320,128]{1,0:T(8,128)(2,1)S(1)}, bf16[320,128]{1,0:T(8,128)(2,1)S(1)}, u32[]{:S(2)}, u32[]{:S(2)}) %collective-permute-start.9) | collective-permute-done | bytes 81952 | tf_op jit(solution)/shard_map/ppermute | solution.py:397
  43.2 0.0 all-to-all-done.1.xm_ref
  43.2 2.7 %occ.1 = f32[32,128]{1,0:T(8,128)S(1)} custom-call(s32[8,128]{1,0:T(8,128)S(1)} %get-tuple-element.22.table_hbm, bf16[32,64,128]{2,1,0:T(8,128)(2,1)S(1)} %all-to-all-done.1.xm_ref, bf16[320,128]{1,0:T(8,128)(2,1)S(1)} %get-tuple-element.31.rest_0_, bf16[320,128]{1,0:T(8,128)(2,1)S(1)} %collective-permute-done.3.rest_1_, ...), custom_call_target="tpu_custom_call" | custom-call | flops 1000000000 | bytes 3000000 | tf_op jit(solution)/shard_map/occ/pallas_call | solution.py:376
  46.0 10.6 %all_to_all.21 = f32[32,1,128]{2,1,0:T(1,128)S(1)} all-to-all(f32[32,1,128]{2,1,0:T(1,128)S(1)} %bitcast.10), channel_id=1, replica_groups=mesh['parts'=1,'basis'=32] {'basis'}, dimensions={0} | all-to-all | bytes 32768 | tf_op jit(solution)/shard_map/all_to_all | solution.py:393
  56.6 0.8 %total.1 = f32[2,64]{1,0:T(2,128)} custom-call(f32[32,128]{1,0:T(8,128)S(1)} %bitcast.11), custom_call_target="tpu_custom_call" | custom-call | flops 1000000000 | bytes 3000000 | tf_op jit(solution)/shard_map/total/pallas_call | solution.py:376
Async XLA Ops:
  1.4 15.8 %all-to-all-start = ((bf16[32,16,128]{2,1,0:T(8,128)(2,1)}), bf16[32,16,128]{2,1,0:T(8,128)(2,1)S(1)}, u32[]{:S(2)}, u32[]{:S(2)}) async-start(bf16[32,16,128]{2,1,0:T(8,128)(2,1)} %format.1), calls=%async_computation | async-start | bytes 262144 | tf_op jit(solution)/shard_map/all_to_all | solution.py:393
  12.7 14.2 %collective-permute-start = (bf16[528,128]{1,0:T(8,128)(2,1)S(1)}, bf16[528,128]{1,0:T(8,128)(2,1)S(1)}, u32[]{:S(2)}, u32[]{:S(2)}) collective-permute-start(bf16[528,128]{1,0:T(8,128)(2,1)S(1)} %get-tuple-element.28), channel_id=1, source_target_pairs={{0,24},{1,25},{2,26},{3,27},{4,28},{5,29},{6,30},{7,31},{8,16},{9,... | collective-permute-start | bytes 405512 | tf_op jit(solution)/shard_map/ppermute | solution.py:397
  16.4 10.5 %collective-permute-start.1 = (bf16[528,128]{1,0:T(8,128)(2,1)S(1)}, bf16[528,128]{1,0:T(8,128)(2,1)S(1)}, u32[]{:S(2)}, u32[]{:S(2)}) collective-permute-start(bf16[528,128]{1,0:T(8,128)(2,1)S(1)} %get-tuple-element.29), channel_id=1, source_target_pairs={{0,8},{1,9},{2,10},{3,11},{4,12},{5,13},{6,14},{7,15},{8,0},{9,1},... | collective-permute-start | bytes 405512 | tf_op jit(solution)/shard_map/ppermute | solution.py:397
  16.4 11.9 %collective-permute-start.2 = (bf16[528,128]{1,0:T(8,128)(2,1)S(1)}, bf16[528,128]{1,0:T(8,128)(2,1)S(1)}, u32[]{:S(2)}, u32[]{:S(2)}) collective-permute-start(bf16[528,128]{1,0:T(8,128)(2,1)S(1)} %get-tuple-element.30), channel_id=1, source_target_pairs={{0,16},{1,17},{2,18},{3,19},{4,20},{5,21},{6,22},{7,23},{8,24},{9,... | collective-permute-start | bytes 405512 | tf_op jit(solution)/shard_map/ppermute | solution.py:397
  21.1 22.1 %all-to-all-start.1 = ((bf16[32,64,128]{2,1,0:T(8,128)(2,1)}), bf16[32,64,128]{2,1,0:T(8,128)(2,1)S(1)}, u32[]{:S(2)}, u32[]{:S(2)}) async-start(bf16[32,64,128]{2,1,0:T(8,128)(2,1)} %get-tuple-element.25), calls=%async_computation.1 | async-start | bytes 1048576 | tf_op jit(solution)/shard_map/all_to_all | solution.py:393
  28.4 3.6 %collective-permute-start.3 = (bf16[320,128]{1,0:T(8,128)(2,1)S(1)}, bf16[320,128]{1,0:T(8,128)(2,1)S(1)}, u32[]{:S(2)}, u32[]{:S(2)}) collective-permute-start(bf16[320,128]{1,0:T(8,128)(2,1)S(1)} %get-tuple-element.32), channel_id=1, source_target_pairs={{0,1},{1,0},{2,3},{3,2},{4,5},{5,4},{6,7},{7,6},{8,9},{9,8},{10,11... | collective-permute-start | bytes 245768 | tf_op jit(solution)/shard_map/ppermute | solution.py:397
  28.5 7.7 %collective-permute-start.4 = (bf16[320,128]{1,0:T(8,128)(2,1)S(1)}, bf16[320,128]{1,0:T(8,128)(2,1)S(1)}, u32[]{:S(2)}, u32[]{:S(2)}) collective-permute-start(bf16[320,128]{1,0:T(8,128)(2,1)S(1)} %get-tuple-element.33), channel_id=1, source_target_pairs={{0,2},{1,3},{2,0},{3,1},{4,6},{5,7},{6,4},{7,5},{8,10},{9,11},{10,... | collective-permute-start | bytes 245768 | tf_op jit(solution)/shard_map/ppermute | solution.py:397
  30.0 7.2 %collective-permute-start.5 = (bf16[320,128]{1,0:T(8,128)(2,1)S(1)}, bf16[320,128]{1,0:T(8,128)(2,1)S(1)}, u32[]{:S(2)}, u32[]{:S(2)}) collective-permute-start(bf16[320,128]{1,0:T(8,128)(2,1)S(1)} %get-tuple-element.34), channel_id=1, source_target_pairs={{0,3},{1,2},{2,1},{3,0},{4,7},{5,6},{6,5},{7,4},{8,11},{9,10},{10,... | collective-permute-start | bytes 245768 | tf_op jit(solution)/shard_map/ppermute | solution.py:397
  30.3 6.9 %collective-permute-start.6 = (bf16[320,128]{1,0:T(8,128)(2,1)S(1)}, bf16[320,128]{1,0:T(8,128)(2,1)S(1)}, u32[]{:S(2)}, u32[]{:S(2)}) collective-permute-start(bf16[320,128]{1,0:T(8,128)(2,1)S(1)} %get-tuple-element.35), channel_id=1, source_target_pairs={{0,4},{1,5},{2,6},{3,7},{4,0},{5,1},{6,2},{7,3},{8,12},{9,13},{10,... | collective-permute-start | bytes 245768 | tf_op jit(solution)/shard_map/ppermute | solution.py:397
  31.8 10.4 %collective-permute-start.7 = (bf16[320,128]{1,0:T(8,128)(2,1)S(1)}, bf16[320,128]{1,0:T(8,128)(2,1)S(1)}, u32[]{:S(2)}, u32[]{:S(2)}) collective-permute-start(bf16[320,128]{1,0:T(8,128)(2,1)S(1)} %get-tuple-element.36), channel_id=1, source_target_pairs={{0,5},{1,4},{2,7},{3,6},{4,1},{5,0},{6,3},{7,2},{8,13},{9,12},{10,... | collective-permute-start | bytes 245768 | tf_op jit(solution)/shard_map/ppermute | solution.py:397
  32.0 10.2 %collective-permute-start.8 = (bf16[320,128]{1,0:T(8,128)(2,1)S(1)}, bf16[320,128]{1,0:T(8,128)(2,1)S(1)}, u32[]{:S(2)}, u32[]{:S(2)}) collective-permute-start(bf16[320,128]{1,0:T(8,128)(2,1)S(1)} %get-tuple-element.37), channel_id=1, source_target_pairs={{0,6},{1,7},{2,4},{3,5},{4,2},{5,3},{6,0},{7,1},{8,14},{9,15},{10,... | collective-permute-start | bytes 245768 | tf_op jit(solution)/shard_map/ppermute | solution.py:397
  36.2 7.0 %collective-permute-start.9 = (bf16[320,128]{1,0:T(8,128)(2,1)S(1)}, bf16[320,128]{1,0:T(8,128)(2,1)S(1)}, u32[]{:S(2)}, u32[]{:S(2)}) collective-permute-start(bf16[320,128]{1,0:T(8,128)(2,1)S(1)} %get-tuple-element.38), channel_id=1, source_target_pairs={{0,7},{1,6},{2,5},{3,4},{4,3},{5,2},{6,1},{7,0},{8,15},{9,14},{10,... | collective-permute-start | bytes 245768 | tf_op jit(solution)/shard_map/ppermute | solution.py:397

commit v4 on v3

--- a/solution.py
+++ b/solution.py
@@ -275,15 +275,23 @@
         wide[d * rows : (d + 1) * rows, :] = source_ref[d, :rows, :].astype(F32)
 
 
-def occ_kernel(aux_dev, table_hbm, xm_ref, *rest):
-    x_refs, (out_ref, table_ref, wide, planes, weights, held, wide_m, sem) = rest[:NEAR], rest[NEAR:]
+def rows_kernel(aux_dev, xm_ref, out_ref, wide):
+    devices, height, _ = xm_ref.shape
+    rows = height // aux_dev
+    widen(xm_ref, height, wide)
+    for r in range(rows):
+        out_ref[r] = by_slot(wide, aux_dev, rows, devices, r).astype(BF16)
+
+
+def occ_kernel(aux_dev, table_hbm, mv_ref, *rest):
+    x_refs, (out_ref, table_ref, wide, planes, weights, held, sem) = rest[:NEAR], rest[NEAR:]
     fetch_table = pltpu.make_async_copy(table_hbm, table_ref, sem)
     fetch_table.start()
     rows = table_ref.shape[1] // PACK
     height = aux_dev * rows
     outer = x_refs[0].shape[0] // (height + 2 * GROUPS)
     devices = outer * NEAR
-    out_rows, aux = xm_ref.shape[1] // aux_dev, aux_dev * devices
+    out_rows, aux = mv_ref.shape[0], mv_ref.shape[1]
     me = lax.axis_index("basis")
     for near, x_ref in enumerate(x_refs):
         for far in range(outer):
@@ -311,7 +319,6 @@
         return carry
 
     lax.fori_loop(0, 2 * devices, build, 0, unroll=32)
-    widen(xm_ref, xm_ref.shape[1], wide_m)
     for r in range(rows):
         row = by_slot(wide, aux_dev, rows, devices, r)
         for steps in range(PACK):
@@ -338,8 +345,7 @@
             blocks.append(weights[pl.ds(a, 2 * BW), :] * of_chunk[place])
         left = jnp.concatenate([sum(parts[1:PACK], parts[0]), sum(parts[PACK + 1 :], parts[PACK])], 1)
         m_occ = mm(left, jnp.concatenate(blocks, 0)).astype(BF16)
-        m_virt = by_slot(wide_m, aux_dev, out_rows, devices, r).astype(BF16)
-        return total + mm_nt(m_occ, m_virt)
+        return total + mm_nt(m_occ, mv_ref[r])
 
     total = lax.fori_loop(0, out_rows, multiply, jnp.zeros((aux, aux), F32), unroll=32)
     out_ref[...] = jnp.concatenate(
@@ -484,6 +490,15 @@
     ))
     for near in range(1, NEAR):
         xt[near] = permute(xt[near], devices, near)
+    mv = call(
+        functools.partial(rows_kernel, aux_dev),
+        vmem((rows_m, aux, LANES), BF16),
+        [vmem((devices * aux_dev * rows_m, LANES), F32)],
+        "v",
+        (xm,),
+        "rows",
+        1,
+    )
     part = call(
         functools.partial(occ_kernel, aux_dev),
         shape((devices, aux_dev * aux), F32),
@@ -493,11 +508,10 @@
             vmem((devices * 2 * GROUPS, LANES), F32),
             vmem((devices * 2 * BW, LANES), BF16),
             vmem(((PACK * rows_t + 1) * aux, LANES), BF16),
-            vmem((devices * aux_dev * rows_m, LANES), F32),
             dma,
         ],
-        "av" + "v" * NEAR,
-        (table, xm, *xt),
+        "am" + "v" * NEAR,
+        (table, mv, *xt),
         "occ",
         1,
     )

time: 57.8 us -> 57.4 us (level)
  waiting for transfers between devices: 9.19 us -> 8.51 us
    ppermute x10, waiting for transfers between devices: 9.19 us -> 3.23 us  [permute(): return lax.ppermute(x, 'basis', [(i, i ^ step) for i in range(devices)])]
    all_to_all x2, waiting for transfers between devices: 0.01 us -> 5.28 us  [exchange(): return lax.all_to_all(x, 'basis', split_axis=0, concat_axis=0, tiled=True)]
    pallas_call x6 -> x7, Pallas kernels: 12.9 us -> 13.2 us  [call(): pl.pallas_call(kernel, out_shape=outs, in_specs=[pl.BlockSpec(memory_spac...]
  transfers between devices with their start and end apart: 12 -> 12, of which waited for: 4 -> 3; matrix products, arithmetic and copies ran while one was open for 0% -> 0% of each run, Pallas kernels for 14% -> 15%
where the time goes in v4:
time: 57.4 us; the launch traced here: 57 us
  starting transfers between devices  24.6 us (43%)
  Pallas kernels  13.2 us (23%)
  blocking collectives  10.6 us (18%)
  waiting for transfers between devices  8.51 us (15%)
    pallas_call x7, Pallas kernels, call(): pl.pallas_call(kernel, out_shape=outs, in_specs=[pl.BlockSpec(memory_spac...  13.2 us
    all_to_all x2, starting transfers between devices, exchange(): return lax.all_to_all(x, 'basis', split_axis=0, concat_axis=0, tiled=True)  13.1 us
    ppermute x10, starting transfers between devices, permute(): return lax.ppermute(x, 'basis', [(i, i ^ step) for i in range(devices)])  11.5 us
    all_to_all x1, blocking collectives, exchange(): return lax.all_to_all(x, 'basis', split_axis=0, concat_axis=0, tiled=True)  10.6 us
    all_to_all x2, waiting for transfers between devices, exchange(): return lax.all_to_all(x, 'basis', split_axis=0, concat_axis=0, tiled=True)  5.28 us
    ppermute x10, waiting for transfers between devices, permute(): return lax.ppermute(x, 'basis', [(i, i ^ step) for i in range(devices)])  3.23 us
  transfers between devices with their start and end apart: 12, of which 3 were waited for; matrix products, arithmetic and copies ran while one was open for 0% of the time, Pallas kernels for 15%

profile of v4, /device:TPU:0, one launch (start us, length us, event | category | flops | bytes accessed | tf_op | source)
XLA Modules:
  0.0 57.0 jit_solution(9919597098382595637)
XLA Ops:
  0.0 1.4 %format.1 = bf16[32,16,128]{2,1,0:T(8,128)(2,1)} custom-call(bf16[2,1024]{1,0:T(2,128)(2,1)} %bitcast.13), custom_call_target="tpu_custom_call" | custom-call | flops 1000000000 | bytes 3000000 | tf_op jit(solution)/shard_map/format/pallas_call | solution.py:382
  1.4 7.3 %all-to-all-start = ((bf16[32,16,128]{2,1,0:T(8,128)(2,1)}), bf16[32,16,128]{2,1,0:T(8,128)(2,1)S(1)}, u32[]{:S(2)}, u32[]{:S(2)}) async-start(bf16[32,16,128]{2,1,0:T(8,128)(2,1)} %format.1), calls=%async_computation | async-start | bytes 262144 | tf_op jit(solution)/shard_map/all_to_all | solution.py:399
  8.7 4.1 %prepare.1 = (bf16[528,128]{1,0:T(8,128)(2,1)S(1)}, bf16[528,128]{1,0:T(8,128)(2,1)S(1)}, bf16[528,128]{1,0:T(8,128)(2,1)S(1)}, bf16[528,128]{1,0:T(8,128)(2,1)S...) custom-call(s32[1,32]{1,0:T(1,128)} %bitcast.17, s32[8,32]{1,0:T(8,128)} %bitcast.14, ...), custom_call_target="tpu_custom_call" | custom-call | flops 5000000000 | bytes 15000000 | tf_op jit(solution)/shard_map/prepare/pallas_call | solution.py:382
  12.7 3.7 %collective-permute-start = (bf16[528,128]{1,0:T(8,128)(2,1)S(1)}, bf16[528,128]{1,0:T(8,128)(2,1)S(1)}, u32[]{:S(2)}, u32[]{:S(2)}) collective-permute-start(bf16[528,128]{1,0:T(8,128)(2,1)S(1)} %get-tuple-element.28), channel_id=1, source_target_pairs={{0,24},{1,25},{2,26},{3,27},{4,28},{5,29},{6,30},{7,31},{8,16},{9,... | collective-permute-start | bytes 405512 | tf_op jit(solution)/shard_map/ppermute | solution.py:403
  16.4 0.0 collective-permute-start.1
  16.4 0.8 %collective-permute-start.2 = (bf16[528,128]{1,0:T(8,128)(2,1)S(1)}, bf16[528,128]{1,0:T(8,128)(2,1)S(1)}, u32[]{:S(2)}, u32[]{:S(2)}) collective-permute-start(bf16[528,128]{1,0:T(8,128)(2,1)S(1)} %get-tuple-element.30), channel_id=1, source_target_pairs={{0,16},{1,17},{2,18},{3,19},{4,20},{5,21},{6,22},{7,23},{8,24},{9,... | collective-permute-start | bytes 405512 | tf_op jit(solution)/shard_map/ppermute | solution.py:403
  17.2 0.0 all-to-all-done.dens_ref
  17.2 3.9 %virt.1 = (bf16[32,64,128]{2,1,0:T(8,128)(2,1)}, f32[8,128]{1,0:T(8,128)S(1)}) custom-call(s32[8,128]{1,0:T(8,128)S(1)} %get-tuple-element.22.table_hbm, bf16[32,16,128]{2,1,0:T(8,128)(2,1)S(1)} %all-to-all-done.dens_ref, bf16[2048,256]{1,0:T(8,128)(2,1)S(1)} %get-tuple-element.23.a_ref, bf16[1024,1024]{1,0:T(8,128)(2,1)} %get-tuple-element.24.perm_hbm), custom_call_target="tpu_custom_call" | custom-call | flops 99999997952 | bytes 300000000 | tf_op jit(solution)/shard_map/virt/pallas_call | solution.py:382
  21.1 5.8 %all-to-all-start.1 = ((bf16[32,64,128]{2,1,0:T(8,128)(2,1)}), bf16[32,64,128]{2,1,0:T(8,128)(2,1)S(1)}, u32[]{:S(2)}, u32[]{:S(2)}) async-start(bf16[32,64,128]{2,1,0:T(8,128)(2,1)} %get-tuple-element.25), calls=%async_computation.1 | async-start | bytes 1048576 | tf_op jit(solution)/shard_map/all_to_all | solution.py:399
  27.0 0.0 collective-permute-done.refs_1_
  27.0 0.0 collective-permute-done.1.refs_2_
  27.0 1.4 %collective-permute-done.2.refs_3_ = bf16[528,128]{1,0:T(8,128)(2,1)S(1)} collective-permute-done((bf16[528,128]{1,0:T(8,128)(2,1)S(1)}, bf16[528,128]{1,0:T(8,128)(2,1)S(1)}, u32[]{:S(2)}, u32[]{:S(2)}) %collective-permute-start.2) | collective-permute-done | bytes 135200 | tf_op jit(solution)/shard_map/ppermute | solution.py:403
  28.3 0.1 regroup.1
  28.4 0.1 collective-permute-start.3
  28.5 1.5 %collective-permute-start.4 = (bf16[320,128]{1,0:T(8,128)(2,1)S(1)}, bf16[320,128]{1,0:T(8,128)(2,1)S(1)}, u32[]{:S(2)}, u32[]{:S(2)}) collective-permute-start(bf16[320,128]{1,0:T(8,128)(2,1)S(1)} %get-tuple-element.33), channel_id=1, source_target_pairs={{0,2},{1,3},{2,0},{3,1},{4,6},{5,7},{6,4},{7,5},{8,10},{9,11},{10,... | collective-permute-start | bytes 245768 | tf_op jit(solution)/shard_map/ppermute | solution.py:403
  30.0 0.3 collective-permute-start.5
  30.3 1.5 %collective-permute-start.6 = (bf16[320,128]{1,0:T(8,128)(2,1)S(1)}, bf16[320,128]{1,0:T(8,128)(2,1)S(1)}, u32[]{:S(2)}, u32[]{:S(2)}) collective-permute-start(bf16[320,128]{1,0:T(8,128)(2,1)S(1)} %get-tuple-element.35), channel_id=1, source_target_pairs={{0,4},{1,5},{2,6},{3,7},{4,0},{5,1},{6,2},{7,3},{8,12},{9,13},{10,... | collective-permute-start | bytes 245768 | tf_op jit(solution)/shard_map/ppermute | solution.py:403
  31.8 0.2 collective-permute-start.7
  32.0 0.0 collective-permute-done.3.rest_1_
  32.0 2.4 %collective-permute-start.8 = (bf16[320,128]{1,0:T(8,128)(2,1)S(1)}, bf16[320,128]{1,0:T(8,128)(2,1)S(1)}, u32[]{:S(2)}, u32[]{:S(2)}) collective-permute-start(bf16[320,128]{1,0:T(8,128)(2,1)S(1)} %get-tuple-element.37), channel_id=1, source_target_pairs={{0,6},{1,7},{2,4},{3,5},{4,2},{5,3},{6,0},{7,1},{8,14},{9,15},{10,... | collective-permute-start | bytes 245768 | tf_op jit(solution)/shard_map/ppermute | solution.py:403
  34.4 1.8 %collective-permute-done.4.rest_2_ = bf16[320,128]{1,0:T(8,128)(2,1)S(1)} collective-permute-done((bf16[320,128]{1,0:T(8,128)(2,1)S(1)}, bf16[320,128]{1,0:T(8,128)(2,1)S(1)}, u32[]{:S(2)}, u32[]{:S(2)}) %collective-permute-start.4) | collective-permute-done | bytes 81952 | tf_op jit(solution)/shard_map/ppermute | solution.py:403
  36.2 1.0 %collective-permute-start.9 = (bf16[320,128]{1,0:T(8,128)(2,1)S(1)}, bf16[320,128]{1,0:T(8,128)(2,1)S(1)}, u32[]{:S(2)}, u32[]{:S(2)}) collective-permute-start(bf16[320,128]{1,0:T(8,128)(2,1)S(1)} %get-tuple-element.38), channel_id=1, source_target_pairs={{0,7},{1,6},{2,5},{3,4},{4,3},{5,2},{6,1},{7,0},{8,15},{9,14},{10,... | collective-permute-start | bytes 245768 | tf_op jit(solution)/shard_map/ppermute | solution.py:403
  37.2 5.3 %all-to-all-done.1.xm_ref = bf16[32,64,128]{2,1,0:T(8,128)(2,1)S(1)} async-done(((bf16[32,64,128]{2,1,0:T(8,128)(2,1)}), bf16[32,64,128]{2,1,0:T(8,128)(2,1)S(1)}, u32[]{:S(2)}, u32[]{:S(2)}) %all-to-all-start.1) | async-done | bytes 524320 | tf_op jit(solution)/shard_map/all_to_all | solution.py:399
  42.5 0.6 %rows.1.mv_ref = bf16[32,64,128]{2,1,0:T(8,128)(2,1)S(1)} custom-call(bf16[32,64,128]{2,1,0:T(8,128)(2,1)S(1)} %all-to-all-done.1.xm_ref), custom_call_target="tpu_custom_call" | custom-call | flops 1000000000 | bytes 3000000 | tf_op jit(solution)/shard_map/rows/pallas_call | solution.py:382
  43.2 0.0 collective-permute-done.5.rest_3_
  43.2 0.0 collective-permute-done.6.rest_4_
  43.2 0.0 collective-permute-done.7.rest_5_
  43.2 0.0 collective-permute-done.8.rest_6_
  43.2 0.0 collective-permute-done.9.rest_7_
  43.2 2.3 %occ.1 = f32[32,128]{1,0:T(8,128)S(1)} custom-call(s32[8,128]{1,0:T(8,128)S(1)} %get-tuple-element.22.table_hbm, bf16[32,64,128]{2,1,0:T(8,128)(2,1)S(1)} %rows.1.mv_ref, bf16[320,128]{1,0:T(8,128)(2,1)S(1)} %get-tuple-element.31.rest_0_, bf16[320,128]{1,0:T(8,128)(2,1)S(1)} %collective-permute-done.3.rest_1_, ...), custom_call_target="tpu_custom_call" | custom-call | flops 1000000000 | bytes 3000000 | tf_op jit(solution)/shard_map/occ/pallas_call | solution.py:382
  45.6 10.6 %all_to_all.21 = f32[32,1,128]{2,1,0:T(1,128)S(1)} all-to-all(f32[32,1,128]{2,1,0:T(1,128)S(1)} %bitcast.10), channel_id=1, replica_groups=mesh['parts'=1,'basis'=32] {'basis'}, dimensions={0} | all-to-all | bytes 32768 | tf_op jit(solution)/shard_map/all_to_all | solution.py:399
  56.2 0.8 %total.1 = f32[2,64]{1,0:T(2,128)} custom-call(f32[32,128]{1,0:T(8,128)S(1)} %bitcast.11), custom_call_target="tpu_custom_call" | custom-call | flops 1000000000 | bytes 3000000 | tf_op jit(solution)/shard_map/total/pallas_call | solution.py:382
Async XLA Ops:
  1.4 15.8 %all-to-all-start = ((bf16[32,16,128]{2,1,0:T(8,128)(2,1)}), bf16[32,16,128]{2,1,0:T(8,128)(2,1)S(1)}, u32[]{:S(2)}, u32[]{:S(2)}) async-start(bf16[32,16,128]{2,1,0:T(8,128)(2,1)} %format.1), calls=%async_computation | async-start | bytes 262144 | tf_op jit(solution)/shard_map/all_to_all | solution.py:399
  12.7 14.2 %collective-permute-start = (bf16[528,128]{1,0:T(8,128)(2,1)S(1)}, bf16[528,128]{1,0:T(8,128)(2,1)S(1)}, u32[]{:S(2)}, u32[]{:S(2)}) collective-permute-start(bf16[528,128]{1,0:T(8,128)(2,1)S(1)} %get-tuple-element.28), channel_id=1, source_target_pairs={{0,24},{1,25},{2,26},{3,27},{4,28},{5,29},{6,30},{7,31},{8,16},{9,... | collective-permute-start | bytes 405512 | tf_op jit(solution)/shard_map/ppermute | solution.py:403
  16.4 10.5 %collective-permute-start.1 = (bf16[528,128]{1,0:T(8,128)(2,1)S(1)}, bf16[528,128]{1,0:T(8,128)(2,1)S(1)}, u32[]{:S(2)}, u32[]{:S(2)}) collective-permute-start(bf16[528,128]{1,0:T(8,128)(2,1)S(1)} %get-tuple-element.29), channel_id=1, source_target_pairs={{0,8},{1,9},{2,10},{3,11},{4,12},{5,13},{6,14},{7,15},{8,0},{9,1},... | collective-permute-start | bytes 405512 | tf_op jit(solution)/shard_map/ppermute | solution.py:403
  16.4 11.9 %collective-permute-start.2 = (bf16[528,128]{1,0:T(8,128)(2,1)S(1)}, bf16[528,128]{1,0:T(8,128)(2,1)S(1)}, u32[]{:S(2)}, u32[]{:S(2)}) collective-permute-start(bf16[528,128]{1,0:T(8,128)(2,1)S(1)} %get-tuple-element.30), channel_id=1, source_target_pairs={{0,16},{1,17},{2,18},{3,19},{4,20},{5,21},{6,22},{7,23},{8,24},{9,... | collective-permute-start | bytes 405512 | tf_op jit(solution)/shard_map/ppermute | solution.py:403
  21.1 21.4 %all-to-all-start.1 = ((bf16[32,64,128]{2,1,0:T(8,128)(2,1)}), bf16[32,64,128]{2,1,0:T(8,128)(2,1)S(1)}, u32[]{:S(2)}, u32[]{:S(2)}) async-start(bf16[32,64,128]{2,1,0:T(8,128)(2,1)} %get-tuple-element.25), calls=%async_computation.1 | async-start | bytes 1048576 | tf_op jit(solution)/shard_map/all_to_all | solution.py:399
  28.4 3.6 %collective-permute-start.3 = (bf16[320,128]{1,0:T(8,128)(2,1)S(1)}, bf16[320,128]{1,0:T(8,128)(2,1)S(1)}, u32[]{:S(2)}, u32[]{:S(2)}) collective-permute-start(bf16[320,128]{1,0:T(8,128)(2,1)S(1)} %get-tuple-element.32), channel_id=1, source_target_pairs={{0,1},{1,0},{2,3},{3,2},{4,5},{5,4},{6,7},{7,6},{8,9},{9,8},{10,11... | collective-permute-start | bytes 245768 | tf_op jit(solution)/shard_map/ppermute | solution.py:403
  28.5 7.7 %collective-permute-start.4 = (bf16[320,128]{1,0:T(8,128)(2,1)S(1)}, bf16[320,128]{1,0:T(8,128)(2,1)S(1)}, u32[]{:S(2)}, u32[]{:S(2)}) collective-permute-start(bf16[320,128]{1,0:T(8,128)(2,1)S(1)} %get-tuple-element.33), channel_id=1, source_target_pairs={{0,2},{1,3},{2,0},{3,1},{4,6},{5,7},{6,4},{7,5},{8,10},{9,11},{10,... | collective-permute-start | bytes 245768 | tf_op jit(solution)/shard_map/ppermute | solution.py:403
  30.0 13.2 %collective-permute-start.5 = (bf16[320,128]{1,0:T(8,128)(2,1)S(1)}, bf16[320,128]{1,0:T(8,128)(2,1)S(1)}, u32[]{:S(2)}, u32[]{:S(2)}) collective-permute-start(bf16[320,128]{1,0:T(8,128)(2,1)S(1)} %get-tuple-element.34), channel_id=1, source_target_pairs={{0,3},{1,2},{2,1},{3,0},{4,7},{5,6},{6,5},{7,4},{8,11},{9,10},{10,... | collective-permute-start | bytes 245768 | tf_op jit(solution)/shard_map/ppermute | solution.py:403
  30.3 12.8 %collective-permute-start.6 = (bf16[320,128]{1,0:T(8,128)(2,1)S(1)}, bf16[320,128]{1,0:T(8,128)(2,1)S(1)}, u32[]{:S(2)}, u32[]{:S(2)}) collective-permute-start(bf16[320,128]{1,0:T(8,128)(2,1)S(1)} %get-tuple-element.35), channel_id=1, source_target_pairs={{0,4},{1,5},{2,6},{3,7},{4,0},{5,1},{6,2},{7,3},{8,12},{9,13},{10,... | collective-permute-start | bytes 245768 | tf_op jit(solution)/shard_map/ppermute | solution.py:403
  31.8 11.4 %collective-permute-start.7 = (bf16[320,128]{1,0:T(8,128)(2,1)S(1)}, bf16[320,128]{1,0:T(8,128)(2,1)S(1)}, u32[]{:S(2)}, u32[]{:S(2)}) collective-permute-start(bf16[320,128]{1,0:T(8,128)(2,1)S(1)} %get-tuple-element.36), channel_id=1, source_target_pairs={{0,5},{1,4},{2,7},{3,6},{4,1},{5,0},{6,3},{7,2},{8,13},{9,12},{10,... | collective-permute-start | bytes 245768 | tf_op jit(solution)/shard_map/ppermute | solution.py:403
  32.0 11.2 %collective-permute-start.8 = (bf16[320,128]{1,0:T(8,128)(2,1)S(1)}, bf16[320,128]{1,0:T(8,128)(2,1)S(1)}, u32[]{:S(2)}, u32[]{:S(2)}) collective-permute-start(bf16[320,128]{1,0:T(8,128)(2,1)S(1)} %get-tuple-element.37), channel_id=1, source_target_pairs={{0,6},{1,7},{2,4},{3,5},{4,2},{5,3},{6,0},{7,1},{8,14},{9,15},{10,... | collective-permute-start | bytes 245768 | tf_op jit(solution)/shard_map/ppermute | solution.py:403
  36.2 7.0 %collective-permute-start.9 = (bf16[320,128]{1,0:T(8,128)(2,1)S(1)}, bf16[320,128]{1,0:T(8,128)(2,1)S(1)}, u32[]{:S(2)}, u32[]{:S(2)}) collective-permute-start(bf16[320,128]{1,0:T(8,128)(2,1)S(1)} %get-tuple-element.38), channel_id=1, source_target_pairs={{0,7},{1,6},{2,5},{3,4},{4,3},{5,2},{6,1},{7,0},{8,15},{9,14},{10,... | collective-permute-start | bytes 245768 | tf_op jit(solution)/shard_map/ppermute | solution.py:403

commit v5 on v4

--- a/solution.py
+++ b/solution.py
@@ -14,6 +14,7 @@
 PACK = LANES // BW
 GROUPS = TILE // LANES
 NEAR = 8
+ORDER = (6, 4, 2, 7, 5, 3, 1, 0)
 
 
 def mm(a, b):
@@ -245,7 +246,7 @@
 
 
 def far_order(outer):
-    return [0, outer - 1, *range(1, outer - 1)]
+    return [0, *range(2, outer), 1]
 
 
 def regroup_kernel(token_ref, *refs):
@@ -293,7 +294,7 @@
     devices = outer * NEAR
     out_rows, aux = mv_ref.shape[0], mv_ref.shape[1]
     me = lax.axis_index("basis")
-    for near, x_ref in enumerate(x_refs):
+    for near, x_ref in zip(ORDER, x_refs):
         for far in range(outer):
             owner = me ^ (far * NEAR + near)
             wide[pl.ds(pl.multiple_of(owner * height, height), height), :] = (
@@ -488,8 +489,7 @@
         "regroup",
         9,
     ))
-    for near in range(1, NEAR):
-        xt[near] = permute(xt[near], devices, near)
+    xt = [permute(xt[near], devices, near) if near else xt[near] for near in ORDER]
     mv = call(
         functools.partial(rows_kernel, aux_dev),
         vmem((rows_m, aux, LANES), BF16),

time: 57.4 us -> 56.5 us (0.984)
  starting transfers between devices: 24.6 us -> 23.1 us
  waiting for transfers between devices: 8.51 us -> 9.11 us
    ppermute x10, waiting for transfers between devices: 3.23 us -> 7.44 us  [permute(): return lax.ppermute(x, 'basis', [(i, i ^ step) for i in range(devices)])]
    all_to_all x2, waiting for transfers between devices: 5.28 us -> 1.67 us  [exchange(): return lax.all_to_all(x, 'basis', split_axis=0, concat_axis=0, tiled=True)]
    ppermute x10, starting transfers between devices: 11.5 us -> 10.7 us  [permute(): return lax.ppermute(x, 'basis', [(i, i ^ step) for i in range(devices)])]
    all_to_all x2, starting transfers between devices: 13.1 us -> 12.4 us  [exchange(): return lax.all_to_all(x, 'basis', split_axis=0, concat_axis=0, tiled=True)]
  transfers between devices with their start and end apart: 12 -> 12, of which waited for: 3 -> 4; matrix products, arithmetic and copies ran while one was open for 0% -> 0% of each run, Pallas kernels for 15% -> 15%
where the time goes in v5:
time: 56.5 us; the launch traced here: 56.1 us
  starting transfers between devices  23.1 us (41%)
  Pallas kernels  13.2 us (23%)
  blocking collectives  10.6 us (19%)
  waiting for transfers between devices  9.11 us (16%)
    pallas_call x7, Pallas kernels, call(): pl.pallas_call(kernel, out_shape=outs, in_specs=[pl.BlockSpec(memory_spac...  13.2 us
    all_to_all x2, starting transfers between devices, exchange(): return lax.all_to_all(x, 'basis', split_axis=0, concat_axis=0, tiled=True)  12.4 us
    ppermute x10, starting transfers between devices, permute(): return lax.ppermute(x, 'basis', [(i, i ^ step) for i in range(devices)])  10.7 us
    all_to_all x1, blocking collectives, exchange(): return lax.all_to_all(x, 'basis', split_axis=0, concat_axis=0, tiled=True)  10.6 us
    ppermute x10, waiting for transfers between devices, permute(): return lax.ppermute(x, 'basis', [(i, i ^ step) for i in range(devices)])  7.44 us
    all_to_all x2, waiting for transfers between devices, exchange(): return lax.all_to_all(x, 'basis', split_axis=0, concat_axis=0, tiled=True)  1.67 us
  transfers between devices with their start and end apart: 12, of which 4 were waited for; matrix products, arithmetic and copies ran while one was open for 0% of the time, Pallas kernels for 15%

profile of v5, /device:TPU:0, one launch (start us, length us, event | category | flops | bytes accessed | tf_op | source)
XLA Modules:
  0.0 56.1 jit_solution(11314607177662512902)
XLA Ops:
  0.0 1.4 %format.1 = bf16[32,16,128]{2,1,0:T(8,128)(2,1)} custom-call(bf16[2,1024]{1,0:T(2,128)(2,1)} %bitcast.13), custom_call_target="tpu_custom_call" | custom-call | flops 1000000000 | bytes 3000000 | tf_op jit(solution)/shard_map/format/pallas_call | solution.py:383
  1.4 7.3 %all-to-all-start = ((bf16[32,16,128]{2,1,0:T(8,128)(2,1)}), bf16[32,16,128]{2,1,0:T(8,128)(2,1)S(1)}, u32[]{:S(2)}, u32[]{:S(2)}) async-start(bf16[32,16,128]{2,1,0:T(8,128)(2,1)} %format.1), calls=%async_computation | async-start | bytes 262144 | tf_op jit(solution)/shard_map/all_to_all | solution.py:400
  8.7 4.0 %prepare.1 = (bf16[528,128]{1,0:T(8,128)(2,1)S(1)}, bf16[528,128]{1,0:T(8,128)(2,1)S(1)}, bf16[528,128]{1,0:T(8,128)(2,1)S(1)}, bf16[528,128]{1,0:T(8,128)(2,1)S...) custom-call(s32[1,32]{1,0:T(1,128)} %bitcast.17, s32[8,32]{1,0:T(8,128)} %bitcast.14, ...), custom_call_target="tpu_custom_call" | custom-call | flops 5000000000 | bytes 15000000 | tf_op jit(solution)/shard_map/prepare/pallas_call | solution.py:383
  12.7 2.7 %collective-permute-start = (bf16[528,128]{1,0:T(8,128)(2,1)S(1)}, bf16[528,128]{1,0:T(8,128)(2,1)S(1)}, u32[]{:S(2)}, u32[]{:S(2)}) collective-permute-start(bf16[528,128]{1,0:T(8,128)(2,1)S(1)} %get-tuple-element.28), channel_id=1, source_target_pairs={{0,16},{1,17},{2,18},{3,19},{4,20},{5,21},{6,22},{7,23},{8,24},{9,... | collective-permute-start | bytes 405512 | tf_op jit(solution)/shard_map/ppermute | solution.py:404
  15.5 1.5 %collective-permute-start.1 = (bf16[528,128]{1,0:T(8,128)(2,1)S(1)}, bf16[528,128]{1,0:T(8,128)(2,1)S(1)}, u32[]{:S(2)}, u32[]{:S(2)}) collective-permute-start(bf16[528,128]{1,0:T(8,128)(2,1)S(1)} %get-tuple-element.29), channel_id=1, source_target_pairs={{0,24},{1,25},{2,26},{3,27},{4,28},{5,29},{6,30},{7,31},{8,16},{9,... | collective-permute-start | bytes 405512 | tf_op jit(solution)/shard_map/ppermute | solution.py:404
  16.9 0.1 collective-permute-start.2
  17.0 0.0 all-to-all-done.dens_ref
  17.0 3.9 %virt.1 = (bf16[32,64,128]{2,1,0:T(8,128)(2,1)}, f32[8,128]{1,0:T(8,128)S(1)}) custom-call(s32[8,128]{1,0:T(8,128)S(1)} %get-tuple-element.22.table_hbm, bf16[32,16,128]{2,1,0:T(8,128)(2,1)S(1)} %all-to-all-done.dens_ref, bf16[2048,256]{1,0:T(8,128)(2,1)S(1)} %get-tuple-element.23.a_ref, bf16[1024,1024]{1,0:T(8,128)(2,1)} %get-tuple-element.24.perm_hbm), custom_call_target="tpu_custom_call" | custom-call | flops 99999997952 | bytes 300000000 | tf_op jit(solution)/shard_map/virt/pallas_call | solution.py:383
  20.9 5.1 %all-to-all-start.1 = ((bf16[32,64,128]{2,1,0:T(8,128)(2,1)}), bf16[32,64,128]{2,1,0:T(8,128)(2,1)S(1)}, u32[]{:S(2)}, u32[]{:S(2)}) async-start(bf16[32,64,128]{2,1,0:T(8,128)(2,1)} %get-tuple-element.25), calls=%async_computation.1 | async-start | bytes 1048576 | tf_op jit(solution)/shard_map/all_to_all | solution.py:400
  26.1 0.0 collective-permute-done.refs_1_
  26.1 0.0 collective-permute-done.1.refs_2_
  26.1 0.5 collective-permute-done.2.refs_3_
  26.6 0.1 regroup.1
  26.7 2.6 %collective-permute-start.3 = (bf16[320,128]{1,0:T(8,128)(2,1)S(1)}, bf16[320,128]{1,0:T(8,128)(2,1)S(1)}, u32[]{:S(2)}, u32[]{:S(2)}) collective-permute-start(bf16[320,128]{1,0:T(8,128)(2,1)S(1)} %get-tuple-element.31), channel_id=1, source_target_pairs={{0,6},{1,7},{2,4},{3,5},{4,2},{5,3},{6,0},{7,1},{8,14},{9,15},{10,... | collective-permute-start | bytes 245768 | tf_op jit(solution)/shard_map/ppermute | solution.py:404
  29.3 0.6 %collective-permute-start.4 = (bf16[320,128]{1,0:T(8,128)(2,1)S(1)}, bf16[320,128]{1,0:T(8,128)(2,1)S(1)}, u32[]{:S(2)}, u32[]{:S(2)}) collective-permute-start(bf16[320,128]{1,0:T(8,128)(2,1)S(1)} %get-tuple-element.32), channel_id=1, source_target_pairs={{0,4},{1,5},{2,6},{3,7},{4,0},{5,1},{6,2},{7,3},{8,12},{9,13},{10,... | collective-permute-start | bytes 245768 | tf_op jit(solution)/shard_map/ppermute | solution.py:404
  29.9 0.4 collective-permute-start.5
  30.2 1.1 %collective-permute-start.6 = (bf16[320,128]{1,0:T(8,128)(2,1)S(1)}, bf16[320,128]{1,0:T(8,128)(2,1)S(1)}, u32[]{:S(2)}, u32[]{:S(2)}) collective-permute-start(bf16[320,128]{1,0:T(8,128)(2,1)S(1)} %get-tuple-element.34), channel_id=1, source_target_pairs={{0,7},{1,6},{2,5},{3,4},{4,3},{5,2},{6,1},{7,0},{8,15},{9,14},{10,... | collective-permute-start | bytes 245768 | tf_op jit(solution)/shard_map/ppermute | solution.py:404
  31.3 1.8 %collective-permute-start.7 = (bf16[320,128]{1,0:T(8,128)(2,1)S(1)}, bf16[320,128]{1,0:T(8,128)(2,1)S(1)}, u32[]{:S(2)}, u32[]{:S(2)}) collective-permute-start(bf16[320,128]{1,0:T(8,128)(2,1)S(1)} %get-tuple-element.35), channel_id=1, source_target_pairs={{0,5},{1,4},{2,7},{3,6},{4,1},{5,0},{6,3},{7,2},{8,13},{9,12},{10,... | collective-permute-start | bytes 245768 | tf_op jit(solution)/shard_map/ppermute | solution.py:404
  33.1 3.0 %collective-permute-done.3.rest_0_ = bf16[320,128]{1,0:T(8,128)(2,1)S(1)} collective-permute-done((bf16[320,128]{1,0:T(8,128)(2,1)S(1)}, bf16[320,128]{1,0:T(8,128)(2,1)S(1)}, u32[]{:S(2)}, u32[]{:S(2)}) %collective-permute-start.3) | collective-permute-done | bytes 81952 | tf_op jit(solution)/shard_map/ppermute | solution.py:404
  36.1 0.0 collective-permute-start.8
  36.1 3.9 %collective-permute-done.4.rest_1_ = bf16[320,128]{1,0:T(8,128)(2,1)S(1)} collective-permute-done((bf16[320,128]{1,0:T(8,128)(2,1)S(1)}, bf16[320,128]{1,0:T(8,128)(2,1)S(1)}, u32[]{:S(2)}, u32[]{:S(2)}) %collective-permute-start.4) | collective-permute-done | bytes 81952 | tf_op jit(solution)/shard_map/ppermute | solution.py:404
  40.0 0.0 collective-permute-start.9
  40.0 1.7 %all-to-all-done.1.xm_ref = bf16[32,64,128]{2,1,0:T(8,128)(2,1)S(1)} async-done(((bf16[32,64,128]{2,1,0:T(8,128)(2,1)}), bf16[32,64,128]{2,1,0:T(8,128)(2,1)S(1)}, u32[]{:S(2)}, u32[]{:S(2)}) %all-to-all-start.1) | async-done | bytes 524320 | tf_op jit(solution)/shard_map/all_to_all | solution.py:400
  41.6 0.6 %rows.1.mv_ref = bf16[32,64,128]{2,1,0:T(8,128)(2,1)S(1)} custom-call(bf16[32,64,128]{2,1,0:T(8,128)(2,1)S(1)} %all-to-all-done.1.xm_ref), custom_call_target="tpu_custom_call" | custom-call | flops 1000000000 | bytes 3000000 | tf_op jit(solution)/shard_map/rows/pallas_call | solution.py:383
  42.3 0.0 collective-permute-done.5.rest_2_
  42.3 0.0 collective-permute-done.6.rest_3_
  42.3 0.0 collective-permute-done.7.rest_4_
  42.3 0.0 collective-permute-done.8.rest_5_
  42.3 0.0 collective-permute-done.9.rest_6_
  42.3 2.4 %occ.1 = f32[32,128]{1,0:T(8,128)S(1)} custom-call(s32[8,128]{1,0:T(8,128)S(1)} %get-tuple-element.22.table_hbm, bf16[32,64,128]{2,1,0:T(8,128)(2,1)S(1)} %rows.1.mv_ref, bf16[320,128]{1,0:T(8,128)(2,1)S(1)} %collective-permute-done.3.rest_0_, bf16[320,128]{1,0:T(8,128)(2,1)S(1)} %collective-permute-done.4.rest_1_, ...), custom_call_target="tpu_custom_call" | custom-call | flops 1000000000 | bytes 3000000 | tf_op jit(solution)/shard_map/occ/pallas_call | solution.py:383
  44.7 10.6 %all_to_all.21 = f32[32,1,128]{2,1,0:T(1,128)S(1)} all-to-all(f32[32,1,128]{2,1,0:T(1,128)S(1)} %bitcast.10), channel_id=1, replica_groups=mesh['parts'=1,'basis'=32] {'basis'}, dimensions={0} | all-to-all | bytes 32768 | tf_op jit(solution)/shard_map/all_to_all | solution.py:400
  55.3 0.8 %total.1 = f32[2,64]{1,0:T(2,128)} custom-call(f32[32,128]{1,0:T(8,128)S(1)} %bitcast.11), custom_call_target="tpu_custom_call" | custom-call | flops 1000000000 | bytes 3000000 | tf_op jit(solution)/shard_map/total/pallas_call | solution.py:383
Async XLA Ops:
  1.4 15.6 %all-to-all-start = ((bf16[32,16,128]{2,1,0:T(8,128)(2,1)}), bf16[32,16,128]{2,1,0:T(8,128)(2,1)S(1)}, u32[]{:S(2)}, u32[]{:S(2)}) async-start(bf16[32,16,128]{2,1,0:T(8,128)(2,1)} %format.1), calls=%async_computation | async-start | bytes 262144 | tf_op jit(solution)/shard_map/all_to_all | solution.py:400
  12.7 13.3 %collective-permute-start = (bf16[528,128]{1,0:T(8,128)(2,1)S(1)}, bf16[528,128]{1,0:T(8,128)(2,1)S(1)}, u32[]{:S(2)}, u32[]{:S(2)}) collective-permute-start(bf16[528,128]{1,0:T(8,128)(2,1)S(1)} %get-tuple-element.28), channel_id=1, source_target_pairs={{0,16},{1,17},{2,18},{3,19},{4,20},{5,21},{6,22},{7,23},{8,24},{9,... | collective-permute-start | bytes 405512 | tf_op jit(solution)/shard_map/ppermute | solution.py:404
  15.5 10.6 %collective-permute-start.1 = (bf16[528,128]{1,0:T(8,128)(2,1)S(1)}, bf16[528,128]{1,0:T(8,128)(2,1)S(1)}, u32[]{:S(2)}, u32[]{:S(2)}) collective-permute-start(bf16[528,128]{1,0:T(8,128)(2,1)S(1)} %get-tuple-element.29), channel_id=1, source_target_pairs={{0,24},{1,25},{2,26},{3,27},{4,28},{5,29},{6,30},{7,31},{8,16},{9,... | collective-permute-start | bytes 405512 | tf_op jit(solution)/shard_map/ppermute | solution.py:404
  16.9 9.7 %collective-permute-start.2 = (bf16[528,128]{1,0:T(8,128)(2,1)S(1)}, bf16[528,128]{1,0:T(8,128)(2,1)S(1)}, u32[]{:S(2)}, u32[]{:S(2)}) collective-permute-start(bf16[528,128]{1,0:T(8,128)(2,1)S(1)} %get-tuple-element.30), channel_id=1, source_target_pairs={{0,8},{1,9},{2,10},{3,11},{4,12},{5,13},{6,14},{7,15},{8,0},{9,1},... | collective-permute-start | bytes 405512 | tf_op jit(solution)/shard_map/ppermute | solution.py:404
  20.9 20.7 %all-to-all-start.1 = ((bf16[32,64,128]{2,1,0:T(8,128)(2,1)}), bf16[32,64,128]{2,1,0:T(8,128)(2,1)S(1)}, u32[]{:S(2)}, u32[]{:S(2)}) async-start(bf16[32,64,128]{2,1,0:T(8,128)(2,1)} %get-tuple-element.25), calls=%async_computation.1 | async-start | bytes 1048576 | tf_op jit(solution)/shard_map/all_to_all | solution.py:400
  26.7 9.4 %collective-permute-start.3 = (bf16[320,128]{1,0:T(8,128)(2,1)S(1)}, bf16[320,128]{1,0:T(8,128)(2,1)S(1)}, u32[]{:S(2)}, u32[]{:S(2)}) collective-permute-start(bf16[320,128]{1,0:T(8,128)(2,1)S(1)} %get-tuple-element.31), channel_id=1, source_target_pairs={{0,6},{1,7},{2,4},{3,5},{4,2},{5,3},{6,0},{7,1},{8,14},{9,15},{10,... | collective-permute-start | bytes 245768 | tf_op jit(solution)/shard_map/ppermute | solution.py:404
  29.3 10.7 %collective-permute-start.4 = (bf16[320,128]{1,0:T(8,128)(2,1)S(1)}, bf16[320,128]{1,0:T(8,128)(2,1)S(1)}, u32[]{:S(2)}, u32[]{:S(2)}) collective-permute-start(bf16[320,128]{1,0:T(8,128)(2,1)S(1)} %get-tuple-element.32), channel_id=1, source_target_pairs={{0,4},{1,5},{2,6},{3,7},{4,0},{5,1},{6,2},{7,3},{8,12},{9,13},{10,... | collective-permute-start | bytes 245768 | tf_op jit(solution)/shard_map/ppermute | solution.py:404
  29.9 12.4 %collective-permute-start.5 = (bf16[320,128]{1,0:T(8,128)(2,1)S(1)}, bf16[320,128]{1,0:T(8,128)(2,1)S(1)}, u32[]{:S(2)}, u32[]{:S(2)}) collective-permute-start(bf16[320,128]{1,0:T(8,128)(2,1)S(1)} %get-tuple-element.33), channel_id=1, source_target_pairs={{0,2},{1,3},{2,0},{3,1},{4,6},{5,7},{6,4},{7,5},{8,10},{9,11},{10,... | collective-permute-start | bytes 245768 | tf_op jit(solution)/shard_map/ppermute | solution.py:404
  30.2 12.1 %collective-permute-start.6 = (bf16[320,128]{1,0:T(8,128)(2,1)S(1)}, bf16[320,128]{1,0:T(8,128)(2,1)S(1)}, u32[]{:S(2)}, u32[]{:S(2)}) collective-permute-start(bf16[320,128]{1,0:T(8,128)(2,1)S(1)} %get-tuple-element.34), channel_id=1, source_target_pairs={{0,7},{1,6},{2,5},{3,4},{4,3},{5,2},{6,1},{7,0},{8,15},{9,14},{10,... | collective-permute-start | bytes 245768 | tf_op jit(solution)/shard_map/ppermute | solution.py:404
  31.3 11.0 %collective-permute-start.7 = (bf16[320,128]{1,0:T(8,128)(2,1)S(1)}, bf16[320,128]{1,0:T(8,128)(2,1)S(1)}, u32[]{:S(2)}, u32[]{:S(2)}) collective-permute-start(bf16[320,128]{1,0:T(8,128)(2,1)S(1)} %get-tuple-element.35), channel_id=1, source_target_pairs={{0,5},{1,4},{2,7},{3,6},{4,1},{5,0},{6,3},{7,2},{8,13},{9,12},{10,... | collective-permute-start | bytes 245768 | tf_op jit(solution)/shard_map/ppermute | solution.py:404
  36.1 6.2 %collective-permute-start.8 = (bf16[320,128]{1,0:T(8,128)(2,1)S(1)}, bf16[320,128]{1,0:T(8,128)(2,1)S(1)}, u32[]{:S(2)}, u32[]{:S(2)}) collective-permute-start(bf16[320,128]{1,0:T(8,128)(2,1)S(1)} %get-tuple-element.36), channel_id=1, source_target_pairs={{0,3},{1,2},{2,1},{3,0},{4,7},{5,6},{6,5},{7,4},{8,11},{9,10},{10,... | collective-permute-start | bytes 245768 | tf_op jit(solution)/shard_map/ppermute | solution.py:404
  40.0 2.4 %collective-permute-start.9 = (bf16[320,128]{1,0:T(8,128)(2,1)S(1)}, bf16[320,128]{1,0:T(8,128)(2,1)S(1)}, u32[]{:S(2)}, u32[]{:S(2)}) collective-permute-start(bf16[320,128]{1,0:T(8,128)(2,1)S(1)} %get-tuple-element.37), channel_id=1, source_target_pairs={{0,1},{1,0},{2,3},{3,2},{4,5},{5,4},{6,7},{7,6},{8,9},{9,8},{10,11... | collective-permute-start | bytes 245768 | tf_op jit(solution)/shard_map/ppermute | solution.py:404

commit v6 on v5

--- a/solution.py
+++ b/solution.py
@@ -14,7 +14,7 @@
 PACK = LANES // BW
 GROUPS = TILE // LANES
 NEAR = 8
-ORDER = (6, 4, 2, 7, 5, 3, 1, 0)
+ORDER = (6, 4, 2, 5, 7, 3, 1, 0)
 
 
 def mm(a, b):

time: 56.5 us -> 56.5 us (level)
  no operation moved by 1% of the time
where the time goes in v6:
time: 56.5 us; the launch traced here: 56.1 us
  starting transfers between devices  23.1 us (41%)
  Pallas kernels  13.2 us (23%)
  blocking collectives  10.6 us (19%)
  waiting for transfers between devices  9.11 us (16%)
    pallas_call x7, Pallas kernels, call(): pl.pallas_call(kernel, out_shape=outs, in_specs=[pl.BlockSpec(memory_spac...  13.2 us
    all_to_all x2, starting transfers between devices, exchange(): return lax.all_to_all(x, 'basis', split_axis=0, concat_axis=0, tiled=True)  12.4 us
    ppermute x10, starting transfers between devices, permute(): return lax.ppermute(x, 'basis', [(i, i ^ step) for i in range(devices)])  10.7 us
    all_to_all x1, blocking collectives, exchange(): return lax.all_to_all(x, 'basis', split_axis=0, concat_axis=0, tiled=True)  10.6 us
    ppermute x10, waiting for transfers between devices, permute(): return lax.ppermute(x, 'basis', [(i, i ^ step) for i in range(devices)])  7.44 us
    all_to_all x2, waiting for transfers between devices, exchange(): return lax.all_to_all(x, 'basis', split_axis=0, concat_axis=0, tiled=True)  1.67 us
  transfers between devices with their start and end apart: 12, of which 4 were waited for; matrix products, arithmetic and copies ran while one was open for 0% of the time, Pallas kernels for 15%

profile of v6, /device:TPU:0, one launch (start us, length us, event | category | flops | bytes accessed | tf_op | source)
XLA Modules:
  0.0 56.1 jit_solution(12501930151187901408)
XLA Ops:
  0.0 1.4 %format.1 = bf16[32,16,128]{2,1,0:T(8,128)(2,1)} custom-call(bf16[2,1024]{1,0:T(2,128)(2,1)} %bitcast.13), custom_call_target="tpu_custom_call" | custom-call | flops 1000000000 | bytes 3000000 | tf_op jit(solution)/shard_map/format/pallas_call | solution.py:383
  1.4 7.3 %all-to-all-start = ((bf16[32,16,128]{2,1,0:T(8,128)(2,1)}), bf16[32,16,128]{2,1,0:T(8,128)(2,1)S(1)}, u32[]{:S(2)}, u32[]{:S(2)}) async-start(bf16[32,16,128]{2,1,0:T(8,128)(2,1)} %format.1), calls=%async_computation | async-start | bytes 262144 | tf_op jit(solution)/shard_map/all_to_all | solution.py:400
  8.7 4.0 %prepare.1 = (bf16[528,128]{1,0:T(8,128)(2,1)S(1)}, bf16[528,128]{1,0:T(8,128)(2,1)S(1)}, bf16[528,128]{1,0:T(8,128)(2,1)S(1)}, bf16[528,128]{1,0:T(8,128)(2,1)S...) custom-call(s32[1,32]{1,0:T(1,128)} %bitcast.17, s32[8,32]{1,0:T(8,128)} %bitcast.14, ...), custom_call_target="tpu_custom_call" | custom-call | flops 5000000000 | bytes 15000000 | tf_op jit(solution)/shard_map/prepare/pallas_call | solution.py:383
  12.7 2.7 %collective-permute-start = (bf16[528,128]{1,0:T(8,128)(2,1)S(1)}, bf16[528,128]{1,0:T(8,128)(2,1)S(1)}, u32[]{:S(2)}, u32[]{:S(2)}) collective-permute-start(bf16[528,128]{1,0:T(8,128)(2,1)S(1)} %get-tuple-element.28), channel_id=1, source_target_pairs={{0,16},{1,17},{2,18},{3,19},{4,20},{5,21},{6,22},{7,23},{8,24},{9,... | collective-permute-start | bytes 405512 | tf_op jit(solution)/shard_map/ppermute | solution.py:404
  15.5 1.5 %collective-permute-start.1 = (bf16[528,128]{1,0:T(8,128)(2,1)S(1)}, bf16[528,128]{1,0:T(8,128)(2,1)S(1)}, u32[]{:S(2)}, u32[]{:S(2)}) collective-permute-start(bf16[528,128]{1,0:T(8,128)(2,1)S(1)} %get-tuple-element.29), channel_id=1, source_target_pairs={{0,24},{1,25},{2,26},{3,27},{4,28},{5,29},{6,30},{7,31},{8,16},{9,... | collective-permute-start | bytes 405512 | tf_op jit(solution)/shard_map/ppermute | solution.py:404
  16.9 0.1 collective-permute-start.2
  17.0 0.0 all-to-all-done.dens_ref
  17.0 3.9 %virt.1 = (bf16[32,64,128]{2,1,0:T(8,128)(2,1)}, f32[8,128]{1,0:T(8,128)S(1)}) custom-call(s32[8,128]{1,0:T(8,128)S(1)} %get-tuple-element.22.table_hbm, bf16[32,16,128]{2,1,0:T(8,128)(2,1)S(1)} %all-to-all-done.dens_ref, bf16[2048,256]{1,0:T(8,128)(2,1)S(1)} %get-tuple-element.23.a_ref, bf16[1024,1024]{1,0:T(8,128)(2,1)} %get-tuple-element.24.perm_hbm), custom_call_target="tpu_custom_call" | custom-call | flops 99999997952 | bytes 300000000 | tf_op jit(solution)/shard_map/virt/pallas_call | solution.py:383
  20.9 5.1 %all-to-all-start.1 = ((bf16[32,64,128]{2,1,0:T(8,128)(2,1)}), bf16[32,64,128]{2,1,0:T(8,128)(2,1)S(1)}, u32[]{:S(2)}, u32[]{:S(2)}) async-start(bf16[32,64,128]{2,1,0:T(8,128)(2,1)} %get-tuple-element.25), calls=%async_computation.1 | async-start | bytes 1048576 | tf_op jit(solution)/shard_map/all_to_all | solution.py:400
  26.1 0.0 collective-permute-done.refs_1_
  26.1 0.0 collective-permute-done.1.refs_2_
  26.1 0.5 collective-permute-done.2.refs_3_
  26.6 0.1 regroup.1
  26.7 2.6 %collective-permute-start.3 = (bf16[320,128]{1,0:T(8,128)(2,1)S(1)}, bf16[320,128]{1,0:T(8,128)(2,1)S(1)}, u32[]{:S(2)}, u32[]{:S(2)}) collective-permute-start(bf16[320,128]{1,0:T(8,128)(2,1)S(1)} %get-tuple-element.31), channel_id=1, source_target_pairs={{0,6},{1,7},{2,4},{3,5},{4,2},{5,3},{6,0},{7,1},{8,14},{9,15},{10,... | collective-permute-start | bytes 245768 | tf_op jit(solution)/shard_map/ppermute | solution.py:404
  29.3 0.6 %collective-permute-start.4 = (bf16[320,128]{1,0:T(8,128)(2,1)S(1)}, bf16[320,128]{1,0:T(8,128)(2,1)S(1)}, u32[]{:S(2)}, u32[]{:S(2)}) collective-permute-start(bf16[320,128]{1,0:T(8,128)(2,1)S(1)} %get-tuple-element.32), channel_id=1, source_target_pairs={{0,4},{1,5},{2,6},{3,7},{4,0},{5,1},{6,2},{7,3},{8,12},{9,13},{10,... | collective-permute-start | bytes 245768 | tf_op jit(solution)/shard_map/ppermute | solution.py:404
  29.9 0.4 collective-permute-start.5
  30.2 0.2 collective-permute-start.6
  30.4 2.7 %collective-permute-start.7 = (bf16[320,128]{1,0:T(8,128)(2,1)S(1)}, bf16[320,128]{1,0:T(8,128)(2,1)S(1)}, u32[]{:S(2)}, u32[]{:S(2)}) collective-permute-start(bf16[320,128]{1,0:T(8,128)(2,1)S(1)} %get-tuple-element.35), channel_id=1, source_target_pairs={{0,7},{1,6},{2,5},{3,4},{4,3},{5,2},{6,1},{7,0},{8,15},{9,14},{10,... | collective-permute-start | bytes 245768 | tf_op jit(solution)/shard_map/ppermute | solution.py:404
  33.1 3.0 %collective-permute-done.3.rest_0_ = bf16[320,128]{1,0:T(8,128)(2,1)S(1)} collective-permute-done((bf16[320,128]{1,0:T(8,128)(2,1)S(1)}, bf16[320,128]{1,0:T(8,128)(2,1)S(1)}, u32[]{:S(2)}, u32[]{:S(2)}) %collective-permute-start.3) | collective-permute-done | bytes 81952 | tf_op jit(solution)/shard_map/ppermute | solution.py:404
  36.1 0.0 collective-permute-start.8
  36.1 3.9 %collective-permute-done.4.rest_1_ = bf16[320,128]{1,0:T(8,128)(2,1)S(1)} collective-permute-done((bf16[320,128]{1,0:T(8,128)(2,1)S(1)}, bf16[320,128]{1,0:T(8,128)(2,1)S(1)}, u32[]{:S(2)}, u32[]{:S(2)}) %collective-permute-start.4) | collective-permute-done | bytes 81952 | tf_op jit(solution)/shard_map/ppermute | solution.py:404
  40.0 0.0 collective-permute-start.9
  40.0 1.7 %all-to-all-done.1.xm_ref = bf16[32,64,128]{2,1,0:T(8,128)(2,1)S(1)} async-done(((bf16[32,64,128]{2,1,0:T(8,128)(2,1)}), bf16[32,64,128]{2,1,0:T(8,128)(2,1)S(1)}, u32[]{:S(2)}, u32[]{:S(2)}) %all-to-all-start.1) | async-done | bytes 524320 | tf_op jit(solution)/shard_map/all_to_all | solution.py:400
  41.6 0.6 %rows.1.mv_ref = bf16[32,64,128]{2,1,0:T(8,128)(2,1)S(1)} custom-call(bf16[32,64,128]{2,1,0:T(8,128)(2,1)S(1)} %all-to-all-done.1.xm_ref), custom_call_target="tpu_custom_call" | custom-call | flops 1000000000 | bytes 3000000 | tf_op jit(solution)/shard_map/rows/pallas_call | solution.py:383
  42.3 0.0 collective-permute-done.5.rest_2_
  42.3 0.0 collective-permute-done.6.rest_3_
  42.3 0.0 collective-permute-done.7.rest_4_
  42.3 0.0 collective-permute-done.8.rest_5_
  42.3 0.0 collective-permute-done.9.rest_6_
  42.3 2.4 %occ.1 = f32[32,128]{1,0:T(8,128)S(1)} custom-call(s32[8,128]{1,0:T(8,128)S(1)} %get-tuple-element.22.table_hbm, bf16[32,64,128]{2,1,0:T(8,128)(2,1)S(1)} %rows.1.mv_ref, bf16[320,128]{1,0:T(8,128)(2,1)S(1)} %collective-permute-done.3.rest_0_, bf16[320,128]{1,0:T(8,128)(2,1)S(1)} %collective-permute-done.4.rest_1_, ...), custom_call_target="tpu_custom_call" | custom-call | flops 1000000000 | bytes 3000000 | tf_op jit(solution)/shard_map/occ/pallas_call | solution.py:383
  44.7 10.6 %all_to_all.21 = f32[32,1,128]{2,1,0:T(1,128)S(1)} all-to-all(f32[32,1,128]{2,1,0:T(1,128)S(1)} %bitcast.10), channel_id=1, replica_groups=mesh['parts'=1,'basis'=32] {'basis'}, dimensions={0} | all-to-all | bytes 32768 | tf_op jit(solution)/shard_map/all_to_all | solution.py:400
  55.3 0.8 %total.1 = f32[2,64]{1,0:T(2,128)} custom-call(f32[32,128]{1,0:T(8,128)S(1)} %bitcast.11), custom_call_target="tpu_custom_call" | custom-call | flops 1000000000 | bytes 3000000 | tf_op jit(solution)/shard_map/total/pallas_call | solution.py:383
Async XLA Ops:
  1.4 15.6 %all-to-all-start = ((bf16[32,16,128]{2,1,0:T(8,128)(2,1)}), bf16[32,16,128]{2,1,0:T(8,128)(2,1)S(1)}, u32[]{:S(2)}, u32[]{:S(2)}) async-start(bf16[32,16,128]{2,1,0:T(8,128)(2,1)} %format.1), calls=%async_computation | async-start | bytes 262144 | tf_op jit(solution)/shard_map/all_to_all | solution.py:400
  12.7 13.3 %collective-permute-start = (bf16[528,128]{1,0:T(8,128)(2,1)S(1)}, bf16[528,128]{1,0:T(8,128)(2,1)S(1)}, u32[]{:S(2)}, u32[]{:S(2)}) collective-permute-start(bf16[528,128]{1,0:T(8,128)(2,1)S(1)} %get-tuple-element.28), channel_id=1, source_target_pairs={{0,16},{1,17},{2,18},{3,19},{4,20},{5,21},{6,22},{7,23},{8,24},{9,... | collective-permute-start | bytes 405512 | tf_op jit(solution)/shard_map/ppermute | solution.py:404
  15.5 10.6 %collective-permute-start.1 = (bf16[528,128]{1,0:T(8,128)(2,1)S(1)}, bf16[528,128]{1,0:T(8,128)(2,1)S(1)}, u32[]{:S(2)}, u32[]{:S(2)}) collective-permute-start(bf16[528,128]{1,0:T(8,128)(2,1)S(1)} %get-tuple-element.29), channel_id=1, source_target_pairs={{0,24},{1,25},{2,26},{3,27},{4,28},{5,29},{6,30},{7,31},{8,16},{9,... | collective-permute-start | bytes 405512 | tf_op jit(solution)/shard_map/ppermute | solution.py:404
  16.9 9.7 %collective-permute-start.2 = (bf16[528,128]{1,0:T(8,128)(2,1)S(1)}, bf16[528,128]{1,0:T(8,128)(2,1)S(1)}, u32[]{:S(2)}, u32[]{:S(2)}) collective-permute-start(bf16[528,128]{1,0:T(8,128)(2,1)S(1)} %get-tuple-element.30), channel_id=1, source_target_pairs={{0,8},{1,9},{2,10},{3,11},{4,12},{5,13},{6,14},{7,15},{8,0},{9,1},... | collective-permute-start | bytes 405512 | tf_op jit(solution)/shard_map/ppermute | solution.py:404
  20.9 20.7 %all-to-all-start.1 = ((bf16[32,64,128]{2,1,0:T(8,128)(2,1)}), bf16[32,64,128]{2,1,0:T(8,128)(2,1)S(1)}, u32[]{:S(2)}, u32[]{:S(2)}) async-start(bf16[32,64,128]{2,1,0:T(8,128)(2,1)} %get-tuple-element.25), calls=%async_computation.1 | async-start | bytes 1048576 | tf_op jit(solution)/shard_map/all_to_all | solution.py:400
  26.7 9.4 %collective-permute-start.3 = (bf16[320,128]{1,0:T(8,128)(2,1)S(1)}, bf16[320,128]{1,0:T(8,128)(2,1)S(1)}, u32[]{:S(2)}, u32[]{:S(2)}) collective-permute-start(bf16[320,128]{1,0:T(8,128)(2,1)S(1)} %get-tuple-element.31), channel_id=1, source_target_pairs={{0,6},{1,7},{2,4},{3,5},{4,2},{5,3},{6,0},{7,1},{8,14},{9,15},{10,... | collective-permute-start | bytes 245768 | tf_op jit(solution)/shard_map/ppermute | solution.py:404
  29.3 10.7 %collective-permute-start.4 = (bf16[320,128]{1,0:T(8,128)(2,1)S(1)}, bf16[320,128]{1,0:T(8,128)(2,1)S(1)}, u32[]{:S(2)}, u32[]{:S(2)}) collective-permute-start(bf16[320,128]{1,0:T(8,128)(2,1)S(1)} %get-tuple-element.32), channel_id=1, source_target_pairs={{0,4},{1,5},{2,6},{3,7},{4,0},{5,1},{6,2},{7,3},{8,12},{9,13},{10,... | collective-permute-start | bytes 245768 | tf_op jit(solution)/shard_map/ppermute | solution.py:404
  29.9 12.4 %collective-permute-start.5 = (bf16[320,128]{1,0:T(8,128)(2,1)S(1)}, bf16[320,128]{1,0:T(8,128)(2,1)S(1)}, u32[]{:S(2)}, u32[]{:S(2)}) collective-permute-start(bf16[320,128]{1,0:T(8,128)(2,1)S(1)} %get-tuple-element.33), channel_id=1, source_target_pairs={{0,2},{1,3},{2,0},{3,1},{4,6},{5,7},{6,4},{7,5},{8,10},{9,11},{10,... | collective-permute-start | bytes 245768 | tf_op jit(solution)/shard_map/ppermute | solution.py:404
  30.2 12.1 %collective-permute-start.6 = (bf16[320,128]{1,0:T(8,128)(2,1)S(1)}, bf16[320,128]{1,0:T(8,128)(2,1)S(1)}, u32[]{:S(2)}, u32[]{:S(2)}) collective-permute-start(bf16[320,128]{1,0:T(8,128)(2,1)S(1)} %get-tuple-element.34), channel_id=1, source_target_pairs={{0,5},{1,4},{2,7},{3,6},{4,1},{5,0},{6,3},{7,2},{8,13},{9,12},{10,... | collective-permute-start | bytes 245768 | tf_op jit(solution)/shard_map/ppermute | solution.py:404
  30.4 11.9 %collective-permute-start.7 = (bf16[320,128]{1,0:T(8,128)(2,1)S(1)}, bf16[320,128]{1,0:T(8,128)(2,1)S(1)}, u32[]{:S(2)}, u32[]{:S(2)}) collective-permute-start(bf16[320,128]{1,0:T(8,128)(2,1)S(1)} %get-tuple-element.35), channel_id=1, source_target_pairs={{0,7},{1,6},{2,5},{3,4},{4,3},{5,2},{6,1},{7,0},{8,15},{9,14},{10,... | collective-permute-start | bytes 245768 | tf_op jit(solution)/shard_map/ppermute | solution.py:404
  36.1 6.2 %collective-permute-start.8 = (bf16[320,128]{1,0:T(8,128)(2,1)S(1)}, bf16[320,128]{1,0:T(8,128)(2,1)S(1)}, u32[]{:S(2)}, u32[]{:S(2)}) collective-permute-start(bf16[320,128]{1,0:T(8,128)(2,1)S(1)} %get-tuple-element.36), channel_id=1, source_target_pairs={{0,3},{1,2},{2,1},{3,0},{4,7},{5,6},{6,5},{7,4},{8,11},{9,10},{10,... | collective-permute-start | bytes 245768 | tf_op jit(solution)/shard_map/ppermute | solution.py:404
  40.0 2.4 %collective-permute-start.9 = (bf16[320,128]{1,0:T(8,128)(2,1)S(1)}, bf16[320,128]{1,0:T(8,128)(2,1)S(1)}, u32[]{:S(2)}, u32[]{:S(2)}) collective-permute-start(bf16[320,128]{1,0:T(8,128)(2,1)S(1)} %get-tuple-element.37), channel_id=1, source_target_pairs={{0,1},{1,0},{2,3},{3,2},{4,5},{5,4},{6,7},{7,6},{8,9},{9,8},{10,11... | collective-permute-start | bytes 245768 | tf_op jit(solution)/shard_map/ppermute | solution.py:404
